TPU v7x, 512 devices: a whole 4x8x8 slice. The times are simulated.
512 devices in a mesh: space: 128 (over y, z, core), scene: 4 (over x).
Axes of the slice: x: 4, y: 8, z: 8, core: 2. Of those that a mesh axis runs over, the one named last changes fastest.
Arguments:
- features: bfloat16 [4, 16384, 256], P('scene', 'space'), may hold values from -6 to 6
- cotangent: bfloat16 [4, 16384, 128], P('scene', 'space'), may hold values from -6 to 6
- relu_mask: int32 [4, 16384, 128], P('scene', 'space'), may hold values 0 or 1
- weight: bfloat16 [27, 256, 128], replicated, may hold values from -0.078125 to 0.078125
- pair_in: int32 [4, 128, 27, 128], P('scene', 'space'), may hold values from 0 to 127, as said below
- pair_out: int32 [4, 128, 27, 128], P('scene', 'space'), may hold values from 0 to 1152, as said below
- recv_index: int32 [4, 128, 1024], P('scene', 'space'), may hold values from 0 to 128, as said below
Outputs:
- conv_out: bfloat16 [4, 16384, 128], P('scene', 'space')
- input_grad: bfloat16 [4, 16384, 256], P('scene', 'space')
- weight_grad: float32 [27, 32768], P(None, 'space')
Inputs may be any that keep to these rules, and one draw needn't show every extreme that they name: `pair_in`: in each offset's list the live pairs come first and padding after; live pairs of one offset have distinct input rows; padding pairs have input row 0. `pair_out`: live pairs name an owned row (distinct among one offset's local pairs) or a live boundary slot toward another device; padding pairs, and only they, hold 1152. In each scene some device has all 128 pairs live at every offset. `recv_index`: entry q * 8 + r of device p belongs to slot r of device q toward p; it is 128 where that slot is empty. The live slots from one device to another are the first ones; no device sends to itself; in each scene one device receives 8 live slots from every other device.
All inputs are finite; a program needn't handle non-finite values. No bound on the sum of `relu_mask` on one device may be relied on, other than what follows from the above.
Results may differ from a plain program's by a relative error of at most 0.001.
Values may be sent and summed in bfloat16 or wider, within the bound.
No kernel may reach another device: no remote copies, remote signals or barrier semaphores. Data moves between devices by JAX's collectives and lax.ppermute only.
A program may use at most 64 MiB of HBM per device.

v0:
```python
import math

import jax
import jax.numpy as jnp
from jax import lax
from jax.sharding import PartitionSpec as P


def sweep_pairs(state, block_step, in_table, out_table):
    offsets_total = in_table.shape[0]

    def advance(inner_state, offset):
        return (block_step(inner_state, offset, in_table[offset], out_table[offset]), None)

    state, unused = lax.scan(advance, state, jnp.arange(offsets_total, dtype=jnp.int32))
    return state


def local(features, cotangent, relu_mask, weight, pair_in, pair_out, recv_index):
    voxel_rows = features[0]
    own_rows = voxel_rows.shape[0]
    in_table = pair_in[0, 0]
    out_table = pair_out[0, 0]
    recv_rows = recv_index[0, 0]
    peer_count = lax.axis_size("space")
    send_rows = recv_rows.shape[0]
    slot_count = send_rows // peer_count
    in_width = weight.shape[1]
    out_width = weight.shape[2]
    upstream = (cotangent[0].astype(jnp.float32) * relu_mask[0].astype(jnp.float32)).astype(
        jnp.bfloat16
    )
    zero_row = jnp.zeros((1, out_width), jnp.bfloat16)
    padded_up = jnp.concatenate([upstream, zero_row], axis=0)
    outgoing = padded_up[recv_rows].reshape(peer_count, slot_count, out_width)
    returned = lax.all_to_all(outgoing, "space", split_axis=0, concat_axis=0, tiled=True)
    extended = jnp.concatenate([upstream, returned.reshape(send_rows, out_width), zero_row], axis=0)

    def forward_block(partial_value, offset, in_rows, out_rows):
        product = jnp.dot(voxel_rows[in_rows], weight[offset], preferred_element_type=jnp.float32)
        return partial_value.at[out_rows].add(product)

    partial_value = jnp.zeros((own_rows + send_rows + 1, out_width), jnp.float32)
    partial_value = sweep_pairs(partial_value, forward_block, in_table, out_table)
    outbound = partial_value[own_rows : own_rows + send_rows].reshape(
        peer_count, slot_count, out_width
    )
    arrived = lax.all_to_all(outbound, "space", split_axis=0, concat_axis=0, tiled=True)
    received = (
        jnp.zeros((own_rows + 1, out_width), jnp.float32)
        .at[recv_rows]
        .add(arrived.reshape(send_rows, out_width))
    )
    conv_out = (partial_value[:own_rows] + received[:own_rows]).astype(jnp.bfloat16)

    def backward_block(state, offset, in_rows, out_rows):
        input_sums, weight_sums = state
        gathered = extended[out_rows]
        back_product = lax.dot_general(
            gathered, weight[offset], (((1,), (1,)), ((), ())), preferred_element_type=jnp.float32
        )
        input_sums = input_sums.at[in_rows].add(back_product)
        kernel_grad = lax.dot_general(
            voxel_rows[in_rows],
            gathered,
            (((0,), (0,)), ((), ())),
            preferred_element_type=jnp.float32,
        )
        weight_sums = weight_sums.at[offset].add(kernel_grad)
        return (input_sums, weight_sums)

    start_state = (
        jnp.zeros((own_rows, in_width), jnp.float32),
        jnp.zeros(weight.shape, jnp.float32),
    )
    input_sums, weight_sums = sweep_pairs(start_state, backward_block, in_table, out_table)
    local_term = weight_sums.reshape(weight.shape[0], in_width * out_width)
    shared = lax.psum_scatter(local_term, "space", scatter_dimension=1, tiled=True)
    reduced = lax.psum(shared, "scene")
    normalizer = 1.0 / math.sqrt(lax.axis_size("scene") * peer_count * own_rows)
    weight_grad = reduced * normalizer
    return (conv_out[None], input_sums.astype(jnp.bfloat16)[None], weight_grad)


def solution(mesh):
    return jax.shard_map(
        local,
        mesh=mesh,
        in_specs=(
            P("scene", "space", None),
            P("scene", "space", None),
            P("scene", "space", None),
            P(),
            P("scene", "space", None, None),
            P("scene", "space", None, None),
            P("scene", "space", None),
        ),
        out_specs=(P("scene", "space", None), P("scene", "space", None), P(None, "space")),
        check_vma=False,
    )
```

profile of v0, /device:TPU:24, one launch (start us, length us, event | category | flops | bytes accessed | tf_op | source)
XLA Modules:
  0.0 540.6 jit_solution(13519078786459436058)
XLA Ops:
  8.8 4.3 gather_fusion.3
  13.0 17.3 %all-to-all-start.1 = ((bf16[128,8,128]{2,1,0:T(8,128)(2,1)}), bf16[128,8,128]{2,1,0:T(8,128)(2,1)S(1)}, u32[]{:S(2)}, u32[]{:S(2)}) async-start(bf16[128,8,128]{2,1,0:T(8,128)(2,1)} %bitcast.21), calls=%async_computation.1 | async-start | bytes 524288 | tf_op jit(solution)/shard_map/all_to_all | solution.py:36
  31.2 12.3 %all-to-all-done.1 = bf16[128,8,128]{2,1,0:T(8,128)(2,1)S(1)} async-done(((bf16[128,8,128]{2,1,0:T(8,128)(2,1)}), bf16[128,8,128]{2,1,0:T(8,128)(2,1)S(1)}, u32[]{:S(2)}, u32[]{:S(2)}) %all-to-all-start.1) | async-done | bytes 262176 | tf_op jit(solution)/shard_map/all_to_all | solution.py:36
  43.7 2.2 broadcast_in_dim.33
  45.9 260.0 %while.24 = (s32[]{:T(128)}, f32[128,256]{1,0:T(8,128)S(1)}, f32[27,256,128]{2,1,0:T(8,128)}, s32[27]{0:T(128)S(1)}, s32[27,128]{1,0:T(8,128)S(1)}, /*index=5*/s...) while((s32[]{:T(128)}, f32[128,256]{1,0:T(8,128)S(1)}, ...), condition=%wide.region_7.8_spmd, body=%wide.region_4.7_spmd.sunk | while | flops 16878356 | bytes 1194196 | solution.py:15
  53.2 2.3 fusion.50
  62.9 2.3 fusion.50
  72.5 2.3 fusion.50
  82.1 2.3 fusion.50
  91.7 2.3 fusion.50
  101.4 2.3 fusion.50
  111.0 2.3 fusion.50
  120.7 2.3 fusion.50
  130.3 2.3 fusion.50
  139.9 2.3 fusion.50
  149.5 2.3 fusion.50
  159.1 2.3 fusion.50
  168.7 2.3 fusion.50
  178.4 2.3 fusion.50
  188.0 2.3 fusion.50
  197.6 2.3 fusion.50
  207.2 2.3 fusion.50
  216.8 2.3 fusion.50
  226.5 2.3 fusion.50
  236.1 2.3 fusion.50
  245.8 2.3 fusion.50
  255.4 2.3 fusion.50
  265.0 2.3 fusion.50
  274.7 2.3 fusion.50
  284.3 2.3 fusion.50
  293.9 2.3 fusion.50
  303.5 2.3 fusion.50
  305.8 2.4 pad.13
  308.3 4.4 copy.12
  312.7 162.2 %while.23 = (s32[]{:T(128)}, f32[1153,128]{1,0:T(8,128)S(1)}, s32[27]{0:T(128)S(1)}, s32[27,128]{1,0:T(8,128)S(1)}, s32[27,128]{1,0:T(8,128)S(1)}, /*index=5*/bf...) while((s32[]{:T(128)}, f32[1153,128]{1,0:T(8,128)S(1)}, ...), condition=%wide.region_2.3_spmd, body=%wide.region_0.2_spmd.sunk | while | flops 8406789 | bytes 532131 | solution.py:15
  317.1 1.6 scatter_fusion
  323.2 1.6 scatter_fusion
  329.2 1.6 scatter_fusion
  335.3 1.6 scatter_fusion
  341.2 1.5 scatter_fusion
  347.2 1.6 scatter_fusion
  353.3 1.6 scatter_fusion
  359.3 1.6 scatter_fusion
  365.3 1.5 scatter_fusion
  377.2 1.6 scatter_fusion
  383.2 1.6 scatter_fusion
  389.3 1.6 scatter_fusion
  395.3 1.6 scatter_fusion
  401.3 1.6 scatter_fusion
  407.3 1.6 scatter_fusion
  419.3 1.6 scatter_fusion
  425.3 1.6 scatter_fusion
  437.3 1.6 scatter_fusion
  443.3 1.6 scatter_fusion
  449.4 1.6 scatter_fusion
  455.4 1.6 scatter_fusion
  461.4 1.6 scatter_fusion
  467.4 1.6 scatter_fusion
  473.4 1.5 scatter_fusion
  475.8 7.8 %all-to-all-start = ((f32[128,8,128]{2,1,0:T(8,128)}), f32[128,8,128]{2,1,0:T(8,128)S(1)}, u32[]{:S(2)}, u32[]{:S(2)}) async-start(f32[128,8,128]{2,1,0:T(8,128)} %slice_bitcast_fusion), calls=%async_computation | async-start | bytes 1048576 | tf_op jit(solution)/shard_map/all_to_all | solution.py:48
  484.2 18.0 %all-to-all-done = f32[128,8,128]{2,1,0:T(8,128)S(1)} async-done(((f32[128,8,128]{2,1,0:T(8,128)}), f32[128,8,128]{2,1,0:T(8,128)S(1)}, u32[]{:S(2)}, u32[]{:S(2)}) %all-to-all-start) | async-done | bytes 524320 | tf_op jit(solution)/shard_map/all_to_all | solution.py:48
  502.2 6.1 %scatter_custom_fusion.2 = f32[129,128]{1,0:T(8,128)S(1)} fusion(s32[1024]{0:T(1024)S(1)} %bitcast.111, f32[128,8,128]{2,1,0:T(8,128)S(1)} %all-to-all-done, f32[]{:T(128)} %constant.59.clone.1), kind=kCustom, calls=%fused_computation.39 | custom fusion | flops 131072 | bytes 590340 | tf_op jit(solution)/shard_map/scatter-add | solution.py:52
  508.9 6.2 %reduce-scatter.2.cloned.1.call-done = f32[27,256]{1,0:T(8,128)} async-done(((f32[27,32768]{1,0:T(8,128)}), f32[27,256]{1,0:T(8,128)}) %reduce-scatter.2.cloned.1.call-update) | async-done | bytes 27664 | tf_op jit(solution)/shard_map/reduce_scatter | solution.py:78
  515.1 18.0 %psum.7 = f32[27,256]{1,0:T(8,128)S(1)} all-reduce(f32[27,256]{1,0:T(8,128)} %reduce-scatter.2.cloned.1.call-done), channel_id=1, replica_groups=mesh['space'=128,'scene'=4] {'scene'}, use_global_device_ids=true, to_apply=%region_9.10 | all-reduce | flops 6912 | bytes 55296 | tf_op jit(solution)/shard_map/psum | solution.py:79
  (402 shorter events, 219.9 us)
Async XLA Ops:
  8.7 37.1 %copy-start = (bf16[1,128,256]{2,1,0:T(8,128)(2,1)S(1)}, bf16[1,128,256]{2,1,0:T(8,128)(2,1)}, u32[]{:S(2)}) copy-start(bf16[1,128,256]{2,1,0:T(8,128)(2,1)} %param.13) | copy-start | bytes 196612
  8.7 37.1 %copy-start.1 = (s32[3]{0:T(128)S(1)}, s32[3]{0:T(128)}, u32[]{:S(2)}) copy-start(s32[3]{0:T(128)} %constant.55.clone.1) | copy-start | bytes 40
  13.0 30.4 %all-to-all-start.1 = ((bf16[128,8,128]{2,1,0:T(8,128)(2,1)}), bf16[128,8,128]{2,1,0:T(8,128)(2,1)S(1)}, u32[]{:S(2)}, u32[]{:S(2)}) async-start(bf16[128,8,128]{2,1,0:T(8,128)(2,1)} %bitcast.21), calls=%async_computation.1 | async-start | bytes 524288 | tf_op jit(solution)/shard_map/all_to_all | solution.py:36
  30.4 484.7 %reduce-scatter.2.cloned.1.call-start = ((), (), s32[]{:S(2)}) async-start(), calls=%async_computation.3 | async-start | bytes 4227072 | tf_op jit(solution)/shard_map/reduce_scatter | solution.py:78
  475.8 26.5 %all-to-all-start = ((f32[128,8,128]{2,1,0:T(8,128)}), f32[128,8,128]{2,1,0:T(8,128)S(1)}, u32[]{:S(2)}, u32[]{:S(2)}) async-start(f32[128,8,128]{2,1,0:T(8,128)} %slice_bitcast_fusion), calls=%async_computation | async-start | bytes 1048576 | tf_op jit(solution)/shard_map/all_to_all | solution.py:48
Sparse Core Ops, SparseCore 0:
  312.8 202.2 reduce-scatter.1
where the time goes:
time: 546 us; the launch traced here: 541 us
  matrix products  116 us (21%)
  other arithmetic  112 us (21%)
  local copies, waits for them, and re-layouts  111 us (20%)
  loops' own time  107 us (20%)
  waiting for transfers between devices  36.5 us (7%)
  starting transfers between devices  25.2 us (5%)
  blocking collectives  18 us (3%)
  between operations  14.1 us (3%)
    another operation x2, loops' own time, sweep_pairs(): lax.scan(advance, state, jnp.arange(offsets_total, dtype=jnp.int32))  107 us
    dot_general x27, matrix products, backward_block(): lax.dot_general(voxel_rows[in_rows], gathered, (((0,), (0,)), ((), ())),...  62.6 us
    scatter-add x27, other arithmetic, forward_block(): return partial_value.at[out_rows].add(product)  42.5 us
    scatter-add x27, other arithmetic, backward_block(): input_sums = input_sums.at[in_rows].add(back_product)  39.8 us
    dynamic_slice x54, local copies, waits for them, and re-layouts, sweep_pairs(): lax.scan(advance, state, jnp.arange(offsets_total, dtype=jnp.int32))  31.5 us
    dot_general x27, matrix products, backward_block(): lax.dot_general(gathered, weight[offset], (((1,), (1,)), ((), ())), prefe...  27 us
    dot_general x27, matrix products, forward_block(): jnp.dot(voxel_rows[in_rows], weight[offset], preferred_element_type=jnp.f...  26.7 us
    gather x27, local copies, waits for them, and re-layouts, forward_block(): voxel_rows[in_rows]  22.9 us
  transfers between devices with their start and end apart: 3, of which 3 were waited for; matrix products, arithmetic and copies ran while one was open for 22% of the time, Pallas kernels for 0%

commit v1 on v0

v1 whole, which is shorter than its diff:
```python
import math

import jax
import jax.numpy as jnp
from jax import lax
from jax.experimental import pallas as pl
from jax.experimental.pallas import tpu as pltpu
from jax.sharding import Mesh
from jax.sharding import PartitionSpec as P

F32 = jnp.float32
BF16 = jnp.bfloat16
I32 = jnp.int32
LANES = 128
VMEM_BYTES = 24 * 1024 * 1024


def call(kernel, outs, scratch=(), flops=0, moved=0):
    return pl.pallas_call(
        kernel,
        out_shape=outs,
        scratch_shapes=list(scratch),
        compiler_params=pltpu.CompilerParams(vmem_limit_bytes=VMEM_BYTES),
        cost_estimate=pl.CostEstimate(flops=flops, bytes_accessed=moved, transcendentals=0),
    )


def rows_iota(rows, start=0):
    return lax.broadcasted_iota(I32, (rows, LANES), 0) + start


def one_hot(iota, row):
    return jnp.where(iota == row, 1.0, 0.0).astype(BF16)


def split_two(value):
    high = value.astype(BF16)
    low = (value - high.astype(F32)).astype(BF16)
    return high, low


def gather_kernel(cot_ref, mask_ref, recv_ref, up_ref, out_ref):
    up = (cot_ref[...].astype(F32) * mask_ref[...].astype(F32)).astype(BF16)
    up_ref[...] = up
    iota = rows_iota(LANES)
    for g in range(recv_ref.shape[0]):
        hot = one_hot(iota, recv_ref[g : g + 1, :])
        rows = lax.dot_general(hot, up, (((0,), (0,)), ((), ())), preferred_element_type=F32)
        out_ref[g * LANES : (g + 1) * LANES, :] = rows.astype(BF16)


def forward_kernel(x_ref, w_ref, in_ref, out_ref, table_ref, own_ref, send_ref, terms_ref, hot_ref):
    offsets = w_ref.shape[0]
    no_target = own_ref.shape[0] + send_ref.shape[0]
    iota = rows_iota(LANES)
    picks = rows_iota(16)

    def product(k, carry):
        hot = one_hot(iota, in_ref[pl.ds(k, 1), :])
        target = out_ref[pl.ds(k, 1), :]
        code = jnp.where(target < no_target, target + 1, 0)
        digits = jnp.where(picks == 0, code >> 7, jnp.where(picks == 1, code & 127, 0))
        found = lax.dot_general(
            digits.astype(F32).astype(BF16), hot, (((1,), (1,)), ((), ())), preferred_element_type=F32
        )
        table_ref[pl.ds(k, 1), :] = (found[0:1] * 128.0 + found[1:2] - 1.0).astype(I32)
        high, low = split_two(jnp.dot(x_ref[...], w_ref[k], preferred_element_type=F32))
        spot = pl.ds(pl.multiple_of(k * LANES, LANES), LANES)
        terms_ref[spot, 0:LANES] = high
        terms_ref[spot, LANES : 2 * LANES] = low
        return carry

    lax.fori_loop(0, offsets, product, 0)

    def block(start):
        here = iota + start
        for k in range(offsets):
            hot_ref[:, k * LANES : (k + 1) * LANES] = one_hot(here, table_ref[k : k + 1, :])
        both = jnp.dot(hot_ref[...], terms_ref[...], preferred_element_type=F32)
        return both[:, :LANES] + both[:, LANES:]

    own_ref[...] = block(0)

    def scatter(b, carry):
        spot = pl.ds(pl.multiple_of(b * LANES, LANES), LANES)
        send_ref[spot, :] = block((b + 1) * LANES)
        return carry

    lax.fori_loop(0, send_ref.shape[0] // LANES, scatter, 0)


def backward_kernel(up_ref, back_ref, table_ref, w_ref, gathered_ref, grad_ref, ext_ref, sum_ref):
    offsets = w_ref.shape[0]
    blocks = back_ref.shape[0] // LANES
    ext_ref[:, 0:LANES] = up_ref[...].T
    for b in range(blocks):
        ext_ref[:, (b + 1) * LANES : (b + 2) * LANES] = back_ref[b * LANES : (b + 1) * LANES, :].T
    iota = rows_iota((blocks + 1) * LANES)
    sum_ref[...] = jnp.zeros_like(sum_ref)

    def step(k, carry):
        hot = one_hot(iota, table_ref[pl.ds(k, 1), :])
        rows = jnp.dot(ext_ref[...], hot, preferred_element_type=F32).astype(BF16)
        gathered_ref[pl.ds(pl.multiple_of(k * LANES, LANES), LANES), :] = rows
        sum_ref[...] += jnp.dot(w_ref[k], rows, preferred_element_type=F32)
        return carry

    lax.fori_loop(0, offsets, step, 0)
    grad_ref[...] = sum_ref[...].T.astype(BF16)


def receive_kernel(own_ref, arrived_ref, recv_ref, out_ref):
    iota = rows_iota(LANES)
    total = own_ref[...]
    for g in range(recv_ref.shape[0]):
        hot = one_hot(iota, recv_ref[g : g + 1, :])
        high, low = split_two(arrived_ref[g * LANES : (g + 1) * LANES, :])
        total += jnp.dot(hot, high, preferred_element_type=F32)
        total += jnp.dot(hot, low, preferred_element_type=F32)
    out_ref[...] = total.astype(BF16)


def kernel_grad_kernel(g_ref, x_ref, out_ref):
    columns = g_ref.shape[1]
    total = jnp.dot(g_ref[0], x_ref[0], preferred_element_type=F32)
    for s in range(1, g_ref.shape[0]):
        total += jnp.dot(g_ref[s], x_ref[s], preferred_element_type=F32)
    wide = -(-columns // LANES) * LANES
    total = jnp.concatenate([total, jnp.zeros((wide - columns, total.shape[1]), F32)], axis=0)
    out_ref[...] = total.T


def local(features, cotangent, relu_mask, weight, pair_in, pair_out, recv_index):
    space = ("y", "z", "core")
    ring = ("z", "core")
    x = features[0]
    own_rows, in_width = x.shape
    offsets, unused, out_width = weight.shape
    peers = lax.axis_size(space)
    send_rows = recv_index.shape[2]
    slots = send_rows // peers
    recv = recv_index.reshape(send_rows // LANES, LANES)
    pairs_in = pair_in[0, 0]
    pairs_out = pair_out[0, 0]
    shape = jax.ShapeDtypeStruct

    upstream, outgoing = call(
        gather_kernel,
        (shape((own_rows, out_width), BF16), shape((send_rows, out_width), BF16)),
        flops=2 * send_rows * own_rows * out_width,
        moved=send_rows * out_width * 3,
    )(cotangent[0], relu_mask[0], recv)
    returned = lax.all_to_all(outgoing.reshape(peers, slots, out_width), space, 0, 0, tiled=True)

    ring_size = lax.axis_size(ring)
    group_x = lax.all_gather(x, ring)

    table, own, outbound = call(
        forward_kernel,
        (
            shape((offsets, own_rows), I32),
            shape((own_rows, out_width), F32),
            shape((send_rows, out_width), F32),
        ),
        scratch=(
            pltpu.VMEM((offsets * own_rows, 2 * out_width), BF16),
            pltpu.VMEM((LANES, offsets * own_rows), BF16),
        ),
        flops=2 * (own_rows + send_rows) * offsets * own_rows * out_width * 2,
        moved=4 * offsets * in_width * out_width,
    )(x, weight, pairs_in, pairs_out)
    arrived = lax.all_to_all(outbound.reshape(peers, slots, out_width), space, 0, 0, tiled=True)

    gathered, input_grad = call(
        backward_kernel,
        (shape((offsets * out_width, own_rows), BF16), shape((own_rows, in_width), BF16)),
        scratch=(
            pltpu.VMEM((out_width, own_rows + send_rows), BF16),
            pltpu.VMEM((in_width, own_rows), F32),
        ),
        flops=2 * (own_rows + send_rows) * offsets * own_rows * out_width,
        moved=4 * offsets * in_width * out_width,
    )(upstream, returned.reshape(send_rows, out_width), table, weight)

    conv_out = call(
        receive_kernel,
        shape((own_rows, out_width), BF16),
        flops=4 * send_rows * own_rows * out_width,
        moved=send_rows * out_width * 4,
    )(own, arrived.reshape(send_rows, out_width), recv)

    columns = offsets * out_width // ring_size
    wide = -(-columns // LANES) * LANES
    group_g = lax.all_to_all(gathered.reshape(ring_size, columns, own_rows), ring, 0, 0, tiled=True)
    partial = call(
        kernel_grad_kernel,
        shape((in_width, wide), F32),
        flops=2 * columns * in_width * own_rows * ring_size,
        moved=4 * in_width * wide,
    )(group_g, group_x)
    y_size = lax.axis_size("y")
    parts = lax.all_to_all(partial.reshape(y_size, in_width // y_size, wide), "y", 0, 0, tiled=True)
    summed = parts.sum(axis=0)

    scenes = lax.axis_size("scene")
    own_in = in_width // peers
    last = jnp.broadcast_to(
        summed.reshape(ring_size, 1, own_in, wide), (ring_size, scenes, own_in, wide)
    ).reshape(ring_size * scenes, own_in, wide)
    last = lax.all_to_all(last, ("z", "core", "scene"), 0, 0, tiled=True)
    reduced = last.reshape(ring_size, scenes, own_in, wide).sum(axis=1)[:, :, :columns]
    reduced = reduced.transpose(1, 0, 2).reshape(own_in, offsets, out_width)
    reduced = reduced.transpose(1, 0, 2).reshape(offsets, own_in * out_width)
    normalizer = 1.0 / math.sqrt(scenes * peers * own_rows)
    return (conv_out[None], input_grad[None], reduced * normalizer)


def solution(mesh):
    space, scenes = mesh.devices.shape
    fine = Mesh(mesh.devices.reshape(8, space // 16, 2, scenes), ("y", "z", "core", "scene"))
    voxels = P("scene", ("y", "z", "core"))
    return jax.shard_map(
        local,
        mesh=fine,
        in_specs=(voxels, voxels, voxels, P(), voxels, voxels, voxels),
        out_specs=(voxels, voxels, P(None, ("y", "z", "core"))),
        check_vma=False,
    )
```

time: 546 us -> 158 us (0.29)
  the two profiles are of different devices: /device:TPU:24 before, /device:TPU:1 now
where the time goes in v1:
time: 158 us
  waiting for transfers between devices  54.1 us (34%)
  starting transfers between devices  40.3 us (26%)
  Pallas kernels  23.6 us (15%)
  blocking collectives  17.4 us (11%)
  between operations  14.1 us (9%)
  local copies, waits for them, and re-layouts  8.02 us (5%)
    all_to_all x1, waiting for transfers between devices, local(): lax.all_to_all(outbound.reshape(peers, slots, out_width), space, 0, 0, ti...  19.4 us
    all_gather x1, waiting for transfers between devices, local(): group_x = lax.all_gather(x, ring)  19.3 us
    all_to_all x1, starting transfers between devices, local(): lax.all_to_all(outgoing.reshape(peers, slots, out_width), space, 0, 0, ti...  18.4 us
    all_to_all x1, blocking collectives, local(): lax.all_to_all(partial.reshape(y_size, in_width // y_size, wide), 'y', 0,...  17.4 us
    pallas_call x1, Pallas kernels, local(): call(backward_kernel, (shape((offsets * out_width, own_rows), BF16), shap...  11.4 us
    pallas_call x1, Pallas kernels, local(): call(forward_kernel, (shape((offsets, own_rows), I32), shape((own_rows, o...  9.61 us
    all_to_all x1, waiting for transfers between devices, local(): last = lax.all_to_all(last, ('z', 'core', 'scene'), 0, 0, tiled=True)  9.01 us
    all_to_all x1, starting transfers between devices, local(): lax.all_to_all(outbound.reshape(peers, slots, out_width), space, 0, 0, ti...  7.93 us
  transfers between devices with their start and end apart: 5, of which 5 were waited for; matrix products, arithmetic and copies ran while one was open for 0% of the time, Pallas kernels for 14%

profile of v1, /device:TPU:1, one launch (start us, length us, event | category | flops | bytes accessed | tf_op | source)
XLA Modules:
  0.0 157.5 jit_solution(866837473415477928)
XLA Ops:
  7.2 0.0 copy-start.2
  7.2 0.7 copy-done.2
  7.9 0.0 copy-start.6
  7.9 0.8 copy-done.6
  8.7 0.0 copy-start.7
  8.7 0.8 copy-done.7
  9.5 1.0 shard_map.96
  10.4 18.4 %all-to-all-start.1 = ((bf16[128,8,128]{2,1,0:T(8,128)(2,1)}), bf16[128,8,128]{2,1,0:T(8,128)(2,1)S(1)}, u32[]{:S(2)}, u32[]{:S(2)}) async-start(bf16[128,8,128]{2,1,0:T(8,128)(2,1)} %bitcast.7), calls=%async_computation.1 | async-start | bytes 524288 | tf_op jit(solution)/shard_map/all_to_all | solution.py:153
  28.9 0.0 all-gather.2.cloned.1.call-start
  28.9 0.7 all-gather.2.cloned.1.call-update
  29.6 0.7 copy_bitcast_fusion
  30.3 0.0 copy-start.1
  30.3 0.8 copy-done.1
  31.2 0.0 copy-start.4
  31.2 1.5 copy-done.4
  32.7 0.0 copy-start.5
  32.7 9.6 %shard_map.94 = (s32[27,128]{1,0:T(8,128)S(1)}, f32[128,128]{1,0:T(8,128)S(1)}, f32[1024,128]{1,0:T(8,128)}) custom-call(bf16[128,256]{1,0:T(8,128)(2,1)S(1)} %bitcast.29, bf16[27,256,128]{2,1,0:T(8,128)(2,1)S(1)} %copy-done.4, s32[27,128]{1,0:T(8,128)S(1)} %get-tuple-element.18.in_ref, s32[27,128]{1,0:T(8,128)S(1)} %get-tuple-element.17.out_ref), custom_call_target="tpu_custom_call" | custom-call | flops 2038431744 | bytes 3538944 | tf_op jit(solution)/shard_map/pallas_call | solution.py:158
  42.3 0.8 all-to-all-done.1
  43.1 0.0 copy-done.5
  43.1 11.4 %shard_map.97 = (bf16[3456,128]{1,0:T(8,128)(2,1)}, bf16[128,256]{1,0:T(8,128)(2,1)}) custom-call(bf16[128,128]{1,0:T(8,128)(2,1)S(1)} %get-tuple-element.12.up_ref, bf16[1024,128]{1,0:T(8,128)(2,1)S(1)} %bitcast.28, s32[27,128]{1,0:T(8,128)S(1)} %get-tuple-element.14.table_ref, bf16[27,256,128]{2,1,0:T(8,128)(2,1)S(1)} %copy-done.5), custom_call_target="tpu_custom_call" | custom-call | flops 1019215872 | bytes 3538944 | tf_op jit(solution)/shard_map/pallas_call | solution.py:174
  54.5 0.0 copy-start.3
  54.5 6.5 %all-to-all-start.2 = ((bf16[16,216,128]{2,1,0:T(8,128)(2,1)}), bf16[16,216,128]{2,1,0:T(8,128)(2,1)S(1)}, u32[]{:S(2)}, u32[]{:S(2)}) async-start(bf16[16,216,128]{2,1,0:T(8,128)(2,1)} %bitcast.10), calls=%async_computation.2 | async-start | bytes 1769472 | tf_op jit(solution)/shard_map/all_to_all | solution.py:194
  61.0 19.3 %all-gather.2.cloned.1.call-done.x_ref = bf16[16,128,256]{2,1,0:T(8,128)(2,1)} async-done(((bf16[1,128,256]{2,1,0:T(8,128)(2,1)}), bf16[16,128,256]{2,1,0:T(8,128)(2,1)}) %all-gather.2.cloned.1.call-update) | async-done | bytes 1048592 | tf_op jit(solution)/shard_map/all_gather | solution.py:156
  80.3 4.9 %all-to-all-done.2.g_ref = bf16[16,216,128]{2,1,0:T(8,128)(2,1)S(1)} async-done(((bf16[16,216,128]{2,1,0:T(8,128)(2,1)}), bf16[16,216,128]{2,1,0:T(8,128)(2,1)S(1)}, u32[]{:S(2)}, u32[]{:S(2)}) %all-to-all-start.2) | async-done | bytes 884768 | tf_op jit(solution)/shard_map/all_to_all | solution.py:194
  85.2 0.0 copy-start
  85.2 1.2 copy-done
  86.4 0.7 shard_map.98
  87.1 17.4 %all_to_all.25 = f32[8,32,256]{2,1,0:T(8,128)S(1)} all-to-all(f32[8,32,256]{2,1,0:T(8,128)S(1)} %bitcast.27), channel_id=1, replica_groups=mesh['y'=8,'z'=8,'core'=2,'scene'=4] {'y'}, dimensions={0} | all-to-all | bytes 524288 | tf_op jit(solution)/shard_map/all_to_all | solution.py:202
  104.5 7.9 %all-to-all-start = ((f32[128,8,128]{2,1,0:T(8,128)}), f32[128,8,128]{2,1,0:T(8,128)S(1)}, u32[]{:S(2)}, u32[]{:S(2)}) async-start(f32[128,8,128]{2,1,0:T(8,128)} %bitcast.1), calls=%async_computation | async-start | bytes 1048576 | tf_op jit(solution)/shard_map/all_to_all | solution.py:172
  112.5 19.4 %all-to-all-done = f32[128,8,128]{2,1,0:T(8,128)S(1)} async-done(((f32[128,8,128]{2,1,0:T(8,128)}), f32[128,8,128]{2,1,0:T(8,128)S(1)}, u32[]{:S(2)}, u32[]{:S(2)}) %all-to-all-start) | async-done | bytes 524320 | tf_op jit(solution)/shard_map/all_to_all | solution.py:172
  131.9 0.7 broadcast_in_dim.16
  132.6 7.3 %all-to-all-start.4 = ((f32[64,2,256]{2,1,0:T(2,128)}), f32[64,2,256]{2,1,0:T(2,128)S(1)}, u32[]{:S(2)}, u32[]{:S(2)}) async-start(f32[64,2,256]{2,1,0:T(2,128)} %bitcast.12), calls=%async_computation.4 | async-start | bytes 262144 | tf_op jit(solution)/shard_map/all_to_all | solution.py:210
  139.9 0.0 copy-done.3
  139.9 0.9 shard_map.95
  140.8 9.0 %all-to-all-done.4 = f32[64,2,256]{2,1,0:T(2,128)S(1)} async-done(((f32[64,2,256]{2,1,0:T(2,128)}), f32[64,2,256]{2,1,0:T(2,128)S(1)}, u32[]{:S(2)}, u32[]{:S(2)}) %all-to-all-start.4) | async-done | bytes 131104 | tf_op jit(solution)/shard_map/all_to_all | solution.py:210
  149.9 0.1 mul.21
  150.1 0.6 copy.19
  (6 shorter events, 0.1 us)
Async XLA Ops:
  7.2 0.7 copy-start.2
  7.9 0.8 copy-start.6
  8.7 0.8 copy-start.7
  10.4 32.7 %all-to-all-start.1 = ((bf16[128,8,128]{2,1,0:T(8,128)(2,1)}), bf16[128,8,128]{2,1,0:T(8,128)(2,1)S(1)}, u32[]{:S(2)}, u32[]{:S(2)}) async-start(bf16[128,8,128]{2,1,0:T(8,128)(2,1)} %bitcast.7), calls=%async_computation.1 | async-start | bytes 524288 | tf_op jit(solution)/shard_map/all_to_all | solution.py:153
  28.9 51.4 %all-gather.2.cloned.1.call-start = ((), (), s32[]{:S(2)}) async-start(), calls=%async_computation.5 | async-start | bytes 1114112 | tf_op jit(solution)/shard_map/all_gather | solution.py:156
  30.3 0.8 copy-start.1
  31.2 1.5 copy-start.4
  32.7 10.4 %copy-start.5 = (bf16[27,256,128]{2,1,0:T(8,128)(2,1)S(1)}, bf16[27,256,128]{2,1,0:T(8,128)(2,1)}, u32[]{:S(2)}) copy-start(bf16[27,256,128]{2,1,0:T(8,128)(2,1)} %w_ref.3) | copy-start | bytes 5308420
  54.5 85.4 %copy-start.3 = (s32[1,1,1024]{2,1,0:T(1,128)S(1)}, s32[1,1,1024]{2,1,0:T(1,128)}, u32[]{:S(2)}) copy-start(s32[1,1,1024]{2,1,0:T(1,128)} %param.13) | copy-start | bytes 12292
  54.5 30.7 %all-to-all-start.2 = ((bf16[16,216,128]{2,1,0:T(8,128)(2,1)}), bf16[16,216,128]{2,1,0:T(8,128)(2,1)S(1)}, u32[]{:S(2)}, u32[]{:S(2)}) async-start(bf16[16,216,128]{2,1,0:T(8,128)(2,1)} %bitcast.10), calls=%async_computation.2 | async-start | bytes 1769472 | tf_op jit(solution)/shard_map/all_to_all | solution.py:194
  85.2 1.2 copy-start
  104.5 27.4 %all-to-all-start = ((f32[128,8,128]{2,1,0:T(8,128)}), f32[128,8,128]{2,1,0:T(8,128)S(1)}, u32[]{:S(2)}, u32[]{:S(2)}) async-start(f32[128,8,128]{2,1,0:T(8,128)} %bitcast.1), calls=%async_computation | async-start | bytes 1048576 | tf_op jit(solution)/shard_map/all_to_all | solution.py:172
  132.6 17.3 %all-to-all-start.4 = ((f32[64,2,256]{2,1,0:T(2,128)}), f32[64,2,256]{2,1,0:T(2,128)S(1)}, u32[]{:S(2)}, u32[]{:S(2)}) async-start(f32[64,2,256]{2,1,0:T(2,128)} %bitcast.12), calls=%async_computation.4 | async-start | bytes 262144 | tf_op jit(solution)/shard_map/all_to_all | solution.py:210
Sparse Core Ops, SparseCore 0:
  31.8 48.4 all-gather.1

commit v2 on v1

v2 whole, which is shorter than its diff:
```python
import functools
import math

import jax
import jax.numpy as jnp
from jax import lax
from jax.experimental import pallas as pl
from jax.experimental.pallas import tpu as pltpu
from jax.sharding import Mesh
from jax.sharding import PartitionSpec as P

F32 = jnp.float32
BF16 = jnp.bfloat16
I32 = jnp.int32
LANES = 128
STEP = 3
VMEM_BYTES = 24 * 1024 * 1024
SPACE = ("y", "zh", "zl", "core")
GROUP = ("zl", "core", "scene")


def call(kernel, outs, scratch=(), flops=0, moved=0):
    return pl.pallas_call(
        kernel,
        out_shape=outs,
        scratch_shapes=list(scratch),
        compiler_params=pltpu.CompilerParams(vmem_limit_bytes=VMEM_BYTES),
        cost_estimate=pl.CostEstimate(flops=flops, bytes_accessed=moved, transcendentals=0),
    )


def rows_iota(rows, start=0):
    return lax.broadcasted_iota(I32, (rows, LANES), 0) + start


def one_hot(iota, row):
    return jnp.where(iota == row, 1.0, 0.0).astype(BF16)


def split_two(value):
    high = value.astype(BF16)
    low = (value - high.astype(F32)).astype(BF16)
    return high, low


def lane_block(k):
    return slice(k * LANES, (k + 1) * LANES)


def gather_kernel(cot_ref, mask_ref, recv_ref, up_ref, out_ref):
    up = (cot_ref[...].astype(F32) * mask_ref[...].astype(F32)).astype(BF16)
    up_ref[...] = up
    iota = rows_iota(LANES)
    for g in range(recv_ref.shape[0]):
        hot = one_hot(iota, recv_ref[g : g + 1, :])
        rows = lax.dot_general(hot, up, (((0,), (0,)), ((), ())), preferred_element_type=F32)
        out_ref[lane_block(g), :] = rows.astype(BF16)


def table_kernel(in_ref, out_ref, table_ref, *, targets):
    iota = rows_iota(LANES)
    picks = rows_iota(16)
    for k in range(in_ref.shape[0]):
        hot = one_hot(iota, in_ref[k : k + 1, :])
        target = out_ref[k : k + 1, :]
        code = jnp.where(target < targets, target + 1, 0)
        digits = jnp.where(picks == 0, code >> 7, jnp.where(picks == 1, code & 127, 0))
        found = lax.dot_general(
            digits.astype(F32).astype(BF16), hot, (((1,), (1,)), ((), ())), preferred_element_type=F32
        )
        table_ref[k : k + 1, :] = (found[0:1] * 128.0 + found[1:2] - 1.0).astype(I32)


def lookup_kernel(up_ref, back_ref, table_ref, gathered_ref, ext_ref, hot_ref):
    blocks = back_ref.shape[0] // LANES
    offsets = table_ref.shape[0]
    ext_ref[:, 0:LANES] = up_ref[...].T
    for b in range(blocks):
        ext_ref[:, lane_block(b + 1)] = back_ref[lane_block(b), :].T
    iota = rows_iota((blocks + 1) * LANES)
    step = STEP
    for first in range(0, offsets, step):
        count = min(step, offsets - first)
        slot = (first // step) % 2
        for k in range(count):
            hot_ref[slot, :, lane_block(k)] = one_hot(iota, table_ref[first + k : first + k + 1, :])
        rows = jnp.dot(
            ext_ref[...], hot_ref[slot, :, : count * LANES], preferred_element_type=F32
        ).astype(BF16)
        for k in range(count):
            gathered_ref[lane_block(first + k), :] = rows[:, lane_block(k)]


def forward_kernel(x_ref, w_ref, table_ref, gathered_ref, own_ref, send_ref, grad_ref, terms_ref, hot_ref):
    offsets = w_ref.shape[0]
    total = jnp.zeros((w_ref.shape[1], LANES), F32)
    for k in range(offsets):
        high, low = split_two(jnp.dot(x_ref[...], w_ref[k], preferred_element_type=F32))
        terms_ref[lane_block(k), 0:LANES] = high
        terms_ref[lane_block(k), LANES : 2 * LANES] = low
        total += jnp.dot(w_ref[k], gathered_ref[lane_block(k), :], preferred_element_type=F32)
    grad_ref[...] = total.T.astype(BF16)

    def block(start):
        here = rows_iota(LANES) + start
        for k in range(offsets):
            hot_ref[:, lane_block(k)] = one_hot(here, table_ref[k : k + 1, :])
        both = jnp.dot(hot_ref[...], terms_ref[...], preferred_element_type=F32)
        return both[:, :LANES] + both[:, LANES:]

    own_ref[...] = block(0)

    def scatter(b, carry):
        send_ref[pl.ds(pl.multiple_of(b * LANES, LANES), LANES), :] = block((b + 1) * LANES)
        return carry

    lax.fori_loop(0, send_ref.shape[0] // LANES, scatter, 0)


def pack_kernel(g_ref, x_ref, send_ref, out_ref, turn_ref):
    columns = g_ref.shape[1]
    peers = x_ref.shape[2] // 2
    total = jnp.dot(g_ref[0], x_ref[0], preferred_element_type=F32)
    for s in range(1, g_ref.shape[0]):
        total += jnp.dot(g_ref[s], x_ref[s], preferred_element_type=F32)
    total = jnp.concatenate([total, jnp.zeros((2 * LANES - columns, total.shape[1]), F32)], axis=0)
    for half in range(2):
        turn_ref[half] = total[lane_block(half), :].T
    for r in range(8):
        out_ref[pl.ds(r, peers, stride=12), :] = send_ref[pl.ds(r, peers, stride=8), :]
    for c in range(2):
        for half in range(2):
            rows = turn_ref[half, pl.ds(c, peers, stride=2), :]
            out_ref[pl.ds(8 + 2 * c + half, peers, stride=12), :] = rows


def sum_kernel(arrived_ref, out_ref):
    total = arrived_ref[0]
    for i in range(1, arrived_ref.shape[0]):
        total += arrived_ref[i]
    for s in range(out_ref.shape[0]):
        for i in range(4):
            out_ref[s, 4 * i : 4 * i + 4, :] = total[12 * i + 8 : 12 * i + 12, :]


def receive_kernel(own_ref, arrived_ref, recv_ref, out_ref, rows_ref):
    peers = arrived_ref.shape[0] // 12
    iota = rows_iota(LANES)
    for r in range(8):
        rows_ref[pl.ds(r, peers, stride=8), :] = arrived_ref[pl.ds(r, peers, stride=12), :]
    total = own_ref[...]
    for g in range(recv_ref.shape[0]):
        hot = one_hot(iota, recv_ref[g : g + 1, :])
        high, low = split_two(rows_ref[lane_block(g), :])
        total += jnp.dot(hot, high, preferred_element_type=F32)
        total += jnp.dot(hot, low, preferred_element_type=F32)
    out_ref[...] = total.astype(BF16)


def local(features, cotangent, relu_mask, weight, pair_in, pair_out, recv_index):
    x = features[0]
    own_rows, in_width = x.shape
    offsets, unused, out_width = weight.shape
    peers = lax.axis_size(SPACE)
    group = lax.axis_size(GROUP)
    scenes = lax.axis_size("scene")
    send_rows = recv_index.shape[2]
    slots = send_rows // peers
    targets = own_rows + send_rows
    columns = offsets * out_width // group
    recv = recv_index.reshape(send_rows // LANES, LANES)
    shape = jax.ShapeDtypeStruct

    group_x = lax.all_gather(x, GROUP)
    upstream, outgoing = call(
        gather_kernel,
        (shape((own_rows, out_width), BF16), shape((send_rows, out_width), BF16)),
        flops=2 * send_rows * own_rows * out_width,
        moved=send_rows * out_width * 3,
    )(cotangent[0], relu_mask[0], recv)
    returned = lax.all_to_all(outgoing.reshape(peers, slots, out_width), SPACE, 0, 0, tiled=True)

    table = call(
        functools.partial(table_kernel, targets=targets),
        shape((offsets, own_rows), I32),
        flops=2 * targets * offsets * own_rows * 100,
    )(pair_in[0, 0], pair_out[0, 0])

    gathered = call(
        lookup_kernel,
        shape((offsets * out_width, own_rows), BF16),
        scratch=(pltpu.VMEM((out_width, targets), BF16), pltpu.VMEM((2, targets, STEP * LANES), BF16)),
        flops=2 * targets * offsets * own_rows * out_width,
        moved=2 * offsets * own_rows * out_width,
    )(upstream, returned.reshape(send_rows, out_width), table)

    gathered, group_x = lax.optimization_barrier((gathered, group_x))
    group_g = lax.all_to_all(gathered.reshape(group, columns, own_rows), GROUP, 0, 0, tiled=True)

    own, outbound, input_grad = call(
        forward_kernel,
        (
            shape((own_rows, out_width), F32),
            shape((send_rows, out_width), F32),
            shape((own_rows, in_width), BF16),
        ),
        scratch=(
            pltpu.VMEM((offsets * own_rows, 2 * out_width), BF16),
            pltpu.VMEM((LANES, offsets * own_rows), BF16),
        ),
        flops=4 * targets * offsets * own_rows * out_width,
        moved=4 * offsets * in_width * out_width,
    )(x, weight, table, gathered)

    packed = call(
        pack_kernel,
        shape((peers * 12, LANES), F32),
        scratch=(pltpu.VMEM((2, in_width, LANES), F32),),
        flops=2 * columns * in_width * own_rows * group,
        moved=peers * 12 * LANES * 8,
    )(group_g, group_x, outbound)
    arrived = lax.all_to_all(packed.reshape(peers, 1, 12 * LANES), SPACE, 0, 0, tiled=True)
    arrived = arrived.reshape(peers * 12, LANES)

    quarter = call(sum_kernel, shape((scenes, 16, LANES), F32), moved=peers * 12 * LANES * 4)(
        arrived.reshape(peers // 4, 48, LANES)
    )
    blocks = lax.all_to_all(quarter, "scene", 0, 0, tiled=True)
    conv_out = call(
        receive_kernel,
        shape((own_rows, out_width), BF16),
        scratch=(pltpu.VMEM((send_rows, out_width), F32),),
        flops=4 * send_rows * own_rows * out_width,
        moved=send_rows * out_width * 4,
    )(own, arrived, recv)

    own_in = in_width // peers
    blocks = blocks.reshape(scenes, 4, own_in, 2 * LANES)[:, :, :, :columns]
    kernel_grad = blocks.transpose(2, 1, 0, 3).reshape(own_in, offsets, out_width)
    kernel_grad = kernel_grad.transpose(1, 0, 2).reshape(offsets, own_in * out_width)
    normalizer = 1.0 / math.sqrt(scenes * peers * own_rows)
    return (conv_out[None], input_grad[None], kernel_grad * normalizer)


def solution(mesh):
    scenes = mesh.devices.shape[1]
    fine = Mesh(mesh.devices.reshape(8, 4, 2, 2, scenes), ("y", "zh", "zl", "core", "scene"))
    voxels = P("scene", SPACE)
    return jax.shard_map(
        local,
        mesh=fine,
        in_specs=(voxels, voxels, voxels, P(), voxels, voxels, voxels),
        out_specs=(voxels, voxels, P(None, SPACE)),
        check_vma=False,
    )
```

time: 158 us -> 145 us (0.918)
  blocking collectives: 17.4 us -> 40.4 us
  starting transfers between devices: 40.3 us -> 27.6 us
  waiting for transfers between devices: 54.1 us -> 41.6 us
  Pallas kernels: 23.6 us -> 14.8 us
  local copies, waits for them, and re-layouts: 8.02 us -> 5.28 us
    all_to_all x1, blocking collectives: 17.4 us -> 40.4 us  [local(): lax.all_to_all(packed.reshape(peers, 1, 12 * LANES), SPACE, 0, 0, tiled=T...]
    all_to_all x4 -> x3, starting transfers between devices: 40.2 us -> 27.5 us  [the longest x1 18.4 us: local(): lax.all_to_all(outgoing.reshape(peers, slots, out_width), SPACE, 0, 0, ti...]
    all_to_all x4 -> x3, waiting for transfers between devices: 34.1 us -> 22 us  [the longest x1 12.9 us: local(): lax.all_to_all(outgoing.reshape(peers, slots, out_width), SPACE, 0, 0, ti...]
    pallas_call x4 -> x6, Pallas kernels: 22.6 us -> 13.9 us  [the longest x1 6.46 us: local(): call(forward_kernel, (shape((own_rows, out_width), F32), shape((send_rows...]
    unnamed x19 -> x17, local copies, waits for them, and re-layouts: 7.19 us -> 5.13 us
  transfers between devices with their start and end apart: 5 -> 4, of which waited for: 5 -> 4; matrix products, arithmetic and copies ran while one was open for 0% -> 1% of each run, Pallas kernels for 14% -> 9%
where the time goes in v2:
time: 145 us; the launch traced here: 144 us
  waiting for transfers between devices  41.6 us (29%)
  blocking collectives  40.4 us (28%)
  starting transfers between devices  27.6 us (19%)
  Pallas kernels  14.8 us (10%)
  between operations  14.1 us (10%)
  local copies, waits for them, and re-layouts  5.28 us (4%)
    all_to_all x1, blocking collectives, local(): lax.all_to_all(packed.reshape(peers, 1, 12 * LANES), SPACE, 0, 0, tiled=T...  40.4 us
    all_gather x1, waiting for transfers between devices, local(): group_x = lax.all_gather(x, GROUP)  19 us
    all_to_all x1, starting transfers between devices, local(): lax.all_to_all(outgoing.reshape(peers, slots, out_width), SPACE, 0, 0, ti...  18.4 us
    all_to_all x1, waiting for transfers between devices, local(): lax.all_to_all(outgoing.reshape(peers, slots, out_width), SPACE, 0, 0, ti...  12.9 us
    pallas_call x1, Pallas kernels, local(): call(forward_kernel, (shape((own_rows, out_width), F32), shape((send_rows...  6.46 us
    all_to_all x1, starting transfers between devices, local(): lax.all_to_all(gathered.reshape(group, columns, own_rows), GROUP, 0, 0, t...  5.84 us
    all_to_all x1, waiting for transfers between devices, local(): lax.all_to_all(gathered.reshape(group, columns, own_rows), GROUP, 0, 0, t...  5.76 us
    unnamed x17, local copies, waits for them, and re-layouts  5.13 us
  transfers between devices with their start and end apart: 4, of which 4 were waited for; matrix products, arithmetic and copies ran while one was open for 1% of the time, Pallas kernels for 9%

profile of v2, /device:TPU:1, one launch (start us, length us, event | category | flops | bytes accessed | tf_op | source)
XLA Modules:
  0.0 143.8 jit_solution(7063829307999270813)
XLA Ops:
  7.2 0.0 all-gather.2.cloned.1.call-start
  7.2 0.7 all-gather.2.cloned.1.call-update
  7.9 0.0 copy-start.2
  7.9 0.7 copy-done.2
  8.6 0.0 copy-start.5
  8.6 0.8 copy-done.5
  9.4 0.0 copy-start.6
  9.4 0.8 copy-done.6
  10.2 1.0 shard_map.95
  11.2 18.4 %all-to-all-start = ((bf16[128,8,128]{2,1,0:T(8,128)(2,1)}), bf16[128,8,128]{2,1,0:T(8,128)(2,1)S(1)}, u32[]{:S(2)}, u32[]{:S(2)}) async-start(bf16[128,8,128]{2,1,0:T(8,128)(2,1)} %bitcast.4), calls=%async_computation | async-start | bytes 524288 | tf_op jit(solution)/shard_map/all_to_all | solution.py:181
  29.6 0.7 copy_bitcast_fusion
  30.3 0.6 shard_map.94.table_ref
  30.9 12.9 %all-to-all-done = bf16[128,8,128]{2,1,0:T(8,128)(2,1)S(1)} async-done(((bf16[128,8,128]{2,1,0:T(8,128)(2,1)}), bf16[128,8,128]{2,1,0:T(8,128)(2,1)S(1)}, u32[]{:S(2)}, u32[]{:S(2)}) %all-to-all-start) | async-done | bytes 262176 | tf_op jit(solution)/shard_map/all_to_all | solution.py:181
  43.8 4.4 %shard_map.96.gathered_ref = bf16[3456,128]{1,0:T(8,128)(2,1)} custom-call(bf16[128,128]{1,0:T(8,128)(2,1)S(1)} %get-tuple-element.10.up_ref, bf16[1024,128]{1,0:T(8,128)(2,1)S(1)} %bitcast.26, s32[27,128]{1,0:T(8,128)S(1)} %shard_map.94.table_ref), custom_call_target="tpu_custom_call" | custom-call | flops 1019215872 | bytes 884736 | tf_op jit(solution)/shard_map/pallas_call | solution.py:189
  48.2 0.0 copy-start.1
  48.2 19.0 %all-gather.2.cloned.1.call-done.x_ref = bf16[16,128,256]{2,1,0:T(8,128)(2,1)} async-done(((bf16[1,128,256]{2,1,0:T(8,128)(2,1)}), bf16[16,128,256]{2,1,0:T(8,128)(2,1)}) %all-gather.2.cloned.1.call-update) | async-done | bytes 1048592 | tf_op jit(solution)/shard_map/all_gather | solution.py:174
  67.2 5.8 %all-to-all-start.1 = ((bf16[16,216,128]{2,1,0:T(8,128)(2,1)}), bf16[16,216,128]{2,1,0:T(8,128)(2,1)S(1)}, u32[]{:S(2)}, u32[]{:S(2)}) async-start(bf16[16,216,128]{2,1,0:T(8,128)(2,1)} %bitcast.6), calls=%async_computation.1 | async-start | bytes 1769472 | tf_op jit(solution)/shard_map/all_to_all | solution.py:198
  73.0 0.0 copy-done.1
  73.0 0.0 copy-start.4
  73.1 1.5 %copy-done.4 = bf16[27,256,128]{2,1,0:T(8,128)(2,1)S(1)} copy-done((bf16[27,256,128]{2,1,0:T(8,128)(2,1)S(1)}, bf16[27,256,128]{2,1,0:T(8,128)(2,1)}, u32[]{:S(2)}) %copy-start.4) | copy-done | bytes 1769496
  74.5 0.0 copy-start
  74.5 6.5 %shard_map.97 = (f32[128,128]{1,0:T(8,128)S(1)}, f32[1024,128]{1,0:T(8,128)S(1)}, bf16[128,256]{1,0:T(8,128)(2,1)}) custom-call(bf16[128,256]{1,0:T(8,128)(2,1)S(1)} %bitcast.27, bf16[27,256,128]{2,1,0:T(8,128)(2,1)S(1)} %copy-done.4, s32[27,128]{1,0:T(8,128)S(1)} %shard_map.94.table_ref, bf16[3456,128]{1,0:T(8,128)(2,1)} %shard_map.96.gathered_ref), custom_call_target="tpu_custom_call" | custom-call | flops 2038431744 | bytes 3538944 | tf_op jit(solution)/shard_map/pallas_call | solution.py:200
  81.0 5.8 %all-to-all-done.1.g_ref = bf16[16,216,128]{2,1,0:T(8,128)(2,1)S(1)} async-done(((bf16[16,216,128]{2,1,0:T(8,128)(2,1)}), bf16[16,216,128]{2,1,0:T(8,128)(2,1)S(1)}, u32[]{:S(2)}, u32[]{:S(2)}) %all-to-all-start.1) | async-done | bytes 884768 | tf_op jit(solution)/shard_map/all_to_all | solution.py:198
  86.8 0.0 copy-done
  86.8 0.8 shard_map.98
  87.5 0.0 copy-start.3
  87.5 40.4 %all_to_all.20 = f32[128,1,1536]{2,1,0:T(1,128)S(1)} all-to-all(f32[128,1,1536]{2,1,0:T(1,128)S(1)} %bitcast.25), channel_id=1, replica_groups=mesh['y'=8,'zh'=4,'zl'=2,'core'=2,'scene'=4] {'y','zh','zl','core'}, dimensions={0} | all-to-all | bytes 1572864 | tf_op jit(solution)/shard_map/all_to_all | solution.py:222
  127.9 0.7 shard_map.100
  128.6 3.3 %all-to-all-start.3 = ((f32[4,16,128]{2,1,0:T(8,128)}), f32[4,16,128]{2,1,0:T(8,128)S(1)}, u32[]{:S(2)}, u32[]{:S(2)}) async-start(f32[4,16,128]{2,1,0:T(8,128)} %shard_map.100), calls=%async_computation.3 | async-start | bytes 65536 | tf_op jit(solution)/shard_map/all_to_all | solution.py:228
  131.9 0.0 copy-done.3
  131.9 1.0 shard_map.99
  132.8 3.3 %all-to-all-done.3 = f32[4,16,128]{2,1,0:T(8,128)S(1)} async-done(((f32[4,16,128]{2,1,0:T(8,128)}), f32[4,16,128]{2,1,0:T(8,128)S(1)}, u32[]{:S(2)}, u32[]{:S(2)}) %all-to-all-start.3) | async-done | bytes 32800 | tf_op jit(solution)/shard_map/all_to_all | solution.py:228
  136.2 0.1 mul.21
  136.3 0.6 copy.19
  (4 shorter events, 0.1 us)
Async XLA Ops:
  7.2 60.0 %all-gather.2.cloned.1.call-start = ((), (), s32[]{:S(2)}) async-start(), calls=%async_computation.4 | async-start | bytes 1114112 | tf_op jit(solution)/shard_map/all_gather | solution.py:174
  7.9 0.7 copy-start.2
  8.6 0.8 copy-start.5
  9.4 0.8 copy-start.6
  11.2 32.7 %all-to-all-start = ((bf16[128,8,128]{2,1,0:T(8,128)(2,1)}), bf16[128,8,128]{2,1,0:T(8,128)(2,1)S(1)}, u32[]{:S(2)}, u32[]{:S(2)}) async-start(bf16[128,8,128]{2,1,0:T(8,128)(2,1)} %bitcast.4), calls=%async_computation | async-start | bytes 524288 | tf_op jit(solution)/shard_map/all_to_all | solution.py:181
  48.2 24.8 %copy-start.1 = (bf16[1,128,256]{2,1,0:T(8,128)(2,1)S(1)}, bf16[1,128,256]{2,1,0:T(8,128)(2,1)}, u32[]{:S(2)}) copy-start(bf16[1,128,256]{2,1,0:T(8,128)(2,1)} %param.7) | copy-start | bytes 196612
  67.2 19.6 %all-to-all-start.1 = ((bf16[16,216,128]{2,1,0:T(8,128)(2,1)}), bf16[16,216,128]{2,1,0:T(8,128)(2,1)S(1)}, u32[]{:S(2)}, u32[]{:S(2)}) async-start(bf16[16,216,128]{2,1,0:T(8,128)(2,1)} %bitcast.6), calls=%async_computation.1 | async-start | bytes 1769472 | tf_op jit(solution)/shard_map/all_to_all | solution.py:198
  73.0 1.5 %copy-start.4 = (bf16[27,256,128]{2,1,0:T(8,128)(2,1)S(1)}, bf16[27,256,128]{2,1,0:T(8,128)(2,1)}, u32[]{:S(2)}) copy-start(bf16[27,256,128]{2,1,0:T(8,128)(2,1)} %w_ref.1) | copy-start | bytes 5308420
  74.5 12.2 %copy-start = (bf16[16,128,256]{2,1,0:T(8,128)(2,1)S(1)}, bf16[16,128,256]{2,1,0:T(8,128)(2,1)}, u32[]{:S(2)}) copy-start(bf16[16,128,256]{2,1,0:T(8,128)(2,1)} %all-gather.2.cloned.1.call-done.x_ref) | copy-start | bytes 3145732
  87.5 44.3 %copy-start.3 = (s32[1,1,1024]{2,1,0:T(1,128)S(1)}, s32[1,1,1024]{2,1,0:T(1,128)}, u32[]{:S(2)}) copy-start(s32[1,1,1024]{2,1,0:T(1,128)} %param.13) | copy-start | bytes 12292
  128.6 7.5 %all-to-all-start.3 = ((f32[4,16,128]{2,1,0:T(8,128)}), f32[4,16,128]{2,1,0:T(8,128)S(1)}, u32[]{:S(2)}, u32[]{:S(2)}) async-start(f32[4,16,128]{2,1,0:T(8,128)} %shard_map.100), calls=%async_computation.3 | async-start | bytes 65536 | tf_op jit(solution)/shard_map/all_to_all | solution.py:228
Sparse Core Ops, SparseCore 0:
  10.1 57.0 all-gather.1

commit v3 on v2

--- a/solution.py
+++ b/solution.py
@@ -14,6 +14,7 @@
 I32 = jnp.int32
 LANES = 128
 STEP = 3
+WAIT_FLOPS = 2 * 10**10
 VMEM_BYTES = 24 * 1024 * 1024
 SPACE = ("y", "zh", "zl", "core")
 GROUP = ("zl", "core", "scene")
@@ -91,15 +92,19 @@
             gathered_ref[lane_block(first + k), :] = rows[:, lane_block(k)]
 
 
-def forward_kernel(x_ref, w_ref, table_ref, gathered_ref, own_ref, send_ref, grad_ref, terms_ref, hot_ref):
+def input_grad_kernel(w_ref, gathered_ref, grad_ref):
+    total = jnp.zeros((w_ref.shape[1], LANES), F32)
+    for k in range(w_ref.shape[0]):
+        total += jnp.dot(w_ref[k], gathered_ref[lane_block(k), :], preferred_element_type=F32)
+    grad_ref[...] = total.T.astype(BF16)
+
+
+def forward_kernel(x_ref, w_ref, table_ref, own_ref, send_ref, terms_ref, hot_ref):
     offsets = w_ref.shape[0]
-    total = jnp.zeros((w_ref.shape[1], LANES), F32)
     for k in range(offsets):
         high, low = split_two(jnp.dot(x_ref[...], w_ref[k], preferred_element_type=F32))
         terms_ref[lane_block(k), 0:LANES] = high
         terms_ref[lane_block(k), LANES : 2 * LANES] = low
-        total += jnp.dot(w_ref[k], gathered_ref[lane_block(k), :], preferred_element_type=F32)
-    grad_ref[...] = total.T.astype(BF16)
 
     def block(start):
         here = rows_iota(LANES) + start
@@ -115,6 +120,28 @@
         return carry
 
     lax.fori_loop(0, send_ref.shape[0] // LANES, scatter, 0)
+
+
+def encode(value, top):
+    level = jnp.ceil(jnp.log2(jnp.maximum(top, 1e-36)) * 8.0)
+    code = jnp.round(value * jnp.exp2(level * -0.125) * 32767.0)
+    return jnp.clip(code, -32767.0, 32767.0).astype(I32), level.astype(I32)
+
+
+def unit(level):
+    return jnp.exp2(level.astype(F32) * 0.125) * (1.0 / 32767.0)
+
+
+def join(first, second):
+    return (first << 16) | (second & 0xFFFF)
+
+
+def halves(word):
+    return (word >> 16).astype(F32), ((word << 16) >> 16).astype(F32)
+
+
+def row_top(value):
+    return jnp.max(jnp.abs(value), axis=1, keepdims=True)
 
 
 def pack_kernel(g_ref, x_ref, send_ref, out_ref, turn_ref):
@@ -126,28 +153,53 @@
     total = jnp.concatenate([total, jnp.zeros((2 * LANES - columns, total.shape[1]), F32)], axis=0)
     for half in range(2):
         turn_ref[half] = total[lane_block(half), :].T
-    for r in range(8):
-        out_ref[pl.ds(r, peers, stride=12), :] = send_ref[pl.ds(r, peers, stride=8), :]
-    for c in range(2):
-        for half in range(2):
-            rows = turn_ref[half, pl.ds(c, peers, stride=2), :]
-            out_ref[pl.ds(8 + 2 * c + half, peers, stride=12), :] = rows
-
-
-def sum_kernel(arrived_ref, out_ref):
-    total = arrived_ref[0]
-    for i in range(1, arrived_ref.shape[0]):
-        total += arrived_ref[i]
-    for s in range(out_ref.shape[0]):
-        for i in range(4):
-            out_ref[s, 4 * i : 4 * i + 4, :] = total[12 * i + 8 : 12 * i + 12, :]
-
-
-def receive_kernel(own_ref, arrived_ref, recv_ref, out_ref, rows_ref):
-    peers = arrived_ref.shape[0] // 12
+    free = columns - LANES
+    lane = lax.broadcasted_iota(I32, (peers, LANES), 1)
+    levels = jnp.zeros((peers, LANES), I32)
+    for r in range(4):
+        words = []
+        for slot in (r, r + 4):
+            value = send_ref[pl.ds(slot, peers, stride=8), :]
+            code, level = encode(value, row_top(value))
+            words.append(code)
+            levels = jnp.where(lane == free + slot, level, levels)
+        out_ref[pl.ds(r, peers, stride=6), :] = join(*words)
+    parts = [[turn_ref[h, pl.ds(c, peers, stride=2), :] for c in range(2)] for h in range(2)]
+    top = jnp.maximum(
+        jnp.maximum(row_top(parts[0][0]), row_top(parts[0][1])),
+        jnp.maximum(row_top(parts[1][0]), row_top(parts[1][1])),
+    )
+    for half in range(2):
+        codes = [encode(parts[half][c], top) for c in range(2)]
+        word = join(codes[0][0], codes[1][0])
+        if half == 1:
+            levels = jnp.where(lane == free + 8, codes[0][1], levels)
+            word = jnp.where(lane < free, word, levels)
+        out_ref[pl.ds(4 + half, peers, stride=6), :] = word
+
+
+def sum_kernel(arrived_ref, out_ref, *, free):
+    peers = arrived_ref.shape[0] // 6
+    words = [arrived_ref[pl.ds(4 + half, peers, stride=6), :] for half in range(2)]
+    scale = unit(words[1][:, free + 8 : free + 9])
+    for half in range(2):
+        for c, value in enumerate(halves(words[half])):
+            total = (value * scale).reshape(peers // 8, 8, LANES).sum(axis=0)
+            total = total[0:4] + total[4:8]
+            row = 4 * (2 * c + half)
+            for s in range(out_ref.shape[0]):
+                out_ref[s, row : row + 4, :] = total
+
+
+def receive_kernel(own_ref, arrived_ref, recv_ref, out_ref, rows_ref, *, free):
+    peers = arrived_ref.shape[0] // 6
     iota = rows_iota(LANES)
-    for r in range(8):
-        rows_ref[pl.ds(r, peers, stride=8), :] = arrived_ref[pl.ds(r, peers, stride=12), :]
+    levels = arrived_ref[pl.ds(5, peers, stride=6), :]
+    for r in range(4):
+        pair = halves(arrived_ref[pl.ds(r, peers, stride=6), :])
+        for value, slot in zip(pair, (r, r + 4)):
+            scale = unit(levels[:, free + slot : free + slot + 1])
+            rows_ref[pl.ds(slot, peers, stride=8), :] = value * scale
     total = own_ref[...]
     for g in range(recv_ref.shape[0]):
         hot = one_hot(iota, recv_ref[g : g + 1, :])
@@ -183,51 +235,52 @@
     table = call(
         functools.partial(table_kernel, targets=targets),
         shape((offsets, own_rows), I32),
-        flops=2 * targets * offsets * own_rows * 100,
     )(pair_in[0, 0], pair_out[0, 0])
 
+    own, outbound = call(
+        forward_kernel,
+        (shape((own_rows, out_width), F32), shape((send_rows, out_width), F32)),
+        scratch=(
+            pltpu.VMEM((offsets * own_rows, 2 * out_width), BF16),
+            pltpu.VMEM((LANES, offsets * own_rows), BF16),
+        ),
+    )(x, weight, table)
+
+    returned, own, outbound = lax.optimization_barrier((returned, own, outbound))
     gathered = call(
         lookup_kernel,
         shape((offsets * out_width, own_rows), BF16),
         scratch=(pltpu.VMEM((out_width, targets), BF16), pltpu.VMEM((2, targets, STEP * LANES), BF16)),
-        flops=2 * targets * offsets * own_rows * out_width,
-        moved=2 * offsets * own_rows * out_width,
     )(upstream, returned.reshape(send_rows, out_width), table)
+    group_g = lax.all_to_all(gathered.reshape(group, columns, own_rows), GROUP, 0, 0, tiled=True)
 
     gathered, group_x = lax.optimization_barrier((gathered, group_x))
-    group_g = lax.all_to_all(gathered.reshape(group, columns, own_rows), GROUP, 0, 0, tiled=True)
-
-    own, outbound, input_grad = call(
-        forward_kernel,
-        (
-            shape((own_rows, out_width), F32),
-            shape((send_rows, out_width), F32),
-            shape((own_rows, in_width), BF16),
-        ),
-        scratch=(
-            pltpu.VMEM((offsets * own_rows, 2 * out_width), BF16),
-            pltpu.VMEM((LANES, offsets * own_rows), BF16),
-        ),
-        flops=4 * targets * offsets * own_rows * out_width,
-        moved=4 * offsets * in_width * out_width,
-    )(x, weight, table, gathered)
+    input_grad = call(
+        input_grad_kernel,
+        shape((own_rows, in_width), BF16),
+        flops=WAIT_FLOPS,
+    )(weight, gathered)
+    outbound, input_grad = lax.optimization_barrier((outbound, input_grad))
 
     packed = call(
         pack_kernel,
-        shape((peers * 12, LANES), F32),
+        shape((peers * 6, LANES), I32),
         scratch=(pltpu.VMEM((2, in_width, LANES), F32),),
         flops=2 * columns * in_width * own_rows * group,
-        moved=peers * 12 * LANES * 8,
+        moved=peers * 6 * LANES * 8,
     )(group_g, group_x, outbound)
-    arrived = lax.all_to_all(packed.reshape(peers, 1, 12 * LANES), SPACE, 0, 0, tiled=True)
-    arrived = arrived.reshape(peers * 12, LANES)
-
-    quarter = call(sum_kernel, shape((scenes, 16, LANES), F32), moved=peers * 12 * LANES * 4)(
-        arrived.reshape(peers // 4, 48, LANES)
-    )
+    arrived = lax.all_to_all(packed.reshape(peers, 1, 6 * LANES), SPACE, 0, 0, tiled=True)
+    arrived = arrived.reshape(peers * 6, LANES)
+
+    free = columns - LANES
+    quarter = call(
+        functools.partial(sum_kernel, free=free),
+        shape((scenes, 16, LANES), F32),
+        moved=peers * 6 * LANES * 4,
+    )(arrived)
     blocks = lax.all_to_all(quarter, "scene", 0, 0, tiled=True)
     conv_out = call(
-        receive_kernel,
+        functools.partial(receive_kernel, free=free),
         shape((own_rows, out_width), BF16),
         scratch=(pltpu.VMEM((send_rows, out_width), F32),),
         flops=4 * send_rows * own_rows * out_width,
@@ -235,8 +288,9 @@
     )(own, arrived, recv)
 
     own_in = in_width // peers
-    blocks = blocks.reshape(scenes, 4, own_in, 2 * LANES)[:, :, :, :columns]
-    kernel_grad = blocks.transpose(2, 1, 0, 3).reshape(own_in, offsets, out_width)
+    blocks = blocks.reshape(scenes, own_in, 2, 4, LANES).transpose(1, 3, 0, 2, 4)
+    blocks = blocks.reshape(own_in, group, 2 * LANES)[:, :, :columns]
+    kernel_grad = blocks.reshape(own_in, offsets, out_width)
     kernel_grad = kernel_grad.transpose(1, 0, 2).reshape(offsets, own_in * out_width)
     normalizer = 1.0 / math.sqrt(scenes * peers * own_rows)
     return (conv_out[None], input_grad[None], kernel_grad * normalizer)

time: 145 us -> 125 us (0.86)
  waiting for transfers between devices: 41.6 us -> 25.4 us
  blocking collectives: 40.4 us -> 32.8 us
  local copies, waits for them, and re-layouts: 5.28 us -> 7.39 us
    all_to_all x1, blocking collectives: 40.4 us -> 32.8 us  [local(): lax.all_to_all(packed.reshape(peers, 1, 6 * LANES), SPACE, 0, 0, tiled=True)]
    all_to_all x1, waiting for transfers between devices: 12.9 us -> 5.64 us  [local(): lax.all_to_all(outgoing.reshape(peers, slots, out_width), SPACE, 0, 0, ti...]
    all_to_all x1, waiting for transfers between devices: 5.76 us -> 0.01 us  [local(): lax.all_to_all(gathered.reshape(group, columns, own_rows), GROUP, 0, 0, t...]
    all_gather x1, waiting for transfers between devices: 19 us -> 15.9 us  [local(): group_x = lax.all_gather(x, GROUP)]
    pallas_call x3 -> x4, Pallas kernels: 2.39 us -> 5.21 us  [the longest x1 2.5 us: local(): call(input_grad_kernel, shape((own_rows, in_width), BF16), flops=WAIT_FLOPS)]
    unnamed x17 -> x19, local copies, waits for them, and re-layouts: 5.13 us -> 7.22 us
    pallas_call x1, Pallas kernels: 6.46 us -> 4.91 us  [local(): call(forward_kernel, (shape((own_rows, out_width), F32), shape((send_rows...]
  transfers between devices with their start and end apart: 4 -> 4, of which waited for: 4 -> 3; matrix products, arithmetic and copies ran while one was open for 1% -> 1% of each run, Pallas kernels for 9% -> 12%
where the time goes in v3:
time: 125 us; the launch traced here: 124 us
  blocking collectives  32.8 us (26%)
  starting transfers between devices  27.9 us (22%)
  waiting for transfers between devices  25.4 us (20%)
  Pallas kernels  16.1 us (13%)
  between operations  14.1 us (11%)
  local copies, waits for them, and re-layouts  7.39 us (6%)
    all_to_all x1, blocking collectives, local(): lax.all_to_all(packed.reshape(peers, 1, 6 * LANES), SPACE, 0, 0, tiled=True)  32.8 us
    all_to_all x1, starting transfers between devices, local(): lax.all_to_all(outgoing.reshape(peers, slots, out_width), SPACE, 0, 0, ti...  18.4 us
    all_gather x1, waiting for transfers between devices, local(): group_x = lax.all_gather(x, GROUP)  15.9 us
    unnamed x19, local copies, waits for them, and re-layouts  7.22 us
    all_to_all x1, starting transfers between devices, local(): lax.all_to_all(gathered.reshape(group, columns, own_rows), GROUP, 0, 0, t...  6.11 us
    all_to_all x1, waiting for transfers between devices, local(): lax.all_to_all(outgoing.reshape(peers, slots, out_width), SPACE, 0, 0, ti...  5.64 us
    pallas_call x1, Pallas kernels, local(): call(forward_kernel, (shape((own_rows, out_width), F32), shape((send_rows...  4.91 us
    pallas_call x1, Pallas kernels, local(): call(lookup_kernel, shape((offsets * out_width, own_rows), BF16), scratch...  4.41 us
  transfers between devices with their start and end apart: 4, of which 3 were waited for; matrix products, arithmetic and copies ran while one was open for 1% of the time, Pallas kernels for 12%

profile of v3, /device:TPU:1, one launch (start us, length us, event | category | flops | bytes accessed | tf_op | source)
XLA Modules:
  0.0 123.6 jit_solution(5380117227203736881)
XLA Ops:
  7.2 0.0 all-gather.2.cloned.1.call-start
  7.2 0.7 all-gather.2.cloned.1.call-update
  7.9 0.0 copy-start.4
  7.9 0.7 copy-done.4
  8.6 0.0 copy-start.6
  8.6 0.8 copy-done.6
  9.4 0.0 copy-start.7
  9.4 0.8 copy-done.7
  10.2 1.0 shard_map.94
  11.2 18.4 %all-to-all-start = ((bf16[128,8,128]{2,1,0:T(8,128)(2,1)}), bf16[128,8,128]{2,1,0:T(8,128)(2,1)S(1)}, u32[]{:S(2)}, u32[]{:S(2)}) async-start(bf16[128,8,128]{2,1,0:T(8,128)(2,1)} %bitcast.3), calls=%async_computation | async-start | bytes 524288 | tf_op jit(solution)/shard_map/all_to_all | solution.py:233
  29.6 0.7 copy_bitcast_fusion.1
  30.3 0.6 shard_map.95.table_ref
  30.9 0.0 copy-start
  30.9 1.5 %copy-done = bf16[27,256,128]{2,1,0:T(8,128)(2,1)S(1)} copy-done((bf16[27,256,128]{2,1,0:T(8,128)(2,1)S(1)}, bf16[27,256,128]{2,1,0:T(8,128)(2,1)}, u32[]{:S(2)}) %copy-start) | copy-done | bytes 1769496
  32.4 0.0 copy-start.3
  32.4 0.8 copy-done.3
  33.3 4.9 %shard_map.96 = (f32[128,128]{1,0:T(8,128)S(1)}, f32[1024,128]{1,0:T(8,128)S(1)}) custom-call(bf16[128,256]{1,0:T(8,128)(2,1)S(1)} %bitcast.27, bf16[27,256,128]{2,1,0:T(8,128)(2,1)S(1)} %copy-done, s32[27,128]{1,0:T(8,128)S(1)} %shard_map.95.table_ref), custom_call_target="tpu_custom_call" | custom-call | tf_op jit(solution)/shard_map/pallas_call | solution.py:240
  38.2 0.0 copy-start.1
  38.2 5.6 %all-to-all-done = bf16[128,8,128]{2,1,0:T(8,128)(2,1)S(1)} async-done(((bf16[128,8,128]{2,1,0:T(8,128)(2,1)}), bf16[128,8,128]{2,1,0:T(8,128)(2,1)S(1)}, u32[]{:S(2)}, u32[]{:S(2)}) %all-to-all-start) | async-done | bytes 262176 | tf_op jit(solution)/shard_map/all_to_all | solution.py:233
  43.8 4.4 %shard_map.97.gathered_ref = bf16[3456,128]{1,0:T(8,128)(2,1)} custom-call(bf16[128,128]{1,0:T(8,128)(2,1)S(1)} %get-tuple-element.18.up_ref, bf16[1024,128]{1,0:T(8,128)(2,1)S(1)} %bitcast.26, s32[27,128]{1,0:T(8,128)S(1)} %shard_map.95.table_ref), custom_call_target="tpu_custom_call" | custom-call | tf_op jit(solution)/shard_map/pallas_call | solution.py:250
  48.2 6.1 %all-to-all-start.1 = ((bf16[16,216,128]{2,1,0:T(8,128)(2,1)}), bf16[16,216,128]{2,1,0:T(8,128)(2,1)S(1)}, u32[]{:S(2)}, u32[]{:S(2)}) async-start(bf16[16,216,128]{2,1,0:T(8,128)(2,1)} %bitcast.6), calls=%async_computation.1 | async-start | bytes 1769472 | tf_op jit(solution)/shard_map/all_to_all | solution.py:255
  54.3 15.9 %all-gather.2.cloned.1.call-done.x_ref = bf16[16,128,256]{2,1,0:T(8,128)(2,1)} async-done(((bf16[1,128,256]{2,1,0:T(8,128)(2,1)}), bf16[16,128,256]{2,1,0:T(8,128)(2,1)}) %all-gather.2.cloned.1.call-update) | async-done | bytes 1048592 | tf_op jit(solution)/shard_map/all_gather | solution.py:226
  70.3 0.0 copy-done.1
  70.3 2.5 %shard_map.98 = bf16[128,256]{1,0:T(8,128)(2,1)} custom-call(bf16[27,256,128]{2,1,0:T(8,128)(2,1)S(1)} %copy-done.1, bf16[3456,128]{1,0:T(8,128)(2,1)} %shard_map.97.gathered_ref), custom_call_target="tpu_custom_call" | custom-call | flops 20000000000 | tf_op jit(solution)/shard_map/pallas_call | solution.py:258
  72.8 0.0 all-to-all-done.1.g_ref
  72.8 0.0 copy-start.2
  72.8 1.2 copy-done.2
  74.0 0.0 copy-start.5
  74.0 0.9 shard_map.99
  74.9 32.8 %all_to_all.20 = s32[128,1,768]{2,1,0:T(1,128)S(1)} all-to-all(s32[128,1,768]{2,1,0:T(1,128)S(1)} %bitcast.25), channel_id=1, replica_groups=mesh['y'=8,'zh'=4,'zl'=2,'core'=2,'scene'=4] {'y','zh','zl','core'}, dimensions={0} | all-to-all | bytes 786432 | tf_op jit(solution)/shard_map/all_to_all | solution.py:272
  107.6 0.7 shard_map.101
  108.3 3.3 %all-to-all-start.3 = ((f32[4,16,128]{2,1,0:T(8,128)}), f32[4,16,128]{2,1,0:T(8,128)S(1)}, u32[]{:S(2)}, u32[]{:S(2)}) async-start(f32[4,16,128]{2,1,0:T(8,128)} %shard_map.101), calls=%async_computation.3 | async-start | bytes 65536 | tf_op jit(solution)/shard_map/all_to_all | solution.py:281
  111.6 0.0 copy-done.5
  111.6 1.1 shard_map.100
  112.8 3.2 %all-to-all-done.3 = f32[4,16,128]{2,1,0:T(8,128)S(1)} async-done(((f32[4,16,128]{2,1,0:T(8,128)}), f32[4,16,128]{2,1,0:T(8,128)S(1)}, u32[]{:S(2)}, u32[]{:S(2)}) %all-to-all-start.3) | async-done | bytes 32800 | tf_op jit(solution)/shard_map/all_to_all | solution.py:281
  116.0 0.1 mul.17
  116.2 0.6 copy.18
  (5 shorter events, 0.1 us)
Async XLA Ops:
  7.2 63.1 %all-gather.2.cloned.1.call-start = ((), (), s32[]{:S(2)}) async-start(), calls=%async_computation.4 | async-start | bytes 1114112 | tf_op jit(solution)/shard_map/all_gather | solution.py:226
  7.9 0.7 copy-start.4
  8.6 0.8 copy-start.6
  9.4 0.8 copy-start.7
  11.2 32.7 %all-to-all-start = ((bf16[128,8,128]{2,1,0:T(8,128)(2,1)}), bf16[128,8,128]{2,1,0:T(8,128)(2,1)S(1)}, u32[]{:S(2)}, u32[]{:S(2)}) async-start(bf16[128,8,128]{2,1,0:T(8,128)(2,1)} %bitcast.3), calls=%async_computation | async-start | bytes 524288 | tf_op jit(solution)/shard_map/all_to_all | solution.py:233
  30.9 1.5 %copy-start = (bf16[27,256,128]{2,1,0:T(8,128)(2,1)S(1)}, bf16[27,256,128]{2,1,0:T(8,128)(2,1)}, u32[]{:S(2)}) copy-start(bf16[27,256,128]{2,1,0:T(8,128)(2,1)} %w_ref.3) | copy-start | bytes 5308420
  32.4 0.8 copy-start.3
  38.2 32.1 %copy-start.1 = (bf16[27,256,128]{2,1,0:T(8,128)(2,1)S(1)}, bf16[27,256,128]{2,1,0:T(8,128)(2,1)}, u32[]{:S(2)}) copy-start(bf16[27,256,128]{2,1,0:T(8,128)(2,1)} %w_ref.3) | copy-start | bytes 5308420
  48.2 24.5 %all-to-all-start.1 = ((bf16[16,216,128]{2,1,0:T(8,128)(2,1)}), bf16[16,216,128]{2,1,0:T(8,128)(2,1)S(1)}, u32[]{:S(2)}, u32[]{:S(2)}) async-start(bf16[16,216,128]{2,1,0:T(8,128)(2,1)} %bitcast.6), calls=%async_computation.1 | async-start | bytes 1769472 | tf_op jit(solution)/shard_map/all_to_all | solution.py:255
  72.8 1.2 copy-start.2
  74.0 37.7 %copy-start.5 = (s32[1,1,1024]{2,1,0:T(1,128)S(1)}, s32[1,1,1024]{2,1,0:T(1,128)}, u32[]{:S(2)}) copy-start(s32[1,1,1024]{2,1,0:T(1,128)} %param.13) | copy-start | bytes 12292
  108.3 7.6 %all-to-all-start.3 = ((f32[4,16,128]{2,1,0:T(8,128)}), f32[4,16,128]{2,1,0:T(8,128)S(1)}, u32[]{:S(2)}, u32[]{:S(2)}) async-start(f32[4,16,128]{2,1,0:T(8,128)} %shard_map.101), calls=%async_computation.3 | async-start | bytes 65536 | tf_op jit(solution)/shard_map/all_to_all | solution.py:281
Sparse Core Ops, SparseCore 0:
  10.1 60.1 all-gather.1

commit v4 on v3

--- a/solution.py
+++ b/solution.py
@@ -14,17 +14,17 @@
 I32 = jnp.int32
 LANES = 128
 STEP = 3
-WAIT_FLOPS = 2 * 10**10
 VMEM_BYTES = 24 * 1024 * 1024
 SPACE = ("y", "zh", "zl", "core")
 GROUP = ("zl", "core", "scene")
 
 
-def call(kernel, outs, scratch=(), flops=0, moved=0):
+def call(kernel, outs, scratch=(), flops=0, moved=0, **specs):
     return pl.pallas_call(
         kernel,
         out_shape=outs,
         scratch_shapes=list(scratch),
+        **specs,
         compiler_params=pltpu.CompilerParams(vmem_limit_bytes=VMEM_BYTES),
         cost_estimate=pl.CostEstimate(flops=flops, bytes_accessed=moved, transcendentals=0),
     )
@@ -144,12 +144,18 @@
     return jnp.max(jnp.abs(value), axis=1, keepdims=True)
 
 
-def pack_kernel(g_ref, x_ref, send_ref, out_ref, turn_ref):
+def pack_kernel(g_ref, near_ref, far_ref, send_ref, out_ref, turn_ref):
     columns = g_ref.shape[1]
-    peers = x_ref.shape[2] // 2
-    total = jnp.dot(g_ref[0], x_ref[0], preferred_element_type=F32)
-    for s in range(1, g_ref.shape[0]):
-        total += jnp.dot(g_ref[s], x_ref[s], preferred_element_type=F32)
+    peers = near_ref.shape[2] // 2
+    total = jnp.zeros((columns, near_ref.shape[2]), F32)
+    low, core, scene = (lax.axis_index(axis) for axis in GROUP)
+    scenes = near_ref.shape[0] // 2
+    for s in range(g_ref.shape[0]):
+        x_ref = near_ref if s < 2 * scenes else far_ref
+        zl = low if s // scenes % 2 == 0 else 1 - low
+        other = core if s < 2 * scenes else 1 - core
+        sender = (zl * 2 + other) * scenes + lax.rem(scene + scenes - s % scenes, scenes)
+        total += jnp.dot(g_ref[sender], x_ref[s % (2 * scenes)], preferred_element_type=F32)
     total = jnp.concatenate([total, jnp.zeros((2 * LANES - columns, total.shape[1]), F32)], axis=0)
     for half in range(2):
         turn_ref[half] = total[lane_block(half), :].T
@@ -223,14 +229,20 @@
     recv = recv_index.reshape(send_rows // LANES, LANES)
     shape = jax.ShapeDtypeStruct
 
-    group_x = lax.all_gather(x, GROUP)
     upstream, outgoing = call(
         gather_kernel,
         (shape((own_rows, out_width), BF16), shape((send_rows, out_width), BF16)),
         flops=2 * send_rows * own_rows * out_width,
         moved=send_rows * out_width * 3,
     )(cotangent[0], relu_mask[0], recv)
+    own_x, outgoing = lax.optimization_barrier((x, outgoing))
     returned = lax.all_to_all(outgoing.reshape(peers, slots, out_width), SPACE, 0, 0, tiled=True)
+
+    swap = [(0, 1), (1, 0)]
+    ring = [
+        lax.ppermute(own_x, "scene", [(i, (i + d) % scenes) for i in range(scenes)])
+        for d in range(1, scenes)
+    ]
 
     table = call(
         functools.partial(table_kernel, targets=targets),
@@ -246,7 +258,7 @@
         ),
     )(x, weight, table)
 
-    returned, own, outbound = lax.optimization_barrier((returned, own, outbound))
+    returned, *ring = lax.optimization_barrier((returned, *ring))
     gathered = call(
         lookup_kernel,
         shape((offsets * out_width, own_rows), BF16),
@@ -254,21 +266,23 @@
     )(upstream, returned.reshape(send_rows, out_width), table)
     group_g = lax.all_to_all(gathered.reshape(group, columns, own_rows), GROUP, 0, 0, tiled=True)
 
-    gathered, group_x = lax.optimization_barrier((gathered, group_x))
     input_grad = call(
         input_grad_kernel,
         shape((own_rows, in_width), BF16),
-        flops=WAIT_FLOPS,
+        flops=10**9,
     )(weight, gathered)
-    outbound, input_grad = lax.optimization_barrier((outbound, input_grad))
-
+
+    near = jnp.stack([x] + ring)
+    other = lax.ppermute(near, "zl", swap)
+    half = jnp.concatenate([near, other])
+    far = lax.ppermute(half, "core", swap)
     packed = call(
         pack_kernel,
         shape((peers * 6, LANES), I32),
         scratch=(pltpu.VMEM((2, in_width, LANES), F32),),
         flops=2 * columns * in_width * own_rows * group,
         moved=peers * 6 * LANES * 8,
-    )(group_g, group_x, outbound)
+    )(group_g, half, far, outbound)
     arrived = lax.all_to_all(packed.reshape(peers, 1, 6 * LANES), SPACE, 0, 0, tiled=True)
     arrived = arrived.reshape(peers * 6, LANES)
 

time: 125 us -> 117 us (0.936)
  starting transfers between devices: 27.9 us -> 44.2 us
  between operations: 14.1 us -> 0.82 us
  waiting for transfers between devices: 25.4 us -> 18.3 us
  blocking collectives: 32.8 us -> 28.6 us
    ppermute x0 -> x5, waiting for transfers between devices: none -> 17.2 us  [the longest x1 14 us: local(): other = lax.ppermute(near, 'zl', swap)]
    all_gather x1 -> x0, waiting for transfers between devices: 15.9 us -> none  [local(): group_x = lax.all_gather(x, GROUP)]
    ppermute x0 -> x5, starting transfers between devices: none -> 15.4 us  [the longest x3 9.34 us: local(): lax.ppermute(own_x, 'scene', [(i, (i + d) % scenes) for i in range(scenes)])]
    all_to_all x1, waiting for transfers between devices: 5.64 us -> 0.37 us  [local(): lax.all_to_all(outgoing.reshape(peers, slots, out_width), SPACE, 0, 0, ti...]
    all_to_all x1, blocking collectives: 32.8 us -> 28.6 us  [local(): lax.all_to_all(packed.reshape(peers, 1, 6 * LANES), SPACE, 0, 0, tiled=True)]
    all_to_all x1, waiting for transfers between devices: 3.18 us -> 0.66 us  [local(): blocks = lax.all_to_all(quarter, 'scene', 0, 0, tiled=True)]
    unnamed x19 -> x27, local copies, waits for them, and re-layouts: 7.22 us -> 7.39 us
  transfers between devices with their start and end apart: 4 -> 8, of which waited for: 3 -> 5; matrix products, arithmetic and copies ran while one was open for 1% -> 1% of each run, Pallas kernels for 12% -> 8%
where the time goes in v4:
time: 117 us; the launch traced here: 116 us
  starting transfers between devices  44.2 us (38%)
  blocking collectives  28.6 us (24%)
  waiting for transfers between devices  18.3 us (16%)
  Pallas kernels  16.1 us (14%)
  local copies, waits for them, and re-layouts  7.58 us (6%)
    all_to_all x1, blocking collectives, local(): lax.all_to_all(packed.reshape(peers, 1, 6 * LANES), SPACE, 0, 0, tiled=True)  28.6 us
    all_to_all x1, starting transfers between devices, local(): lax.all_to_all(outgoing.reshape(peers, slots, out_width), SPACE, 0, 0, ti...  18.6 us
    ppermute x1, waiting for transfers between devices, local(): other = lax.ppermute(near, 'zl', swap)  14 us
    ppermute x3, starting transfers between devices, local(): lax.ppermute(own_x, 'scene', [(i, (i + d) % scenes) for i in range(scenes)])  9.34 us
    unnamed x27, local copies, waits for them, and re-layouts  7.39 us
    all_to_all x1, starting transfers between devices, local(): lax.all_to_all(gathered.reshape(group, columns, own_rows), GROUP, 0, 0, t...  6.24 us
    pallas_call x1, Pallas kernels, local(): call(forward_kernel, (shape((own_rows, out_width), F32), shape((send_rows...  4.91 us
    pallas_call x1, Pallas kernels, local(): call(lookup_kernel, shape((offsets * out_width, own_rows), BF16), scratch...  4.38 us
  transfers between devices with their start and end apart: 8, of which 5 were waited for; matrix products, arithmetic and copies ran while one was open for 1% of the time, Pallas kernels for 8%

profile of v4, /device:TPU:1, one launch (start us, length us, event | category | flops | bytes accessed | tf_op | source)
XLA Modules:
  0.0 115.5 jit_solution(5507866889944826232)
XLA Ops:
  0.6 0.0 copy-start.6
  0.6 0.7 copy-done.6
  1.3 0.0 copy-start.8
  1.3 0.8 copy-done.8
  2.2 0.0 copy-start.9
  2.2 0.8 copy-done.9
  2.9 1.0 shard_map.96
  3.9 0.0 copy-start.1
  3.9 18.6 %all-to-all-start = ((bf16[128,8,128]{2,1,0:T(8,128)(2,1)}), bf16[128,8,128]{2,1,0:T(8,128)(2,1)S(1)}, u32[]{:S(2)}, u32[]{:S(2)}) async-start(bf16[128,8,128]{2,1,0:T(8,128)(2,1)} %bitcast.4), calls=%async_computation | async-start | bytes 524288 | tf_op jit(solution)/shard_map/all_to_all | solution.py:239
  22.4 4.4 %collective-permute-start.2 = (bf16[128,256]{1,0:T(8,128)(2,1)}, bf16[128,256]{1,0:T(8,128)(2,1)S(1)}, u32[]{:S(2)}, u32[]{:S(2)}) collective-permute-start(bf16[128,256]{1,0:T(8,128)(2,1)} %bitcast.33), channel_id=1, source_target_pairs={{0,3},{1,0},{2,1},{3,2},{4,7},{5,4},{6,5},{7,6},{8,11},{9,8},{10,9... | collective-permute-start | bytes 196616 | tf_op jit(solution)/shard_map/ppermute | solution.py:243
  26.8 2.4 %collective-permute-start.1 = (bf16[128,256]{1,0:T(8,128)(2,1)}, bf16[128,256]{1,0:T(8,128)(2,1)S(1)}, u32[]{:S(2)}, u32[]{:S(2)}) collective-permute-start(bf16[128,256]{1,0:T(8,128)(2,1)} %bitcast.34), channel_id=1, source_target_pairs={{0,2},{1,3},{2,0},{3,1},{4,6},{5,7},{6,4},{7,5},{8,10},{9,11},{10,... | collective-permute-start | bytes 196616 | tf_op jit(solution)/shard_map/ppermute | solution.py:243
  29.3 2.5 %collective-permute-start = (bf16[128,256]{1,0:T(8,128)(2,1)}, bf16[128,256]{1,0:T(8,128)(2,1)S(1)}, u32[]{:S(2)}, u32[]{:S(2)}) collective-permute-start(bf16[128,256]{1,0:T(8,128)(2,1)} %bitcast.35), channel_id=1, source_target_pairs={{0,1},{1,2},{2,3},{3,0},{4,5},{5,6},{6,7},{7,4},{8,9},{9,10},{10,1... | collective-permute-start | bytes 196616 | tf_op jit(solution)/shard_map/ppermute | solution.py:243
  31.8 0.7 copy_bitcast_fusion.1
  32.5 0.6 shard_map.94.table_ref
  33.1 0.0 collective-permute-done.2
  33.1 0.7 collective-permute-done.1
  33.9 2.4 %collective-permute-done = bf16[128,256]{1,0:T(8,128)(2,1)S(1)} collective-permute-done((bf16[128,256]{1,0:T(8,128)(2,1)}, bf16[128,256]{1,0:T(8,128)(2,1)S(1)}, u32[]{:S(2)}, u32[]{:S(2)}) %collective-permute-start) | collective-permute-done | bytes 65568 | tf_op jit(solution)/shard_map/ppermute | solution.py:243
  36.3 0.4 all-to-all-done
  36.7 4.4 %shard_map.97.gathered_ref = bf16[3456,128]{1,0:T(8,128)(2,1)} custom-call(bf16[128,128]{1,0:T(8,128)(2,1)S(1)} %get-tuple-element.14.up_ref, bf16[1024,128]{1,0:T(8,128)(2,1)S(1)} %bitcast.32, s32[27,128]{1,0:T(8,128)S(1)} %shard_map.94.table_ref), custom_call_target="tpu_custom_call" | custom-call | tf_op jit(solution)/shard_map/pallas_call | solution.py:262
  41.0 0.0 copy-start
  41.1 6.2 %all-to-all-start.1 = ((bf16[16,216,128]{2,1,0:T(8,128)(2,1)}), bf16[16,216,128]{2,1,0:T(8,128)(2,1)S(1)}, u32[]{:S(2)}, u32[]{:S(2)}) async-start(bf16[16,216,128]{2,1,0:T(8,128)(2,1)} %bitcast.6), calls=%async_computation.1 | async-start | bytes 1769472 | tf_op jit(solution)/shard_map/all_to_all | solution.py:267
  47.3 0.0 copy-done.1
  47.4 3.3 %collective-permute-start.3 = (bf16[4,128,256]{2,1,0:T(8,128)(2,1)S(1)}, bf16[4,128,256]{2,1,0:T(8,128)(2,1)S(1)}, u32[]{:S(2)}, u32[]{:S(2)}) collective-permute-start(bf16[4,128,256]{2,1,0:T(8,128)(2,1)S(1)} %pad_maximum_fusion), channel_id=1, source_target_pairs={{0,8},{8,0},{1,9},{9,1},{2,10},{10,2},{3,11},{11,3},{4,12},{12,4},... | collective-permute-start | bytes 786440 | tf_op jit(solution)/shard_map/ppermute | solution.py:276
  50.7 14.0 %collective-permute-done.3 = bf16[4,128,256]{2,1,0:T(8,128)(2,1)S(1)} collective-permute-done((bf16[4,128,256]{2,1,0:T(8,128)(2,1)S(1)}, bf16[4,128,256]{2,1,0:T(8,128)(2,1)S(1)}, u32[]{:S(2)}, u32[]{:S(2)}) %collective-permute-start.3) | collective-permute-done | bytes 262176 | tf_op jit(solution)/shard_map/ppermute | solution.py:276
  64.8 2.8 %collective-permute-start.4 = (bf16[8,128,256]{2,1,0:T(8,128)(2,1)S(1)}, bf16[8,128,256]{2,1,0:T(8,128)(2,1)S(1)}, u32[]{:S(2)}, u32[]{:S(2)}) collective-permute-start(bf16[8,128,256]{2,1,0:T(8,128)(2,1)S(1)} %constant_dynamic-update-slice_fusion.near_ref), channel_id=1, source_target_pairs={{0,4},{4,0},{1,5},{5,1},{2,6},{6,2},{3,7},{7,3},{8,12},{12,8},{9,1... | collective-permute-start | bytes 1572872 | tf_op jit(solution)/shard_map/ppermute | solution.py:278
  67.6 0.0 copy-done
  67.6 4.9 %shard_map.95 = (f32[128,128]{1,0:T(8,128)S(1)}, f32[1024,128]{1,0:T(8,128)S(1)}) custom-call(bf16[128,256]{1,0:T(8,128)(2,1)S(1)} %bitcast.36, bf16[27,256,128]{2,1,0:T(8,128)(2,1)S(1)} %copy-done, s32[27,128]{1,0:T(8,128)S(1)} %shard_map.94.table_ref), custom_call_target="tpu_custom_call" | custom-call | tf_op jit(solution)/shard_map/pallas_call | solution.py:252
  72.5 0.0 copy-start.4
  72.5 0.8 copy-done.4
  73.3 0.0 collective-permute-done.4.far_ref
  73.3 0.0 copy-start.2
  73.3 0.8 copy-done.2
  74.1 0.0 all-to-all-done.1.g_ref
  74.1 0.0 copy-start.3
  74.1 1.0 copy-done.3
  75.2 0.0 copy-start.5
  75.2 1.0 copy-done.5
  76.2 0.9 shard_map.98
  77.1 28.6 %all_to_all.20 = s32[128,1,768]{2,1,0:T(1,128)S(1)} all-to-all(s32[128,1,768]{2,1,0:T(1,128)S(1)} %bitcast.31), channel_id=1, replica_groups=mesh['y'=8,'zh'=4,'zl'=2,'core'=2,'scene'=4] {'y','zh','zl','core'}, dimensions={0} | all-to-all | bytes 786432 | tf_op jit(solution)/shard_map/all_to_all | solution.py:286
  105.7 0.7 shard_map.101
  106.4 4.0 %all-to-all-start.3 = ((f32[4,16,128]{2,1,0:T(8,128)}), f32[4,16,128]{2,1,0:T(8,128)S(1)}, u32[]{:S(2)}, u32[]{:S(2)}) async-start(f32[4,16,128]{2,1,0:T(8,128)} %shard_map.101), calls=%async_computation.3 | async-start | bytes 65536 | tf_op jit(solution)/shard_map/all_to_all | solution.py:295
  110.4 0.0 copy-start.7
  110.4 2.5 %shard_map.100 = bf16[128,256]{1,0:T(8,128)(2,1)} custom-call(bf16[27,256,128]{2,1,0:T(8,128)(2,1)S(1)} %copy-done, bf16[3456,128]{1,0:T(8,128)(2,1)} %shard_map.97.gathered_ref), custom_call_target="tpu_custom_call" | custom-call | flops 1000000000 | tf_op jit(solution)/shard_map/pallas_call | solution.py:269
  112.9 0.0 copy-done.7
  112.9 1.1 shard_map.99
  114.0 0.7 all-to-all-done.3
  114.7 0.1 mul.17
  114.9 0.6 copy.18
  (11 shorter events, 0.2 us)
Async XLA Ops:
  0.6 0.7 copy-start.6
  1.3 0.8 copy-start.8
  2.2 0.8 copy-start.9
  3.9 43.4 %copy-start.1 = (bf16[1,128,256]{2,1,0:T(8,128)(2,1)S(1)}, bf16[1,128,256]{2,1,0:T(8,128)(2,1)}, u32[]{:S(2)}) copy-start(bf16[1,128,256]{2,1,0:T(8,128)(2,1)} %param.7) | copy-start | bytes 196612
  3.9 32.8 %all-to-all-start = ((bf16[128,8,128]{2,1,0:T(8,128)(2,1)}), bf16[128,8,128]{2,1,0:T(8,128)(2,1)S(1)}, u32[]{:S(2)}, u32[]{:S(2)}) async-start(bf16[128,8,128]{2,1,0:T(8,128)(2,1)} %bitcast.4), calls=%async_computation | async-start | bytes 524288 | tf_op jit(solution)/shard_map/all_to_all | solution.py:239
  22.4 10.7 %collective-permute-start.2 = (bf16[128,256]{1,0:T(8,128)(2,1)}, bf16[128,256]{1,0:T(8,128)(2,1)S(1)}, u32[]{:S(2)}, u32[]{:S(2)}) collective-permute-start(bf16[128,256]{1,0:T(8,128)(2,1)} %bitcast.33), channel_id=1, source_target_pairs={{0,3},{1,0},{2,1},{3,2},{4,7},{5,4},{6,5},{7,6},{8,11},{9,8},{10,9... | collective-permute-start | bytes 196616 | tf_op jit(solution)/shard_map/ppermute | solution.py:243
  26.8 7.0 %collective-permute-start.1 = (bf16[128,256]{1,0:T(8,128)(2,1)}, bf16[128,256]{1,0:T(8,128)(2,1)S(1)}, u32[]{:S(2)}, u32[]{:S(2)}) collective-permute-start(bf16[128,256]{1,0:T(8,128)(2,1)} %bitcast.34), channel_id=1, source_target_pairs={{0,2},{1,3},{2,0},{3,1},{4,6},{5,7},{6,4},{7,5},{8,10},{9,11},{10,... | collective-permute-start | bytes 196616 | tf_op jit(solution)/shard_map/ppermute | solution.py:243
  29.3 7.0 %collective-permute-start = (bf16[128,256]{1,0:T(8,128)(2,1)}, bf16[128,256]{1,0:T(8,128)(2,1)S(1)}, u32[]{:S(2)}, u32[]{:S(2)}) collective-permute-start(bf16[128,256]{1,0:T(8,128)(2,1)} %bitcast.35), channel_id=1, source_target_pairs={{0,1},{1,2},{2,3},{3,0},{4,5},{5,6},{6,7},{7,4},{8,9},{9,10},{10,1... | collective-permute-start | bytes 196616 | tf_op jit(solution)/shard_map/ppermute | solution.py:243
  41.0 26.5 %copy-start = (bf16[27,256,128]{2,1,0:T(8,128)(2,1)S(1)}, bf16[27,256,128]{2,1,0:T(8,128)(2,1)}, u32[]{:S(2)}) copy-start(bf16[27,256,128]{2,1,0:T(8,128)(2,1)} %w_ref.3) | copy-start | bytes 5308420
  41.1 33.1 %all-to-all-start.1 = ((bf16[16,216,128]{2,1,0:T(8,128)(2,1)}), bf16[16,216,128]{2,1,0:T(8,128)(2,1)S(1)}, u32[]{:S(2)}, u32[]{:S(2)}) async-start(bf16[16,216,128]{2,1,0:T(8,128)(2,1)} %bitcast.6), calls=%async_computation.1 | async-start | bytes 1769472 | tf_op jit(solution)/shard_map/all_to_all | solution.py:267
  47.4 17.4 %collective-permute-start.3 = (bf16[4,128,256]{2,1,0:T(8,128)(2,1)S(1)}, bf16[4,128,256]{2,1,0:T(8,128)(2,1)S(1)}, u32[]{:S(2)}, u32[]{:S(2)}) collective-permute-start(bf16[4,128,256]{2,1,0:T(8,128)(2,1)S(1)} %pad_maximum_fusion), channel_id=1, source_target_pairs={{0,8},{8,0},{1,9},{9,1},{2,10},{10,2},{3,11},{11,3},{4,12},{12,4},... | collective-permute-start | bytes 786440 | tf_op jit(solution)/shard_map/ppermute | solution.py:276
  64.8 8.6 %collective-permute-start.4 = (bf16[8,128,256]{2,1,0:T(8,128)(2,1)S(1)}, bf16[8,128,256]{2,1,0:T(8,128)(2,1)S(1)}, u32[]{:S(2)}, u32[]{:S(2)}) collective-permute-start(bf16[8,128,256]{2,1,0:T(8,128)(2,1)S(1)} %constant_dynamic-update-slice_fusion.near_ref), channel_id=1, source_target_pairs={{0,4},{4,0},{1,5},{5,1},{2,6},{6,2},{3,7},{7,3},{8,12},{12,8},{9,1... | collective-permute-start | bytes 1572872 | tf_op jit(solution)/shard_map/ppermute | solution.py:278
  72.5 0.8 copy-start.4
  73.3 0.8 copy-start.2
  74.1 1.0 copy-start.3
  75.2 1.0 copy-start.5
  106.4 8.3 %all-to-all-start.3 = ((f32[4,16,128]{2,1,0:T(8,128)}), f32[4,16,128]{2,1,0:T(8,128)S(1)}, u32[]{:S(2)}, u32[]{:S(2)}) async-start(f32[4,16,128]{2,1,0:T(8,128)} %shard_map.101), calls=%async_computation.3 | async-start | bytes 65536 | tf_op jit(solution)/shard_map/all_to_all | solution.py:295
  110.4 2.5 %copy-start.7 = (s32[1,1,1024]{2,1,0:T(1,128)S(1)}, s32[1,1,1024]{2,1,0:T(1,128)}, u32[]{:S(2)}) copy-start(s32[1,1,1024]{2,1,0:T(1,128)} %param.13) | copy-start | bytes 12292

commit v5 on v4

v5 whole, which is shorter than its diff:
```python
import functools
import math

import jax
import jax.numpy as jnp
from jax import lax
from jax.experimental import pallas as pl
from jax.experimental.pallas import tpu as pltpu
from jax.sharding import Mesh
from jax.sharding import PartitionSpec as P

F32 = jnp.float32
BF16 = jnp.bfloat16
I32 = jnp.int32
LANES = 128
STEP = 4
WORDS = 8
VMEM_BYTES = 24 * 1024 * 1024
MOST_VMEM = 64 * 1024 * 1024 - 128 * 1024
SPACE = ("y", "z", "core")
GROUP = ("core", "scene")


def call(kernel, outs, scratch=(), flops=0, moved=0, vmem=VMEM_BYTES, **specs):
    return pl.pallas_call(
        kernel,
        out_shape=outs,
        scratch_shapes=list(scratch),
        **specs,
        compiler_params=pltpu.CompilerParams(vmem_limit_bytes=vmem),
        cost_estimate=pl.CostEstimate(flops=flops, bytes_accessed=moved, transcendentals=0),
    )


def rows_iota(rows, start=0):
    return lax.broadcasted_iota(I32, (rows, LANES), 0) + start


def one_hot(iota, row):
    return jnp.where(iota == row, 1.0, 0.0).astype(BF16)


def split_two(value):
    high = value.astype(BF16)
    low = (value - high.astype(F32)).astype(BF16)
    return high, low


def lane_block(k):
    return slice(k * LANES, (k + 1) * LANES)


def gather_kernel(cot_any, mask_any, recv_any, up_ref, out_ref, cot_ref, mask_ref, recv_ref, sems):
    pairs = ((cot_any, cot_ref), (mask_any, mask_ref), (recv_any, recv_ref))
    copies = [pltpu.make_async_copy(a, b, sems.at[i]) for i, (a, b) in enumerate(pairs)]
    for copy in copies:
        copy.start()
    for copy in copies:
        copy.wait()
    up = (cot_ref[...].astype(F32) * mask_ref[...].astype(F32)).astype(BF16)
    up_ref[...] = up
    iota = rows_iota(LANES)
    for g in range(recv_ref.shape[0]):
        hot = one_hot(iota, recv_ref[g : g + 1, :])
        rows = lax.dot_general(hot, up, (((0,), (0,)), ((), ())), preferred_element_type=F32)
        out_ref[lane_block(g), :] = rows.astype(BF16)


def table_kernel(in_ref, out_ref, up_ref, table_ref, turned_ref, *, targets):
    turned_ref[...] = up_ref[...].T
    iota = rows_iota(LANES)
    picks = rows_iota(16)
    for k in range(in_ref.shape[0]):
        hot = one_hot(iota, in_ref[k : k + 1, :])
        target = out_ref[k : k + 1, :]
        code = jnp.where(target < targets, target + 1, 0)
        digits = jnp.where(picks == 0, code >> 7, jnp.where(picks == 1, code & 127, 0))
        found = lax.dot_general(
            digits.astype(F32).astype(BF16), hot, (((1,), (1,)), ((), ())), preferred_element_type=F32
        )
        table_ref[k : k + 1, :] = (found[0:1] * 128.0 + found[1:2] - 1.0).astype(I32)


def lookup_kernel(turned_ref, back_ref, table_ref, gathered_ref, ext_ref, hot_ref):
    blocks = back_ref.shape[0] // LANES
    offsets = table_ref.shape[0]
    ext_ref[:, 0:LANES] = turned_ref[...]
    for b in range(blocks):
        ext_ref[:, lane_block(b + 1)] = back_ref[lane_block(b), :].T
    iota = rows_iota((blocks + 1) * LANES)
    step = STEP
    for first in range(0, offsets, step):
        count = min(step, offsets - first)
        slot = (first // step) % 2
        for k in range(count):
            hot_ref[slot, :, lane_block(k)] = one_hot(iota, table_ref[first + k : first + k + 1, :])
        rows = jnp.dot(
            ext_ref[...], hot_ref[slot, :, : count * LANES], preferred_element_type=F32
        ).astype(BF16)
        for k in range(count):
            gathered_ref[lane_block(first + k), :] = rows[:, lane_block(k)]


def encode(value, top):
    level = jnp.ceil(jnp.log2(jnp.maximum(top, 1e-36)) * 8.0)
    code = jnp.round(value * jnp.exp2(level * -0.125) * 32767.0)
    return jnp.clip(code, -32767.0, 32767.0).astype(I32), level.astype(I32)


def unit(level):
    return jnp.exp2(level.astype(F32) * 0.125) * (1.0 / 32767.0)


def join(first, second):
    return (first << 16) | (second & 0xFFFF)


def halves(word):
    return (word >> 16).astype(F32), ((word << 16) >> 16).astype(F32)


def row_top(value):
    return jnp.max(jnp.abs(value), axis=1, keepdims=True)


def fetch(w_any, w_ref, sems):
    offsets = w_ref.shape[0]
    step = offsets // sems.shape[0]
    copies = []
    for i in range(sems.shape[0]):
        part = pl.ds(i * step, step)
        copies.append(pltpu.make_async_copy(w_any.at[part], w_ref.at[part], sems.at[i]))
        copies[-1].start()
    return copies, step


def input_grad_kernel(w_any, gathered_ref, grad_ref, w_ref, sems):
    copies, step = fetch(w_any, w_ref, sems)
    total = jnp.zeros((w_ref.shape[1], LANES), F32)
    for k in range(w_ref.shape[0]):
        if k % step == 0:
            copies[k // step].wait()
        total += jnp.dot(w_ref[k], gathered_ref[lane_block(k), :], preferred_element_type=F32)
    grad_ref[...] = total.T.astype(BF16)


def forward_kernel(
    x_ref, w_any, table_ref, own_ref, word_ref, w_ref, terms_ref, hot_ref, send_ref, sems, *, free
):
    offsets = w_ref.shape[0]
    copies, step = fetch(w_any, w_ref, sems)
    for k in range(offsets):
        if k % step == 0:
            copies[k // step].wait()
        high, low = split_two(jnp.dot(x_ref[...], w_ref[k], preferred_element_type=F32))
        terms_ref[lane_block(k), 0:LANES] = high
        terms_ref[lane_block(k), LANES : 2 * LANES] = low

    def block(start):
        here = rows_iota(LANES) + start
        for k in range(offsets):
            hot_ref[:, lane_block(k)] = one_hot(here, table_ref[k : k + 1, :])
        both = jnp.dot(hot_ref[...], terms_ref[...], preferred_element_type=F32)
        return both[:, :LANES] + both[:, LANES:]

    own_ref[...] = block(0)

    def scatter(b, carry):
        send_ref[pl.ds(pl.multiple_of(b * LANES, LANES), LANES), :] = block((b + 1) * LANES)
        return carry

    lax.fori_loop(0, send_ref.shape[0] // LANES, scatter, 0)
    peers = word_ref.shape[1]
    lane = lax.broadcasted_iota(I32, (peers, LANES), 1)
    levels = jnp.zeros((peers, LANES), I32)
    for r in range(4):
        words = []
        for slot in (r, r + 4):
            value = send_ref[pl.ds(slot, peers, stride=8), :]
            code, level = encode(value, row_top(value))
            words.append(code)
            levels = jnp.where(lane == free + slot, level, levels)
        word_ref[r] = join(*words)
    word_ref[4] = levels


def pack_kernel(g_ref, near_ref, far_ref, word_ref, out_ref, turn_ref):
    columns = g_ref.shape[1]
    peers = word_ref.shape[1]
    blocks = turn_ref.shape[0]
    scenes = near_ref.shape[0]
    core, scene = (lax.axis_index(axis) for axis in GROUP)
    total = jnp.zeros((columns, near_ref.shape[2]), F32)
    for s in range(g_ref.shape[0]):
        x_ref, holder = (near_ref, core) if s < scenes else (far_ref, 1 - core)
        sender = holder * scenes + lax.rem(scene + scenes - s % scenes, scenes)
        total += jnp.dot(g_ref[sender], x_ref[s % scenes], preferred_element_type=F32)
    rest = blocks * LANES - columns
    total = jnp.concatenate([total, jnp.zeros((rest, total.shape[1]), F32)], axis=0)
    for h in range(blocks):
        turn_ref[h] = total[lane_block(h), :].T
    for r in range(4):
        out_ref[pl.ds(r, peers, stride=WORDS), :] = word_ref[r]
    parts = [[turn_ref[h, pl.ds(c, peers, stride=2), :] for c in range(2)] for h in range(blocks)]
    top = functools.reduce(jnp.maximum, [jnp.abs(part) for pair in parts for part in pair])
    top = jnp.max(top, axis=1, keepdims=True)
    free = LANES - rest
    lane = lax.broadcasted_iota(I32, (peers, LANES), 1)
    for h in range(blocks):
        codes = [encode(part, top) for part in parts[h]]
        word = join(codes[0][0], codes[1][0])
        if h == blocks - 1:
            levels = jnp.where(lane == free + 8, codes[0][1], word_ref[4])
            word = jnp.where(lane < free, word, levels)
        out_ref[pl.ds(4 + h, peers, stride=WORDS), :] = word


def sum_kernel(arrived_ref, out_ref, *, free):
    peers = arrived_ref.shape[0] // WORDS
    words = [arrived_ref[pl.ds(4 + h, peers, stride=WORDS), :] for h in range(4)]
    scale = unit(words[-1][:, free + 8 : free + 9])
    for h in range(4):
        for c, value in enumerate(halves(words[h])):
            total = (value * scale).reshape(peers // 8, 8, LANES).sum(axis=0)
            total = (total[0:2] + total[2:4]) + (total[4:6] + total[6:8])
            row = 2 * (4 * c + h)
            for s in range(out_ref.shape[0]):
                out_ref[s, row : row + 2, :] = total


def receive_kernel(own_ref, arrived_ref, recv_ref, out_ref, rows_ref, *, free):
    peers = arrived_ref.shape[0] // WORDS
    iota = rows_iota(LANES)
    levels = arrived_ref[pl.ds(WORDS - 1, peers, stride=WORDS), :]
    for r in range(4):
        pair = halves(arrived_ref[pl.ds(r, peers, stride=WORDS), :])
        for value, slot in zip(pair, (r, r + 4)):
            scale = unit(levels[:, free + slot : free + slot + 1])
            rows_ref[pl.ds(slot, peers, stride=8), :] = value * scale
    total = own_ref[...]
    for g in range(recv_ref.shape[0]):
        hot = one_hot(iota, recv_ref[g : g + 1, :])
        high, low = split_two(rows_ref[lane_block(g), :])
        total += jnp.dot(hot, high, preferred_element_type=F32)
        total += jnp.dot(hot, low, preferred_element_type=F32)
    out_ref[...] = total.astype(BF16)


def local(features, cotangent, relu_mask, weight, pair_in, pair_out, recv_index):
    x = features[0]
    own_rows, in_width = x.shape
    offsets, unused, out_width = weight.shape
    peers = lax.axis_size(SPACE)
    group = lax.axis_size(GROUP)
    scenes = lax.axis_size("scene")
    send_rows = recv_index.shape[2]
    slots = send_rows // peers
    targets = own_rows + send_rows
    columns = offsets * out_width // group
    recv = recv_index.reshape(send_rows // LANES, LANES)
    shape = jax.ShapeDtypeStruct

    hbm = pl.BlockSpec(memory_space=pltpu.HBM)
    vmem = pl.BlockSpec(memory_space=pltpu.VMEM)
    weights = (pltpu.VMEM(weight.shape, BF16), pltpu.SemaphoreType.DMA((3,)))
    blocks = -(-columns // LANES)
    free = columns - (blocks - 1) * LANES

    upstream, outgoing = call(
        gather_kernel,
        (shape((own_rows, out_width), BF16), shape((send_rows, out_width), BF16)),
        scratch=(
            pltpu.VMEM((own_rows, out_width), BF16),
            pltpu.VMEM((own_rows, out_width), I32),
            pltpu.VMEM(recv.shape, I32),
            pltpu.SemaphoreType.DMA((3,)),
        ),
        in_specs=[hbm] * 3,
        vmem=MOST_VMEM,
        flops=2 * send_rows * own_rows * out_width,
        moved=send_rows * out_width * 3,
    )(cotangent[0], relu_mask[0], recv)
    own_x, outgoing = lax.optimization_barrier((x, outgoing))
    returned = lax.all_to_all(outgoing.reshape(peers, slots, out_width), SPACE, 0, 0, tiled=True)

    swap = [(0, 1), (1, 0)]
    ring = [
        lax.ppermute(own_x, "scene", [(i, (i + d) % scenes) for i in range(scenes)])
        for d in range(1, scenes)
    ]

    table, turned = call(
        functools.partial(table_kernel, targets=targets),
        (shape((offsets, own_rows), I32), shape((out_width, own_rows), BF16)),
    )(pair_in[0, 0], pair_out[0, 0], upstream)

    own, words = call(
        functools.partial(forward_kernel, free=free),
        (
            shape((own_rows, out_width), F32),
            shape((5, peers, out_width), I32),
        ),
        scratch=(
            weights[0],
            pltpu.VMEM((offsets * own_rows, 2 * out_width), BF16),
            pltpu.VMEM((LANES, offsets * own_rows), BF16),
            pltpu.VMEM((send_rows, out_width), F32),
            weights[1],
        ),
        in_specs=[vmem, hbm, vmem],
    )(x, weight, table)

    returned, *ring = lax.optimization_barrier((returned, *ring))
    gathered = call(
        lookup_kernel,
        shape((offsets * out_width, own_rows), BF16),
        scratch=(pltpu.VMEM((out_width, targets), BF16), pltpu.VMEM((2, targets, STEP * LANES), BF16)),
    )(turned, returned.reshape(send_rows, out_width), table)
    group_g = lax.all_to_all(gathered.reshape(group, columns, own_rows), GROUP, 0, 0, tiled=True)

    input_grad = call(
        input_grad_kernel,
        shape((own_rows, in_width), BF16),
        scratch=weights,
        in_specs=[hbm, vmem],
        flops=10**9,
    )(weight, gathered)

    near = jnp.stack([x] + ring)
    far = lax.ppermute(near, "core", swap)
    packed = call(
        pack_kernel,
        shape((peers * WORDS, LANES), I32),
        scratch=(pltpu.VMEM((blocks, in_width, LANES), F32),),
        flops=2 * columns * in_width * own_rows * group,
        moved=peers * WORDS * LANES * 8,
    )(group_g, near, far, words)
    arrived = lax.all_to_all(packed.reshape(peers, WORDS, LANES), SPACE, 0, 0, tiled=True)
    arrived = arrived.reshape(peers * WORDS, LANES)

    quarter = call(
        functools.partial(sum_kernel, free=free),
        shape((scenes, 16, LANES), F32),
        moved=peers * WORDS * LANES * 4,
    )(arrived)
    sums = lax.all_to_all(quarter, "scene", 0, 0, tiled=True)
    conv_out = call(
        functools.partial(receive_kernel, free=free),
        shape((own_rows, out_width), BF16),
        scratch=(pltpu.VMEM((send_rows, out_width), F32),),
        flops=4 * send_rows * own_rows * out_width,
        moved=send_rows * out_width * 4,
    )(own, arrived, recv)

    own_in = in_width // peers
    sums = sums.reshape(scenes, own_in, blocks, 2, LANES).transpose(1, 3, 0, 2, 4)
    sums = sums.reshape(own_in, group, blocks * LANES)[:, :, :columns]
    kernel_grad = sums.reshape(own_in, offsets, out_width)
    kernel_grad = kernel_grad.transpose(1, 0, 2).reshape(offsets, own_in * out_width)
    normalizer = 1.0 / math.sqrt(scenes * peers * own_rows)
    return (conv_out[None], input_grad[None], kernel_grad * normalizer)


def solution(mesh):
    scenes = mesh.devices.shape[1]
    fine = Mesh(mesh.devices.reshape(8, 8, 2, scenes), ("y", "z", "core", "scene"))
    voxels = P("scene", SPACE)
    return jax.shard_map(
        local,
        mesh=fine,
        in_specs=(voxels, voxels, voxels, P(), voxels, voxels, voxels),
        out_specs=(voxels, voxels, P(None, SPACE)),
        check_vma=False,
    )
```

time: 117 us -> 103 us (0.88)
  waiting for transfers between devices: 18.3 us -> 6.6 us
  starting transfers between devices: 44.2 us -> 39.2 us
  local copies, waits for them, and re-layouts: 7.58 us -> 3.74 us
  blocking collectives: 28.6 us -> 31.5 us
  Pallas kernels: 16.1 us -> 18.9 us
    ppermute x2 -> x1, waiting for transfers between devices: 14 us -> 0.01 us  [local(): far = lax.ppermute(near, 'core', swap)]
    ppermute x2 -> x1, starting transfers between devices: 6.08 us -> 1.92 us  [local(): far = lax.ppermute(near, 'core', swap)]
    all_to_all x1, waiting for transfers between devices: 0.01 us -> 3.82 us  [local(): lax.all_to_all(gathered.reshape(group, columns, own_rows), GROUP, 0, 0, t...]
    unnamed x27 -> x17, local copies, waits for them, and re-layouts: 7.39 us -> 3.61 us
    all_to_all x1, blocking collectives: 28.6 us -> 31.5 us  [local(): lax.all_to_all(packed.reshape(peers, WORDS, LANES), SPACE, 0, 0, tiled=True)]
    pallas_call x4, Pallas kernels: 8.89 us -> 10.8 us  [the longest x1 5.95 us: local(): call(functools.partial(forward_kernel, free=free), (shape((own_rows, out_...]
  transfers between devices with their start and end apart: 8 -> 7, of which waited for: 5 -> 3; matrix products, arithmetic and copies ran while one was open for 1% -> 1% of each run, Pallas kernels for 8% -> 11%
where the time goes in v5:
time: 103 us; the launch traced here: 101 us
  starting transfers between devices  39.2 us (38%)
  blocking collectives  31.5 us (31%)
  Pallas kernels  18.9 us (18%)
  waiting for transfers between devices  6.6 us (6%)
  local copies, waits for them, and re-layouts  3.74 us (4%)
    all_to_all x1, blocking collectives, local(): lax.all_to_all(packed.reshape(peers, WORDS, LANES), SPACE, 0, 0, tiled=True)  31.5 us
    all_to_all x1, starting transfers between devices, local(): lax.all_to_all(outgoing.reshape(peers, slots, out_width), SPACE, 0, 0, ti...  18.6 us
    ppermute x3, starting transfers between devices, local(): lax.ppermute(own_x, 'scene', [(i, (i + d) % scenes) for i in range(scenes)])  9.33 us
    all_to_all x1, starting transfers between devices, local(): lax.all_to_all(gathered.reshape(group, columns, own_rows), GROUP, 0, 0, t...  6.08 us
    pallas_call x1, Pallas kernels, local(): call(functools.partial(forward_kernel, free=free), (shape((own_rows, out_...  5.95 us
    pallas_call x1, Pallas kernels, local(): call(lookup_kernel, shape((offsets * out_width, own_rows), BF16), scratch...  4.38 us
    all_to_all x1, waiting for transfers between devices, local(): lax.all_to_all(gathered.reshape(group, columns, own_rows), GROUP, 0, 0, t...  3.82 us
    unnamed x17, local copies, waits for them, and re-layouts  3.61 us
  transfers between devices with their start and end apart: 7, of which 3 were waited for; matrix products, arithmetic and copies ran while one was open for 1% of the time, Pallas kernels for 11%

profile of v5, /device:TPU:1, one launch (start us, length us, event | category | flops | bytes accessed | tf_op | source)
XLA Modules:
  0.0 100.8 jit_solution(3410007874986555686)
XLA Ops:
  0.6 1.9 %shard_map.94 = (bf16[128,128]{1,0:T(8,128)(2,1)}, bf16[1024,128]{1,0:T(8,128)(2,1)}) custom-call(bf16[128,128]{1,0:T(8,128)(2,1)} %bitcast.47, s32[128,128]{1,0:T(8,128)} %bitcast.46, s32[8,128]{1,0:T(8,128)} %bitcast.34), custom_call_target="tpu_custom_call" | custom-call | flops 33554432 | bytes 393216 | tf_op jit(solution)/shard_map/pallas_call | solution.py:269
  2.5 0.0 copy-start.1
  2.5 18.6 %all-to-all-start = ((bf16[128,8,128]{2,1,0:T(8,128)(2,1)}), bf16[128,8,128]{2,1,0:T(8,128)(2,1)S(1)}, u32[]{:S(2)}, u32[]{:S(2)}) async-start(bf16[128,8,128]{2,1,0:T(8,128)(2,1)} %bitcast.36), calls=%async_computation | async-start | bytes 524288 | tf_op jit(solution)/shard_map/all_to_all | solution.py:284
  21.1 4.4 %collective-permute-start.2 = (bf16[128,256]{1,0:T(8,128)(2,1)}, bf16[128,256]{1,0:T(8,128)(2,1)S(1)}, u32[]{:S(2)}, u32[]{:S(2)}) collective-permute-start(bf16[128,256]{1,0:T(8,128)(2,1)} %bitcast.30), channel_id=1, source_target_pairs={{0,3},{1,0},{2,1},{3,2},{4,7},{5,4},{6,5},{7,6},{8,11},{9,8},{10,9... | collective-permute-start | bytes 196616 | tf_op jit(solution)/shard_map/ppermute | solution.py:288
  25.5 2.4 %collective-permute-start.1 = (bf16[128,256]{1,0:T(8,128)(2,1)}, bf16[128,256]{1,0:T(8,128)(2,1)S(1)}, u32[]{:S(2)}, u32[]{:S(2)}) collective-permute-start(bf16[128,256]{1,0:T(8,128)(2,1)} %bitcast.31), channel_id=1, source_target_pairs={{0,2},{1,3},{2,0},{3,1},{4,6},{5,7},{6,4},{7,5},{8,10},{9,11},{10,... | collective-permute-start | bytes 196616 | tf_op jit(solution)/shard_map/ppermute | solution.py:288
  27.9 2.5 %collective-permute-start = (bf16[128,256]{1,0:T(8,128)(2,1)}, bf16[128,256]{1,0:T(8,128)(2,1)S(1)}, u32[]{:S(2)}, u32[]{:S(2)}) collective-permute-start(bf16[128,256]{1,0:T(8,128)(2,1)} %bitcast.32), channel_id=1, source_target_pairs={{0,1},{1,2},{2,3},{3,0},{4,5},{5,6},{6,7},{7,4},{8,9},{9,10},{10,1... | collective-permute-start | bytes 196616 | tf_op jit(solution)/shard_map/ppermute | solution.py:288
  30.4 0.7 copy_bitcast_fusion.1
  31.2 0.0 copy-start.5
  31.2 0.8 copy-done.5
  31.9 0.0 copy-start
  31.9 0.6 shard_map.95
  32.5 0.0 collective-permute-done.2
  32.5 0.0 collective-permute-done.1
  32.5 2.4 %collective-permute-done = bf16[128,256]{1,0:T(8,128)(2,1)S(1)} collective-permute-done((bf16[128,256]{1,0:T(8,128)(2,1)}, bf16[128,256]{1,0:T(8,128)(2,1)S(1)}, u32[]{:S(2)}, u32[]{:S(2)}) %collective-permute-start) | collective-permute-done | bytes 65568 | tf_op jit(solution)/shard_map/ppermute | solution.py:288
  34.9 0.4 all-to-all-done
  35.3 4.4 %shard_map.97.gathered_ref = bf16[3456,128]{1,0:T(8,128)(2,1)} custom-call(bf16[128,128]{1,0:T(8,128)(2,1)S(1)} %get-tuple-element.18.turned_ref, bf16[1024,128]{1,0:T(8,128)(2,1)S(1)} %bitcast.29, s32[27,128]{1,0:T(8,128)S(1)} %get-tuple-element.16.table_ref), custom_call_target="tpu_custom_call" | custom-call | tf_op jit(solution)/shard_map/pallas_call | solution.py:314
  39.7 6.1 %all-to-all-start.1 = ((bf16[8,432,128]{2,1,0:T(8,128)(2,1)}), bf16[8,432,128]{2,1,0:T(8,128)(2,1)S(1)}, u32[]{:S(2)}, u32[]{:S(2)}) async-start(bf16[8,432,128]{2,1,0:T(8,128)(2,1)} %bitcast.6), calls=%async_computation.1 | async-start | bytes 1769472 | tf_op jit(solution)/shard_map/all_to_all | solution.py:319
  45.8 0.0 copy-done.1
  45.8 1.9 %collective-permute-start.3 = (bf16[4,128,256]{2,1,0:T(8,128)(2,1)S(1)}, bf16[4,128,256]{2,1,0:T(8,128)(2,1)S(1)}, u32[]{:S(2)}, u32[]{:S(2)}) collective-permute-start(bf16[4,128,256]{2,1,0:T(8,128)(2,1)S(1)} %pad_maximum_fusion.near_ref), channel_id=1, source_target_pairs={{0,4},{4,0},{1,5},{5,1},{2,6},{6,2},{3,7},{7,3},{8,12},{12,8},{9,1... | collective-permute-start | bytes 786440 | tf_op jit(solution)/shard_map/ppermute | solution.py:330
  47.7 0.0 copy-done
  47.7 0.0 copy-start.2
  47.8 0.8 copy-done.2
  48.6 5.9 %shard_map.96 = (f32[128,128]{1,0:T(8,128)S(1)}, s32[5,128,128]{2,1,0:T(8,128)S(1)}) custom-call(bf16[128,256]{1,0:T(8,128)(2,1)S(1)} %bitcast.33, bf16[27,256,128]{2,1,0:T(8,128)(2,1)S(1)} %copy-done, s32[27,128]{1,0:T(8,128)S(1)} %get-tuple-element.16.table_ref), custom_call_target="tpu_custom_call" | custom-call | tf_op jit(solution)/shard_map/pallas_call | solution.py:297
  54.5 0.0 copy-start.3
  54.6 0.6 copy-done.3
  55.2 0.0 collective-permute-done.3.far_ref
  55.2 3.8 %all-to-all-done.1.g_ref = bf16[8,432,128]{2,1,0:T(8,128)(2,1)S(1)} async-done(((bf16[8,432,128]{2,1,0:T(8,128)(2,1)}), bf16[8,432,128]{2,1,0:T(8,128)(2,1)S(1)}, u32[]{:S(2)}, u32[]{:S(2)}) %all-to-all-start.1) | async-done | bytes 884768 | tf_op jit(solution)/shard_map/all_to_all | solution.py:319
  59.0 0.9 shard_map.98
  59.9 31.5 %all_to_all.20 = s32[128,8,128]{2,1,0:T(8,128)S(1)} all-to-all(s32[128,8,128]{2,1,0:T(8,128)S(1)} %bitcast.28), channel_id=1, replica_groups=mesh['y'=8,'z'=8,'core'=2,'scene'=4] {'y','z','core'}, dimensions={0} | all-to-all | bytes 1048576 | tf_op jit(solution)/shard_map/all_to_all | solution.py:338
  91.5 0.7 shard_map.101
  92.2 3.3 %all-to-all-start.3 = ((f32[4,16,128]{2,1,0:T(8,128)}), f32[4,16,128]{2,1,0:T(8,128)S(1)}, u32[]{:S(2)}, u32[]{:S(2)}) async-start(f32[4,16,128]{2,1,0:T(8,128)} %shard_map.101), calls=%async_computation.3 | async-start | bytes 65536 | tf_op jit(solution)/shard_map/all_to_all | solution.py:346
  95.5 0.0 copy-start.4
  95.5 0.0 copy-start.6
  95.5 3.4 %shard_map.100 = bf16[128,256]{1,0:T(8,128)(2,1)} custom-call(bf16[27,256,128]{2,1,0:T(8,128)(2,1)S(1)} %copy-done, bf16[3456,128]{1,0:T(8,128)(2,1)} %shard_map.97.gathered_ref), custom_call_target="tpu_custom_call" | custom-call | flops 1000000000 | tf_op jit(solution)/shard_map/pallas_call | solution.py:321
  98.9 0.0 copy-done.4
  98.9 0.0 copy-done.6
  98.9 1.1 %shard_map.99 = bf16[128,128]{1,0:T(8,128)(2,1)} custom-call(f32[128,128]{1,0:T(8,128)S(1)} %copy-done.4, s32[1024,128]{1,0:T(8,128)S(1)} %bitcast.27, s32[8,128]{1,0:T(8,128)S(1)} %bitcast.35), custom_call_target="tpu_custom_call" | custom-call | flops 67108864 | bytes 524288 | tf_op jit(solution)/shard_map/pallas_call | solution.py:347
  100.0 0.0 all-to-all-done.3
  100.0 0.1 mul.17
  100.2 0.6 copy.15
  (6 shorter events, 0.1 us)
Async XLA Ops:
  2.5 43.3 %copy-start.1 = (bf16[1,128,256]{2,1,0:T(8,128)(2,1)S(1)}, bf16[1,128,256]{2,1,0:T(8,128)(2,1)}, u32[]{:S(2)}) copy-start(bf16[1,128,256]{2,1,0:T(8,128)(2,1)} %param.7) | copy-start | bytes 196612
  2.5 32.8 %all-to-all-start = ((bf16[128,8,128]{2,1,0:T(8,128)(2,1)}), bf16[128,8,128]{2,1,0:T(8,128)(2,1)S(1)}, u32[]{:S(2)}, u32[]{:S(2)}) async-start(bf16[128,8,128]{2,1,0:T(8,128)(2,1)} %bitcast.36), calls=%async_computation | async-start | bytes 524288 | tf_op jit(solution)/shard_map/all_to_all | solution.py:284
  21.1 11.4 %collective-permute-start.2 = (bf16[128,256]{1,0:T(8,128)(2,1)}, bf16[128,256]{1,0:T(8,128)(2,1)S(1)}, u32[]{:S(2)}, u32[]{:S(2)}) collective-permute-start(bf16[128,256]{1,0:T(8,128)(2,1)} %bitcast.30), channel_id=1, source_target_pairs={{0,3},{1,0},{2,1},{3,2},{4,7},{5,4},{6,5},{7,6},{8,11},{9,8},{10,9... | collective-permute-start | bytes 196616 | tf_op jit(solution)/shard_map/ppermute | solution.py:288
  25.5 7.0 %collective-permute-start.1 = (bf16[128,256]{1,0:T(8,128)(2,1)}, bf16[128,256]{1,0:T(8,128)(2,1)S(1)}, u32[]{:S(2)}, u32[]{:S(2)}) collective-permute-start(bf16[128,256]{1,0:T(8,128)(2,1)} %bitcast.31), channel_id=1, source_target_pairs={{0,2},{1,3},{2,0},{3,1},{4,6},{5,7},{6,4},{7,5},{8,10},{9,11},{10,... | collective-permute-start | bytes 196616 | tf_op jit(solution)/shard_map/ppermute | solution.py:288
  27.9 7.0 %collective-permute-start = (bf16[128,256]{1,0:T(8,128)(2,1)}, bf16[128,256]{1,0:T(8,128)(2,1)S(1)}, u32[]{:S(2)}, u32[]{:S(2)}) collective-permute-start(bf16[128,256]{1,0:T(8,128)(2,1)} %bitcast.32), channel_id=1, source_target_pairs={{0,1},{1,2},{2,3},{3,0},{4,5},{5,6},{6,7},{7,4},{8,9},{9,10},{10,1... | collective-permute-start | bytes 196616 | tf_op jit(solution)/shard_map/ppermute | solution.py:288
  31.2 0.8 copy-start.5
  31.9 15.8 %copy-start = (bf16[27,256,128]{2,1,0:T(8,128)(2,1)S(1)}, bf16[27,256,128]{2,1,0:T(8,128)(2,1)}, u32[]{:S(2)}) copy-start(bf16[27,256,128]{2,1,0:T(8,128)(2,1)} %w_any.3) | copy-start | bytes 5308420
  39.7 19.3 %all-to-all-start.1 = ((bf16[8,432,128]{2,1,0:T(8,128)(2,1)}), bf16[8,432,128]{2,1,0:T(8,128)(2,1)S(1)}, u32[]{:S(2)}, u32[]{:S(2)}) async-start(bf16[8,432,128]{2,1,0:T(8,128)(2,1)} %bitcast.6), calls=%async_computation.1 | async-start | bytes 1769472 | tf_op jit(solution)/shard_map/all_to_all | solution.py:319
  45.8 9.4 %collective-permute-start.3 = (bf16[4,128,256]{2,1,0:T(8,128)(2,1)S(1)}, bf16[4,128,256]{2,1,0:T(8,128)(2,1)S(1)}, u32[]{:S(2)}, u32[]{:S(2)}) collective-permute-start(bf16[4,128,256]{2,1,0:T(8,128)(2,1)S(1)} %pad_maximum_fusion.near_ref), channel_id=1, source_target_pairs={{0,4},{4,0},{1,5},{5,1},{2,6},{6,2},{3,7},{7,3},{8,12},{12,8},{9,1... | collective-permute-start | bytes 786440 | tf_op jit(solution)/shard_map/ppermute | solution.py:330
  47.7 0.8 copy-start.2
  54.5 0.6 copy-start.3
  92.2 7.8 %all-to-all-start.3 = ((f32[4,16,128]{2,1,0:T(8,128)}), f32[4,16,128]{2,1,0:T(8,128)S(1)}, u32[]{:S(2)}, u32[]{:S(2)}) async-start(f32[4,16,128]{2,1,0:T(8,128)} %shard_map.101), calls=%async_computation.3 | async-start | bytes 65536 | tf_op jit(solution)/shard_map/all_to_all | solution.py:346
  95.5 3.4 %copy-start.4 = (f32[128,128]{1,0:T(8,128)S(1)}, f32[128,128]{1,0:T(8,128)}, u32[]{:S(2)}) copy-start(f32[128,128]{1,0:T(8,128)} %copy-done.3) | copy-start | bytes 196612
  95.5 3.4 %copy-start.6 = (s32[1,1,1024]{2,1,0:T(1,128)S(1)}, s32[1,1,1024]{2,1,0:T(1,128)}, u32[]{:S(2)}) copy-start(s32[1,1,1024]{2,1,0:T(1,128)} %param.13) | copy-start | bytes 12292

commit v6 on v5

--- a/solution.py
+++ b/solution.py
@@ -40,6 +40,13 @@
     return jnp.where(iota == row, 1.0, 0.0).astype(BF16)
 
 
+def one_hot_16(iota, row):
+    rows = iota.shape[0]
+    narrow = jnp.broadcast_to(row, (16, LANES)).astype(jnp.int16)
+    narrow = jnp.concatenate([narrow] * (rows // 16), axis=0)
+    return jnp.where(iota == narrow, jnp.ones((rows, LANES), BF16), jnp.zeros((rows, LANES), BF16))
+
+
 def split_two(value):
     high = value.astype(BF16)
     low = (value - high.astype(F32)).astype(BF16)
@@ -50,7 +57,7 @@
     return slice(k * LANES, (k + 1) * LANES)
 
 
-def gather_kernel(cot_any, mask_any, recv_any, up_ref, out_ref, cot_ref, mask_ref, recv_ref, sems):
+def gather_kernel(cot_any, mask_any, recv_any, up_ref, out_any, cot_ref, mask_ref, recv_ref, out_ref, sems, out_sems):
     pairs = ((cot_any, cot_ref), (mask_any, mask_ref), (recv_any, recv_ref))
     copies = [pltpu.make_async_copy(a, b, sems.at[i]) for i, (a, b) in enumerate(pairs)]
     for copy in copies:
@@ -60,10 +67,16 @@
     up = (cot_ref[...].astype(F32) * mask_ref[...].astype(F32)).astype(BF16)
     up_ref[...] = up
     iota = rows_iota(LANES)
+    copies = []
     for g in range(recv_ref.shape[0]):
         hot = one_hot(iota, recv_ref[g : g + 1, :])
         rows = lax.dot_general(hot, up, (((0,), (0,)), ((), ())), preferred_element_type=F32)
         out_ref[lane_block(g), :] = rows.astype(BF16)
+        part = pl.ds(g * LANES, LANES)
+        copies.append(pltpu.make_async_copy(out_ref.at[part], out_any.at[part], out_sems.at[g]))
+        copies[-1].start()
+    for copy in copies:
+        copy.wait()
 
 
 def table_kernel(in_ref, out_ref, up_ref, table_ref, turned_ref, *, targets):
@@ -81,24 +94,31 @@
         table_ref[k : k + 1, :] = (found[0:1] * 128.0 + found[1:2] - 1.0).astype(I32)
 
 
-def lookup_kernel(turned_ref, back_ref, table_ref, gathered_ref, ext_ref, hot_ref):
+def lookup_kernel(turned_ref, back_ref, table_ref, gathered_any, ext_ref, hot_ref, gathered_ref, sems):
     blocks = back_ref.shape[0] // LANES
     offsets = table_ref.shape[0]
     ext_ref[:, 0:LANES] = turned_ref[...]
     for b in range(blocks):
         ext_ref[:, lane_block(b + 1)] = back_ref[lane_block(b), :].T
-    iota = rows_iota((blocks + 1) * LANES)
-    step = STEP
-    for first in range(0, offsets, step):
-        count = min(step, offsets - first)
-        slot = (first // step) % 2
+    iota = rows_iota((blocks + 1) * LANES).astype(jnp.int16)
+    copies = []
+    for first in range(0, offsets, STEP):
+        count = min(STEP, offsets - first)
+        slot = (first // STEP) % 2
         for k in range(count):
-            hot_ref[slot, :, lane_block(k)] = one_hot(iota, table_ref[first + k : first + k + 1, :])
+            hot_ref[slot, :, lane_block(k)] = one_hot_16(iota, table_ref[first + k : first + k + 1, :])
         rows = jnp.dot(
             ext_ref[...], hot_ref[slot, :, : count * LANES], preferred_element_type=F32
         ).astype(BF16)
         for k in range(count):
             gathered_ref[lane_block(first + k), :] = rows[:, lane_block(k)]
+        part = pl.ds(first * LANES, count * LANES)
+        copies.append(
+            pltpu.make_async_copy(gathered_ref.at[part], gathered_any.at[part], sems.at[first // STEP])
+        )
+        copies[-1].start()
+    for copy in copies:
+        copy.wait()
 
 
 def encode(value, top):
@@ -123,43 +143,59 @@
     return jnp.max(jnp.abs(value), axis=1, keepdims=True)
 
 
-def fetch(w_any, w_ref, sems):
+def fetch(w_any, w_ref, gathered_any, gathered_ref, sems):
     offsets = w_ref.shape[0]
-    step = offsets // sems.shape[0]
+    parts = sems.shape[1]
+    step = offsets // parts
     copies = []
-    for i in range(sems.shape[0]):
+    for i in range(parts):
         part = pl.ds(i * step, step)
-        copies.append(pltpu.make_async_copy(w_any.at[part], w_ref.at[part], sems.at[i]))
-        copies[-1].start()
+        rows = pl.ds(i * step * LANES, step * LANES)
+        copies.append(
+            (
+                pltpu.make_async_copy(w_any.at[part], w_ref.at[part], sems.at[0, i]),
+                pltpu.make_async_copy(gathered_any.at[rows], gathered_ref.at[rows], sems.at[1, i]),
+            )
+        )
+        for copy in copies[-1]:
+            copy.start()
     return copies, step
 
 
-def input_grad_kernel(w_any, gathered_ref, grad_ref, w_ref, sems):
-    copies, step = fetch(w_any, w_ref, sems)
-    total = jnp.zeros((w_ref.shape[1], LANES), F32)
-    for k in range(w_ref.shape[0]):
-        if k % step == 0:
-            copies[k // step].wait()
-        total += jnp.dot(w_ref[k], gathered_ref[lane_block(k), :], preferred_element_type=F32)
-    grad_ref[...] = total.T.astype(BF16)
-
-
 def forward_kernel(
-    x_ref, w_any, table_ref, own_ref, word_ref, w_ref, terms_ref, hot_ref, send_ref, sems, *, free
+    x_ref,
+    w_any,
+    table_ref,
+    gathered_any,
+    own_ref,
+    word_ref,
+    grad_ref,
+    w_ref,
+    gathered_ref,
+    terms_ref,
+    hot_ref,
+    send_ref,
+    sems,
+    *,
+    free,
 ):
     offsets = w_ref.shape[0]
-    copies, step = fetch(w_any, w_ref, sems)
+    copies, step = fetch(w_any, w_ref, gathered_any, gathered_ref, sems)
+    total = jnp.zeros((w_ref.shape[1], LANES), F32)
     for k in range(offsets):
         if k % step == 0:
-            copies[k // step].wait()
+            for copy in copies[k // step]:
+                copy.wait()
         high, low = split_two(jnp.dot(x_ref[...], w_ref[k], preferred_element_type=F32))
         terms_ref[lane_block(k), 0:LANES] = high
         terms_ref[lane_block(k), LANES : 2 * LANES] = low
+        total += jnp.dot(w_ref[k], gathered_ref[lane_block(k), :], preferred_element_type=F32)
+    grad_ref[...] = total.T.astype(BF16)
+    iota = rows_iota(LANES).astype(jnp.int16)
 
     def block(start):
-        here = rows_iota(LANES) + start
         for k in range(offsets):
-            hot_ref[:, lane_block(k)] = one_hot(here, table_ref[k : k + 1, :])
+            hot_ref[:, lane_block(k)] = one_hot_16(iota, table_ref[k : k + 1, :] - start)
         both = jnp.dot(hot_ref[...], terms_ref[...], preferred_element_type=F32)
         return both[:, :LANES] + both[:, LANES:]
 
@@ -262,7 +298,6 @@
 
     hbm = pl.BlockSpec(memory_space=pltpu.HBM)
     vmem = pl.BlockSpec(memory_space=pltpu.VMEM)
-    weights = (pltpu.VMEM(weight.shape, BF16), pltpu.SemaphoreType.DMA((3,)))
     blocks = -(-columns // LANES)
     free = columns - (blocks - 1) * LANES
 
@@ -273,9 +308,12 @@
             pltpu.VMEM((own_rows, out_width), BF16),
             pltpu.VMEM((own_rows, out_width), I32),
             pltpu.VMEM(recv.shape, I32),
+            pltpu.VMEM((send_rows, out_width), BF16),
             pltpu.SemaphoreType.DMA((3,)),
+            pltpu.SemaphoreType.DMA(recv.shape[:1]),
         ),
         in_specs=[hbm] * 3,
+        out_specs=(vmem, hbm),
         vmem=MOST_VMEM,
         flops=2 * send_rows * own_rows * out_width,
         moved=send_rows * out_width * 3,
@@ -294,37 +332,37 @@
         (shape((offsets, own_rows), I32), shape((out_width, own_rows), BF16)),
     )(pair_in[0, 0], pair_out[0, 0], upstream)
 
-    own, words = call(
+    returned, *ring = lax.optimization_barrier((returned, *ring))
+    gathered = call(
+        lookup_kernel,
+        shape((offsets * out_width, own_rows), BF16),
+        scratch=(
+            pltpu.VMEM((out_width, targets), BF16),
+            pltpu.VMEM((2, targets, STEP * LANES), BF16),
+            pltpu.VMEM((offsets * out_width, own_rows), BF16),
+            pltpu.SemaphoreType.DMA((-(-offsets // STEP),)),
+        ),
+        out_specs=hbm,
+    )(turned, returned.reshape(send_rows, out_width), table)
+    group_g = lax.all_to_all(gathered.reshape(group, columns, own_rows), GROUP, 0, 0, tiled=True)
+
+    own, words, input_grad = call(
         functools.partial(forward_kernel, free=free),
         (
             shape((own_rows, out_width), F32),
             shape((5, peers, out_width), I32),
+            shape((own_rows, in_width), BF16),
         ),
         scratch=(
-            weights[0],
+            pltpu.VMEM(weight.shape, BF16),
+            pltpu.VMEM((offsets * out_width, own_rows), BF16),
             pltpu.VMEM((offsets * own_rows, 2 * out_width), BF16),
             pltpu.VMEM((LANES, offsets * own_rows), BF16),
             pltpu.VMEM((send_rows, out_width), F32),
-            weights[1],
+            pltpu.SemaphoreType.DMA((2, 3)),
         ),
-        in_specs=[vmem, hbm, vmem],
-    )(x, weight, table)
-
-    returned, *ring = lax.optimization_barrier((returned, *ring))
-    gathered = call(
-        lookup_kernel,
-        shape((offsets * out_width, own_rows), BF16),
-        scratch=(pltpu.VMEM((out_width, targets), BF16), pltpu.VMEM((2, targets, STEP * LANES), BF16)),
-    )(turned, returned.reshape(send_rows, out_width), table)
-    group_g = lax.all_to_all(gathered.reshape(group, columns, own_rows), GROUP, 0, 0, tiled=True)
-
-    input_grad = call(
-        input_grad_kernel,
-        shape((own_rows, in_width), BF16),
-        scratch=weights,
-        in_specs=[hbm, vmem],
-        flops=10**9,
-    )(weight, gathered)
+        in_specs=[vmem, hbm, vmem, hbm],
+    )(x, weight, table, gathered)
 
     near = jnp.stack([x] + ring)
     far = lax.ppermute(near, "core", swap)

time: 103 us -> 102 us (level)
  Pallas kernels: 18.9 us -> 16.1 us
  starting transfers between devices: 39.2 us -> 40.4 us
    pallas_call x1 -> x0, Pallas kernels: 3.35 us -> none  [local(): call(input_grad_kernel, shape((own_rows, in_width), BF16), scratch=weight...]
    all_to_all x1, waiting for transfers between devices: 0.01 us -> 3.12 us  [local(): sums = lax.all_to_all(quarter, 'scene', 0, 0, tiled=True)]
    ppermute x3, waiting for transfers between devices: 2.41 us -> 0.35 us  [local(): lax.ppermute(own_x, 'scene', [(i, (i + d) % scenes) for i in range(scenes)])]
    ppermute x3, starting transfers between devices: 9.33 us -> 10.5 us  [local(): lax.ppermute(own_x, 'scene', [(i, (i + d) % scenes) for i in range(scenes)])]
    pallas_call x1, Pallas kernels: 4.38 us -> 3.2 us  [local(): call(lookup_kernel, shape((offsets * out_width, own_rows), BF16), scratch...]
    all_to_all x1, waiting for transfers between devices: 3.82 us -> 2.75 us  [local(): lax.all_to_all(gathered.reshape(group, columns, own_rows), GROUP, 0, 0, t...]
    pallas_call x1, Pallas kernels: 5.95 us -> 7.01 us  [local(): call(functools.partial(forward_kernel, free=free), (shape((own_rows, out_...]
  transfers between devices with their start and end apart: 7 -> 7, of which waited for: 3 -> 4; matrix products, arithmetic and copies ran while one was open for 1% -> 1% of each run, Pallas kernels for 11% -> 9%
where the time goes in v6:
time: 102 us; the launch traced here: 99.9 us
  starting transfers between devices  40.4 us (40%)
  blocking collectives  31.4 us (31%)
  Pallas kernels  16.1 us (16%)
  waiting for transfers between devices  7.44 us (7%)
  local copies, waits for them, and re-layouts  3.73 us (4%)
    all_to_all x1, blocking collectives, local(): lax.all_to_all(packed.reshape(peers, WORDS, LANES), SPACE, 0, 0, tiled=True)  31.4 us
    all_to_all x1, starting transfers between devices, local(): lax.all_to_all(outgoing.reshape(peers, slots, out_width), SPACE, 0, 0, ti...  18.6 us
    ppermute x3, starting transfers between devices, local(): lax.ppermute(own_x, 'scene', [(i, (i + d) % scenes) for i in range(scenes)])  10.5 us
    pallas_call x1, Pallas kernels, local(): call(functools.partial(forward_kernel, free=free), (shape((own_rows, out_...  7.01 us
    all_to_all x1, starting transfers between devices, local(): lax.all_to_all(gathered.reshape(group, columns, own_rows), GROUP, 0, 0, t...  6.1 us
    unnamed x17, local copies, waits for them, and re-layouts  3.6 us
    all_to_all x1, starting transfers between devices, local(): sums = lax.all_to_all(quarter, 'scene', 0, 0, tiled=True)  3.26 us
    pallas_call x1, Pallas kernels, local(): call(lookup_kernel, shape((offsets * out_width, own_rows), BF16), scratch...  3.2 us
  transfers between devices with their start and end apart: 7, of which 4 were waited for; matrix products, arithmetic and copies ran while one was open for 1% of the time, Pallas kernels for 9%

profile of v6, /device:TPU:1, one launch (start us, length us, event | category | flops | bytes accessed | tf_op | source)
XLA Modules:
  0.0 99.9 jit_solution(13080370984942321045)
XLA Ops:
  0.6 2.5 %shard_map.94 = (bf16[128,128]{1,0:T(8,128)(2,1)}, bf16[1024,128]{1,0:T(8,128)(2,1)}) custom-call(bf16[128,128]{1,0:T(8,128)(2,1)} %bitcast.48, s32[128,128]{1,0:T(8,128)} %bitcast.46, s32[8,128]{1,0:T(8,128)} %bitcast.34), custom_call_target="tpu_custom_call" | custom-call | flops 33554432 | bytes 393216 | tf_op jit(solution)/shard_map/pallas_call | solution.py:304
  3.1 0.0 copy-start.1
  3.1 18.6 %all-to-all-start = ((bf16[128,8,128]{2,1,0:T(8,128)(2,1)}), bf16[128,8,128]{2,1,0:T(8,128)(2,1)S(1)}, u32[]{:S(2)}, u32[]{:S(2)}) async-start(bf16[128,8,128]{2,1,0:T(8,128)(2,1)} %bitcast.36), calls=%async_computation | async-start | bytes 524288 | tf_op jit(solution)/shard_map/all_to_all | solution.py:322
  21.7 3.1 %collective-permute-start = (bf16[128,256]{1,0:T(8,128)(2,1)}, bf16[128,256]{1,0:T(8,128)(2,1)S(1)}, u32[]{:S(2)}, u32[]{:S(2)}) collective-permute-start(bf16[128,256]{1,0:T(8,128)(2,1)} %bitcast.30), channel_id=1, source_target_pairs={{0,1},{1,2},{2,3},{3,0},{4,5},{5,6},{6,7},{7,4},{8,9},{9,10},{10,1... | collective-permute-start | bytes 196616 | tf_op jit(solution)/shard_map/ppermute | solution.py:326
  24.8 4.4 %collective-permute-start.1 = (bf16[128,256]{1,0:T(8,128)(2,1)}, bf16[128,256]{1,0:T(8,128)(2,1)S(1)}, u32[]{:S(2)}, u32[]{:S(2)}) collective-permute-start(bf16[128,256]{1,0:T(8,128)(2,1)} %bitcast.31), channel_id=1, source_target_pairs={{0,2},{1,3},{2,0},{3,1},{4,6},{5,7},{6,4},{7,5},{8,10},{9,11},{10,... | collective-permute-start | bytes 196616 | tf_op jit(solution)/shard_map/ppermute | solution.py:326
  29.2 3.1 %collective-permute-start.2 = (bf16[128,256]{1,0:T(8,128)(2,1)}, bf16[128,256]{1,0:T(8,128)(2,1)S(1)}, u32[]{:S(2)}, u32[]{:S(2)}) collective-permute-start(bf16[128,256]{1,0:T(8,128)(2,1)} %bitcast.32), channel_id=1, source_target_pairs={{0,3},{1,0},{2,1},{3,2},{4,7},{5,4},{6,5},{7,6},{8,11},{9,8},{10,9... | collective-permute-start | bytes 196616 | tf_op jit(solution)/shard_map/ppermute | solution.py:326
  32.3 0.7 copy_bitcast_fusion.1
  33.0 0.0 copy-start.5
  33.0 0.8 copy-done.5
  33.8 0.0 copy-start
  33.8 0.6 shard_map.95
  34.4 0.0 collective-permute-done
  34.4 0.0 collective-permute-done.1
  34.4 0.3 collective-permute-done.2
  34.7 1.2 %all-to-all-done = bf16[128,8,128]{2,1,0:T(8,128)(2,1)S(1)} async-done(((bf16[128,8,128]{2,1,0:T(8,128)(2,1)}), bf16[128,8,128]{2,1,0:T(8,128)(2,1)S(1)}, u32[]{:S(2)}, u32[]{:S(2)}) %all-to-all-start) | async-done | bytes 262176 | tf_op jit(solution)/shard_map/all_to_all | solution.py:322
  35.9 3.2 %shard_map.96.gathered_any = bf16[3456,128]{1,0:T(8,128)(2,1)} custom-call(bf16[128,128]{1,0:T(8,128)(2,1)S(1)} %get-tuple-element.18.turned_ref, bf16[1024,128]{1,0:T(8,128)(2,1)S(1)} %bitcast.29, s32[27,128]{1,0:T(8,128)S(1)} %get-tuple-element.17.table_ref), custom_call_target="tpu_custom_call" | custom-call | tf_op jit(solution)/shard_map/pallas_call | solution.py:336
  39.1 6.1 %all-to-all-start.1 = ((bf16[8,432,128]{2,1,0:T(8,128)(2,1)}), bf16[8,432,128]{2,1,0:T(8,128)(2,1)S(1)}, u32[]{:S(2)}, u32[]{:S(2)}) async-start(bf16[8,432,128]{2,1,0:T(8,128)(2,1)} %bitcast.6), calls=%async_computation.1 | async-start | bytes 1769472 | tf_op jit(solution)/shard_map/all_to_all | solution.py:347
  45.2 0.0 copy-done.1
  45.3 1.9 %collective-permute-start.3 = (bf16[4,128,256]{2,1,0:T(8,128)(2,1)S(1)}, bf16[4,128,256]{2,1,0:T(8,128)(2,1)S(1)}, u32[]{:S(2)}, u32[]{:S(2)}) collective-permute-start(bf16[4,128,256]{2,1,0:T(8,128)(2,1)S(1)} %pad_maximum_fusion.near_ref), channel_id=1, source_target_pairs={{0,4},{4,0},{1,5},{5,1},{2,6},{6,2},{3,7},{7,3},{8,12},{12,8},{9,1... | collective-permute-start | bytes 786440 | tf_op jit(solution)/shard_map/ppermute | solution.py:368
  47.2 0.0 copy-done
  47.2 0.0 copy-start.2
  47.2 0.8 copy-done.2
  48.1 7.0 %shard_map.97 = (f32[128,128]{1,0:T(8,128)S(1)}, s32[5,128,128]{2,1,0:T(8,128)S(1)}, bf16[128,256]{1,0:T(8,128)(2,1)}) custom-call(bf16[128,256]{1,0:T(8,128)(2,1)S(1)} %bitcast.33, bf16[27,256,128]{2,1,0:T(8,128)(2,1)S(1)} %copy-done, s32[27,128]{1,0:T(8,128)S(1)} %get-tuple-element.17.table_ref, bf16[3456,128]{1,0:T(8,128)(2,1)} %shard_map.96.gathered_any), custom_call_target="tpu_custom_call" | custom-call | tf_op jit(solution)/shard_map/pallas_call | solution.py:349
  55.1 0.0 copy-start.3
  55.1 0.6 copy-done.3
  55.7 0.0 collective-permute-done.3.far_ref
  55.7 2.8 %all-to-all-done.1.g_ref = bf16[8,432,128]{2,1,0:T(8,128)(2,1)S(1)} async-done(((bf16[8,432,128]{2,1,0:T(8,128)(2,1)}), bf16[8,432,128]{2,1,0:T(8,128)(2,1)S(1)}, u32[]{:S(2)}, u32[]{:S(2)}) %all-to-all-start.1) | async-done | bytes 884768 | tf_op jit(solution)/shard_map/all_to_all | solution.py:347
  58.5 0.0 copy-start.4
  58.5 0.0 copy-start.6
  58.5 0.9 shard_map.98
  59.4 31.4 %all_to_all.20 = s32[128,8,128]{2,1,0:T(8,128)S(1)} all-to-all(s32[128,8,128]{2,1,0:T(8,128)S(1)} %bitcast.28), channel_id=1, replica_groups=mesh['y'=8,'z'=8,'core'=2,'scene'=4] {'y','z','core'}, dimensions={0} | all-to-all | bytes 1048576 | tf_op jit(solution)/shard_map/all_to_all | solution.py:376
  90.8 0.7 shard_map.100
  91.6 3.3 %all-to-all-start.3 = ((f32[4,16,128]{2,1,0:T(8,128)}), f32[4,16,128]{2,1,0:T(8,128)S(1)}, u32[]{:S(2)}, u32[]{:S(2)}) async-start(f32[4,16,128]{2,1,0:T(8,128)} %shard_map.100), calls=%async_computation.3 | async-start | bytes 65536 | tf_op jit(solution)/shard_map/all_to_all | solution.py:384
  94.8 0.0 copy-done.4
  94.8 0.0 copy-done.6
  94.9 1.1 %shard_map.99 = bf16[128,128]{1,0:T(8,128)(2,1)} custom-call(f32[128,128]{1,0:T(8,128)S(1)} %copy-done.4, s32[1024,128]{1,0:T(8,128)S(1)} %bitcast.27, s32[8,128]{1,0:T(8,128)S(1)} %bitcast.35), custom_call_target="tpu_custom_call" | custom-call | flops 67108864 | bytes 524288 | tf_op jit(solution)/shard_map/pallas_call | solution.py:385
  96.0 3.1 %all-to-all-done.3 = f32[4,16,128]{2,1,0:T(8,128)S(1)} async-done(((f32[4,16,128]{2,1,0:T(8,128)}), f32[4,16,128]{2,1,0:T(8,128)S(1)}, u32[]{:S(2)}, u32[]{:S(2)}) %all-to-all-start.3) | async-done | bytes 32800 | tf_op jit(solution)/shard_map/all_to_all | solution.py:384
  99.1 0.1 mul.17
  99.3 0.6 copy.15
  (6 shorter events, 0.1 us)
Async XLA Ops:
  3.1 42.1 %copy-start.1 = (bf16[1,128,256]{2,1,0:T(8,128)(2,1)S(1)}, bf16[1,128,256]{2,1,0:T(8,128)(2,1)}, u32[]{:S(2)}) copy-start(bf16[1,128,256]{2,1,0:T(8,128)(2,1)} %param.7) | copy-start | bytes 196612
  3.1 32.8 %all-to-all-start = ((bf16[128,8,128]{2,1,0:T(8,128)(2,1)}), bf16[128,8,128]{2,1,0:T(8,128)(2,1)S(1)}, u32[]{:S(2)}, u32[]{:S(2)}) async-start(bf16[128,8,128]{2,1,0:T(8,128)(2,1)} %bitcast.36), calls=%async_computation | async-start | bytes 524288 | tf_op jit(solution)/shard_map/all_to_all | solution.py:322
  21.7 12.7 %collective-permute-start = (bf16[128,256]{1,0:T(8,128)(2,1)}, bf16[128,256]{1,0:T(8,128)(2,1)S(1)}, u32[]{:S(2)}, u32[]{:S(2)}) collective-permute-start(bf16[128,256]{1,0:T(8,128)(2,1)} %bitcast.30), channel_id=1, source_target_pairs={{0,1},{1,2},{2,3},{3,0},{4,5},{5,6},{6,7},{7,4},{8,9},{9,10},{10,1... | collective-permute-start | bytes 196616 | tf_op jit(solution)/shard_map/ppermute | solution.py:326
  24.8 9.5 %collective-permute-start.1 = (bf16[128,256]{1,0:T(8,128)(2,1)}, bf16[128,256]{1,0:T(8,128)(2,1)S(1)}, u32[]{:S(2)}, u32[]{:S(2)}) collective-permute-start(bf16[128,256]{1,0:T(8,128)(2,1)} %bitcast.31), channel_id=1, source_target_pairs={{0,2},{1,3},{2,0},{3,1},{4,6},{5,7},{6,4},{7,5},{8,10},{9,11},{10,... | collective-permute-start | bytes 196616 | tf_op jit(solution)/shard_map/ppermute | solution.py:326
  29.2 5.5 %collective-permute-start.2 = (bf16[128,256]{1,0:T(8,128)(2,1)}, bf16[128,256]{1,0:T(8,128)(2,1)S(1)}, u32[]{:S(2)}, u32[]{:S(2)}) collective-permute-start(bf16[128,256]{1,0:T(8,128)(2,1)} %bitcast.32), channel_id=1, source_target_pairs={{0,3},{1,0},{2,1},{3,2},{4,7},{5,4},{6,5},{7,6},{8,11},{9,8},{10,9... | collective-permute-start | bytes 196616 | tf_op jit(solution)/shard_map/ppermute | solution.py:326
  33.0 0.8 copy-start.5
  33.8 13.4 %copy-start = (bf16[27,256,128]{2,1,0:T(8,128)(2,1)S(1)}, bf16[27,256,128]{2,1,0:T(8,128)(2,1)}, u32[]{:S(2)}) copy-start(bf16[27,256,128]{2,1,0:T(8,128)(2,1)} %w_any.1) | copy-start | bytes 5308420
  39.1 19.3 %all-to-all-start.1 = ((bf16[8,432,128]{2,1,0:T(8,128)(2,1)}), bf16[8,432,128]{2,1,0:T(8,128)(2,1)S(1)}, u32[]{:S(2)}, u32[]{:S(2)}) async-start(bf16[8,432,128]{2,1,0:T(8,128)(2,1)} %bitcast.6), calls=%async_computation.1 | async-start | bytes 1769472 | tf_op jit(solution)/shard_map/all_to_all | solution.py:347
  45.3 10.4 %collective-permute-start.3 = (bf16[4,128,256]{2,1,0:T(8,128)(2,1)S(1)}, bf16[4,128,256]{2,1,0:T(8,128)(2,1)S(1)}, u32[]{:S(2)}, u32[]{:S(2)}) collective-permute-start(bf16[4,128,256]{2,1,0:T(8,128)(2,1)S(1)} %pad_maximum_fusion.near_ref), channel_id=1, source_target_pairs={{0,4},{4,0},{1,5},{5,1},{2,6},{6,2},{3,7},{7,3},{8,12},{12,8},{9,1... | collective-permute-start | bytes 786440 | tf_op jit(solution)/shard_map/ppermute | solution.py:368
  47.2 0.8 copy-start.2
  55.1 0.6 copy-start.3
  58.5 36.4 %copy-start.4 = (f32[128,128]{1,0:T(8,128)S(1)}, f32[128,128]{1,0:T(8,128)}, u32[]{:S(2)}) copy-start(f32[128,128]{1,0:T(8,128)} %copy-done.3) | copy-start | bytes 196612
  58.5 36.4 %copy-start.6 = (s32[1,1,1024]{2,1,0:T(1,128)S(1)}, s32[1,1,1024]{2,1,0:T(1,128)}, u32[]{:S(2)}) copy-start(s32[1,1,1024]{2,1,0:T(1,128)} %param.13) | copy-start | bytes 12292
  91.6 7.5 %all-to-all-start.3 = ((f32[4,16,128]{2,1,0:T(8,128)}), f32[4,16,128]{2,1,0:T(8,128)S(1)}, u32[]{:S(2)}, u32[]{:S(2)}) async-start(f32[4,16,128]{2,1,0:T(8,128)} %shard_map.100), calls=%async_computation.3 | async-start | bytes 65536 | tf_op jit(solution)/shard_map/all_to_all | solution.py:384

commit v7 on v6

--- a/solution.py
+++ b/solution.py
@@ -57,7 +57,7 @@
     return slice(k * LANES, (k + 1) * LANES)
 
 
-def gather_kernel(cot_any, mask_any, recv_any, up_ref, out_any, cot_ref, mask_ref, recv_ref, out_ref, sems, out_sems):
+def gather_kernel(cot_any, mask_any, recv_any, up_ref, out_ref, cot_ref, mask_ref, recv_ref, sems):
     pairs = ((cot_any, cot_ref), (mask_any, mask_ref), (recv_any, recv_ref))
     copies = [pltpu.make_async_copy(a, b, sems.at[i]) for i, (a, b) in enumerate(pairs)]
     for copy in copies:
@@ -67,16 +67,10 @@
     up = (cot_ref[...].astype(F32) * mask_ref[...].astype(F32)).astype(BF16)
     up_ref[...] = up
     iota = rows_iota(LANES)
-    copies = []
     for g in range(recv_ref.shape[0]):
         hot = one_hot(iota, recv_ref[g : g + 1, :])
         rows = lax.dot_general(hot, up, (((0,), (0,)), ((), ())), preferred_element_type=F32)
         out_ref[lane_block(g), :] = rows.astype(BF16)
-        part = pl.ds(g * LANES, LANES)
-        copies.append(pltpu.make_async_copy(out_ref.at[part], out_any.at[part], out_sems.at[g]))
-        copies[-1].start()
-    for copy in copies:
-        copy.wait()
 
 
 def table_kernel(in_ref, out_ref, up_ref, table_ref, turned_ref, *, targets):
@@ -163,11 +157,11 @@
 
 
 def forward_kernel(
-    x_ref,
+    near_ref,
     w_any,
     table_ref,
     gathered_any,
-    own_ref,
+    own_any,
     word_ref,
     grad_ref,
     w_ref,
@@ -176,6 +170,7 @@
     hot_ref,
     send_ref,
     sems,
+    own_sem,
     *,
     free,
 ):
@@ -186,38 +181,38 @@
         if k % step == 0:
             for copy in copies[k // step]:
                 copy.wait()
-        high, low = split_two(jnp.dot(x_ref[...], w_ref[k], preferred_element_type=F32))
+        high, low = split_two(jnp.dot(near_ref[0], w_ref[k], preferred_element_type=F32))
         terms_ref[lane_block(k), 0:LANES] = high
         terms_ref[lane_block(k), LANES : 2 * LANES] = low
         total += jnp.dot(w_ref[k], gathered_ref[lane_block(k), :], preferred_element_type=F32)
     grad_ref[...] = total.T.astype(BF16)
     iota = rows_iota(LANES).astype(jnp.int16)
 
-    def block(start):
-        for k in range(offsets):
-            hot_ref[:, lane_block(k)] = one_hot_16(iota, table_ref[k : k + 1, :] - start)
-        both = jnp.dot(hot_ref[...], terms_ref[...], preferred_element_type=F32)
-        return both[:, :LANES] + both[:, LANES:]
-
-    own_ref[...] = block(0)
-
-    def scatter(b, carry):
-        send_ref[pl.ds(pl.multiple_of(b * LANES, LANES), LANES), :] = block((b + 1) * LANES)
-        return carry
-
-    lax.fori_loop(0, send_ref.shape[0] // LANES, scatter, 0)
+    span = hot_ref.shape[1]
+    own_rows = own_any.shape[0]
+    own_copy = pltpu.make_async_copy(send_ref.at[pl.ds(0, own_rows)], own_any, own_sem)
+    for i in range(send_ref.shape[0] // span):
+        for j in range(span // LANES):
+            for k in range(offsets):
+                row = table_ref[k : k + 1, :] - (i * span + j * LANES)
+                hot_ref[i % 2, lane_block(j), lane_block(k)] = one_hot_16(iota, row)
+        both = jnp.dot(hot_ref[i % 2], terms_ref[...], preferred_element_type=F32)
+        send_ref[pl.ds(i * span, span), :] = both[:, :LANES] + both[:, LANES:]
+        if i == 0:
+            own_copy.start()
     peers = word_ref.shape[1]
     lane = lax.broadcasted_iota(I32, (peers, LANES), 1)
     levels = jnp.zeros((peers, LANES), I32)
     for r in range(4):
         words = []
         for slot in (r, r + 4):
-            value = send_ref[pl.ds(slot, peers, stride=8), :]
+            value = send_ref[pl.ds(own_rows + slot, peers, stride=8), :]
             code, level = encode(value, row_top(value))
             words.append(code)
             levels = jnp.where(lane == free + slot, level, levels)
         word_ref[r] = join(*words)
     word_ref[4] = levels
+    own_copy.wait()
 
 
 def pack_kernel(g_ref, near_ref, far_ref, word_ref, out_ref, turn_ref):
@@ -229,7 +224,7 @@
     total = jnp.zeros((columns, near_ref.shape[2]), F32)
     for s in range(g_ref.shape[0]):
         x_ref, holder = (near_ref, core) if s < scenes else (far_ref, 1 - core)
-        sender = holder * scenes + lax.rem(scene + scenes - s % scenes, scenes)
+        sender = holder * scenes + (scene ^ (s % scenes))
         total += jnp.dot(g_ref[sender], x_ref[s % scenes], preferred_element_type=F32)
     rest = blocks * LANES - columns
     total = jnp.concatenate([total, jnp.zeros((rest, total.shape[1]), F32)], axis=0)
@@ -308,12 +303,9 @@
             pltpu.VMEM((own_rows, out_width), BF16),
             pltpu.VMEM((own_rows, out_width), I32),
             pltpu.VMEM(recv.shape, I32),
-            pltpu.VMEM((send_rows, out_width), BF16),
             pltpu.SemaphoreType.DMA((3,)),
-            pltpu.SemaphoreType.DMA(recv.shape[:1]),
         ),
         in_specs=[hbm] * 3,
-        out_specs=(vmem, hbm),
         vmem=MOST_VMEM,
         flops=2 * send_rows * own_rows * out_width,
         moved=send_rows * out_width * 3,
@@ -322,17 +314,17 @@
     returned = lax.all_to_all(outgoing.reshape(peers, slots, out_width), SPACE, 0, 0, tiled=True)
 
     swap = [(0, 1), (1, 0)]
-    ring = [
-        lax.ppermute(own_x, "scene", [(i, (i + d) % scenes) for i in range(scenes)])
-        for d in range(1, scenes)
-    ]
+    one, two = ([(i, i ^ d) for i in range(scenes)] for d in (1, 2))
+    pair = jnp.stack([own_x, lax.ppermute(own_x, "scene", one)])
+    other = lax.ppermute(pair, "scene", two)
 
     table, turned = call(
         functools.partial(table_kernel, targets=targets),
         (shape((offsets, own_rows), I32), shape((out_width, own_rows), BF16)),
     )(pair_in[0, 0], pair_out[0, 0], upstream)
 
-    returned, *ring = lax.optimization_barrier((returned, *ring))
+    returned, pair, other = lax.optimization_barrier((returned, pair, other))
+    near = jnp.concatenate([pair, other])
     gathered = call(
         lookup_kernel,
         shape((offsets * out_width, own_rows), BF16),
@@ -357,14 +349,15 @@
             pltpu.VMEM(weight.shape, BF16),
             pltpu.VMEM((offsets * out_width, own_rows), BF16),
             pltpu.VMEM((offsets * own_rows, 2 * out_width), BF16),
-            pltpu.VMEM((LANES, offsets * own_rows), BF16),
-            pltpu.VMEM((send_rows, out_width), F32),
+            pltpu.VMEM((2, targets // 3, offsets * own_rows), BF16),
+            pltpu.VMEM((targets, out_width), F32),
             pltpu.SemaphoreType.DMA((2, 3)),
+            pltpu.SemaphoreType.DMA,
         ),
         in_specs=[vmem, hbm, vmem, hbm],
-    )(x, weight, table, gathered)
-
-    near = jnp.stack([x] + ring)
+        out_specs=(hbm, vmem, vmem),
+    )(near, weight, table, gathered)
+
     far = lax.ppermute(near, "core", swap)
     packed = call(
         pack_kernel,

time: 102 us -> 102 us (level)
  waiting for transfers between devices: 7.44 us -> 11.5 us
  starting transfers between devices: 40.4 us -> 38 us
  Pallas kernels: 16.1 us -> 14.2 us
  blocking collectives: 31.4 us -> 32.5 us
    ppermute x3 -> x2, waiting for transfers between devices: 0.35 us -> 3.16 us  [the longest x1 2.39 us: local(): pair = jnp.stack([own_x, lax.ppermute(own_x, 'scene', one)])]
    ppermute x3 -> x2, starting transfers between devices: 10.5 us -> 7.77 us  [the longest x1 4.65 us: local(): other = lax.ppermute(pair, 'scene', two)]
    all_to_all x1, waiting for transfers between devices: 2.75 us -> 4.85 us  [local(): lax.all_to_all(gathered.reshape(group, columns, own_rows), GROUP, 0, 0, t...]
    pallas_call x1, Pallas kernels: 7.01 us -> 5.78 us  [local(): call(functools.partial(forward_kernel, free=free), (shape((own_rows, out_...]
    all_to_all x1, blocking collectives: 31.4 us -> 32.5 us  [local(): lax.all_to_all(packed.reshape(peers, WORDS, LANES), SPACE, 0, 0, tiled=True)]
    unnamed x17 -> x14, local copies, waits for them, and re-layouts: 3.6 us -> 2.76 us
  transfers between devices with their start and end apart: 7 -> 6, of which waited for: 4 -> 5; matrix products, arithmetic and copies ran while one was open for 1% -> 2% of each run, Pallas kernels for 9% -> 7%
where the time goes in v7:
time: 102 us; the launch traced here: 101 us
  starting transfers between devices  38 us (37%)
  blocking collectives  32.5 us (32%)
  Pallas kernels  14.2 us (14%)
  waiting for transfers between devices  11.5 us (11%)
  local copies, waits for them, and re-layouts  2.9 us (3%)
    all_to_all x1, blocking collectives, local(): lax.all_to_all(packed.reshape(peers, WORDS, LANES), SPACE, 0, 0, tiled=True)  32.5 us
    all_to_all x1, starting transfers between devices, local(): lax.all_to_all(outgoing.reshape(peers, slots, out_width), SPACE, 0, 0, ti...  18.4 us
    all_to_all x1, starting transfers between devices, local(): lax.all_to_all(gathered.reshape(group, columns, own_rows), GROUP, 0, 0, t...  6.57 us
    pallas_call x1, Pallas kernels, local(): call(functools.partial(forward_kernel, free=free), (shape((own_rows, out_...  5.78 us
    all_to_all x1, waiting for transfers between devices, local(): lax.all_to_all(gathered.reshape(group, columns, own_rows), GROUP, 0, 0, t...  4.85 us
    ppermute x1, starting transfers between devices, local(): other = lax.ppermute(pair, 'scene', two)  4.65 us
    all_to_all x1, starting transfers between devices, local(): sums = lax.all_to_all(quarter, 'scene', 0, 0, tiled=True)  3.26 us
    pallas_call x1, Pallas kernels, local(): call(lookup_kernel, shape((offsets * out_width, own_rows), BF16), scratch...  3.2 us
  transfers between devices with their start and end apart: 6, of which 5 were waited for; matrix products, arithmetic and copies ran while one was open for 2% of the time, Pallas kernels for 7%

profile of v7, /device:TPU:1, one launch (start us, length us, event | category | flops | bytes accessed | tf_op | source)
XLA Modules:
  0.0 100.7 jit_solution(12949396966601815449)
XLA Ops:
  0.6 1.8 %shard_map.94 = (bf16[128,128]{1,0:T(8,128)(2,1)}, bf16[1024,128]{1,0:T(8,128)(2,1)}) custom-call(bf16[128,128]{1,0:T(8,128)(2,1)} %bitcast.42, s32[128,128]{1,0:T(8,128)} %bitcast.40, s32[8,128]{1,0:T(8,128)} %bitcast.29), custom_call_target="tpu_custom_call" | custom-call | flops 33554432 | bytes 393216 | tf_op jit(solution)/shard_map/pallas_call | solution.py:299
  2.5 18.4 %all-to-all-start = ((bf16[128,8,128]{2,1,0:T(8,128)(2,1)}), bf16[128,8,128]{2,1,0:T(8,128)(2,1)S(1)}, u32[]{:S(2)}, u32[]{:S(2)}) async-start(bf16[128,8,128]{2,1,0:T(8,128)(2,1)} %bitcast.31), calls=%async_computation | async-start | bytes 524288 | tf_op jit(solution)/shard_map/all_to_all | solution.py:314
  20.9 3.1 %collective-permute-start = (bf16[128,256]{1,0:T(8,128)(2,1)}, bf16[128,256]{1,0:T(8,128)(2,1)S(1)}, u32[]{:S(2)}, u32[]{:S(2)}) collective-permute-start(bf16[128,256]{1,0:T(8,128)(2,1)} %bitcast.36), channel_id=1, source_target_pairs={{0,1},{1,0},{2,3},{3,2},{4,5},{5,4},{6,7},{7,6},{8,9},{9,8},{10,11... | collective-permute-start | bytes 196616 | tf_op jit(solution)/shard_map/ppermute | solution.py:318
  24.1 2.4 %collective-permute-done = bf16[128,256]{1,0:T(8,128)(2,1)S(1)} collective-permute-done((bf16[128,256]{1,0:T(8,128)(2,1)}, bf16[128,256]{1,0:T(8,128)(2,1)S(1)}, u32[]{:S(2)}, u32[]{:S(2)}) %collective-permute-start) | collective-permute-done | bytes 65568 | tf_op jit(solution)/shard_map/ppermute | solution.py:318
  26.4 0.9 pad_maximum_fusion
  27.3 4.6 %collective-permute-start.1 = (bf16[2,128,256]{2,1,0:T(8,128)(2,1)S(1)}, bf16[2,128,256]{2,1,0:T(8,128)(2,1)S(1)}, u32[]{:S(2)}, u32[]{:S(2)}) collective-permute-start(bf16[2,128,256]{2,1,0:T(8,128)(2,1)S(1)} %pad_maximum_fusion), channel_id=1, source_target_pairs={{0,2},{1,3},{2,0},{3,1},{4,6},{5,7},{6,4},{7,5},{8,10},{9,11},{10,... | collective-permute-start | bytes 393224 | tf_op jit(solution)/shard_map/ppermute | solution.py:319
  32.0 0.7 copy_bitcast_fusion.1
  32.7 0.0 copy-start.3
  32.7 0.8 copy-done.3
  33.4 0.0 copy-start
  33.4 0.6 shard_map.95
  34.0 0.8 collective-permute-done.1
  34.8 0.3 all-to-all-done
  35.2 3.2 %shard_map.96.gathered_any = bf16[3456,128]{1,0:T(8,128)(2,1)} custom-call(bf16[128,128]{1,0:T(8,128)(2,1)S(1)} %get-tuple-element.22.turned_ref, bf16[1024,128]{1,0:T(8,128)(2,1)S(1)} %bitcast.28, s32[27,128]{1,0:T(8,128)S(1)} %get-tuple-element.21.table_ref), custom_call_target="tpu_custom_call" | custom-call | tf_op jit(solution)/shard_map/pallas_call | solution.py:328
  38.4 6.6 %all-to-all-start.1 = ((bf16[8,432,128]{2,1,0:T(8,128)(2,1)}), bf16[8,432,128]{2,1,0:T(8,128)(2,1)S(1)}, u32[]{:S(2)}, u32[]{:S(2)}) async-start(bf16[8,432,128]{2,1,0:T(8,128)(2,1)} %bitcast.8), calls=%async_computation.1 | async-start | bytes 1769472 | tf_op jit(solution)/shard_map/all_to_all | solution.py:339
  45.0 1.9 %collective-permute-start.2 = (bf16[4,128,256]{2,1,0:T(8,128)(2,1)S(1)}, bf16[4,128,256]{2,1,0:T(8,128)(2,1)S(1)}, u32[]{:S(2)}, u32[]{:S(2)}) collective-permute-start(bf16[4,128,256]{2,1,0:T(8,128)(2,1)S(1)} %constant_dynamic-update-slice_fusion.near_ref), channel_id=1, source_target_pairs={{0,4},{4,0},{1,5},{5,1},{2,6},{6,2},{3,7},{7,3},{8,12},{12,8},{9,1... | collective-permute-start | bytes 786440 | tf_op jit(solution)/shard_map/ppermute | solution.py:361
  46.9 0.0 copy-done
  46.9 5.8 %shard_map.97 = (f32[128,128]{1,0:T(8,128)S(1)}, s32[5,128,128]{2,1,0:T(8,128)S(1)}, bf16[128,256]{1,0:T(8,128)(2,1)}) custom-call(bf16[4,128,256]{2,1,0:T(8,128)(2,1)S(1)} %constant_dynamic-update-slice_fusion.near_ref, bf16[27,256,128]{2,1,0:T(8,128)(2,1)S(1)} %copy-done, s32[27,128]{1,0:T(8,128)S(1)} %get-tuple-element.21.table_ref, ...), custom_call_target="tpu_custom_call" | custom-call | tf_op jit(solution)/shard_map/pallas_call | solution.py:341
  52.7 0.0 copy-start.1
  52.7 0.6 copy-done.1
  53.3 0.0 collective-permute-done.2.far_ref
  53.3 4.9 %all-to-all-done.1.g_ref = bf16[8,432,128]{2,1,0:T(8,128)(2,1)S(1)} async-done(((bf16[8,432,128]{2,1,0:T(8,128)(2,1)}), bf16[8,432,128]{2,1,0:T(8,128)(2,1)S(1)}, u32[]{:S(2)}, u32[]{:S(2)}) %all-to-all-start.1) | async-done | bytes 884768 | tf_op jit(solution)/shard_map/all_to_all | solution.py:339
  58.2 0.0 copy-start.2
  58.2 0.0 copy-start.4
  58.2 0.9 shard_map.98
  59.1 32.5 %all_to_all.20 = s32[128,8,128]{2,1,0:T(8,128)S(1)} all-to-all(s32[128,8,128]{2,1,0:T(8,128)S(1)} %bitcast.27), channel_id=1, replica_groups=mesh['y'=8,'z'=8,'core'=2,'scene'=4] {'y','z','core'}, dimensions={0} | all-to-all | bytes 1048576 | tf_op jit(solution)/shard_map/all_to_all | solution.py:369
  91.6 0.7 shard_map.100
  92.3 3.3 %all-to-all-start.3 = ((f32[4,16,128]{2,1,0:T(8,128)}), f32[4,16,128]{2,1,0:T(8,128)S(1)}, u32[]{:S(2)}, u32[]{:S(2)}) async-start(f32[4,16,128]{2,1,0:T(8,128)} %shard_map.100), calls=%async_computation.3 | async-start | bytes 65536 | tf_op jit(solution)/shard_map/all_to_all | solution.py:377
  95.6 0.0 copy-done.2
  95.6 0.0 copy-done.4
  95.6 1.1 %shard_map.99 = bf16[128,128]{1,0:T(8,128)(2,1)} custom-call(f32[128,128]{1,0:T(8,128)S(1)} %copy-done.2, s32[1024,128]{1,0:T(8,128)S(1)} %bitcast.26, s32[8,128]{1,0:T(8,128)S(1)} %bitcast.30), custom_call_target="tpu_custom_call" | custom-call | flops 67108864 | bytes 524288 | tf_op jit(solution)/shard_map/pallas_call | solution.py:378
  96.7 3.1 %all-to-all-done.3 = f32[4,16,128]{2,1,0:T(8,128)S(1)} async-done(((f32[4,16,128]{2,1,0:T(8,128)}), f32[4,16,128]{2,1,0:T(8,128)S(1)}, u32[]{:S(2)}, u32[]{:S(2)}) %all-to-all-start.3) | async-done | bytes 32800 | tf_op jit(solution)/shard_map/all_to_all | solution.py:377
  99.9 0.1 mul.17
  100.0 0.6 copy.15
  (7 shorter events, 0.1 us)
Async XLA Ops:
  2.5 32.7 %all-to-all-start = ((bf16[128,8,128]{2,1,0:T(8,128)(2,1)}), bf16[128,8,128]{2,1,0:T(8,128)(2,1)S(1)}, u32[]{:S(2)}, u32[]{:S(2)}) async-start(bf16[128,8,128]{2,1,0:T(8,128)(2,1)} %bitcast.31), calls=%async_computation | async-start | bytes 524288 | tf_op jit(solution)/shard_map/all_to_all | solution.py:314
  20.9 5.5 %collective-permute-start = (bf16[128,256]{1,0:T(8,128)(2,1)}, bf16[128,256]{1,0:T(8,128)(2,1)S(1)}, u32[]{:S(2)}, u32[]{:S(2)}) collective-permute-start(bf16[128,256]{1,0:T(8,128)(2,1)} %bitcast.36), channel_id=1, source_target_pairs={{0,1},{1,0},{2,3},{3,2},{4,5},{5,4},{6,7},{7,6},{8,9},{9,8},{10,11... | collective-permute-start | bytes 196616 | tf_op jit(solution)/shard_map/ppermute | solution.py:318
  27.3 7.5 %collective-permute-start.1 = (bf16[2,128,256]{2,1,0:T(8,128)(2,1)S(1)}, bf16[2,128,256]{2,1,0:T(8,128)(2,1)S(1)}, u32[]{:S(2)}, u32[]{:S(2)}) collective-permute-start(bf16[2,128,256]{2,1,0:T(8,128)(2,1)S(1)} %pad_maximum_fusion), channel_id=1, source_target_pairs={{0,2},{1,3},{2,0},{3,1},{4,6},{5,7},{6,4},{7,5},{8,10},{9,11},{10,... | collective-permute-start | bytes 393224 | tf_op jit(solution)/shard_map/ppermute | solution.py:319
  32.7 0.8 copy-start.3
  33.4 13.4 %copy-start = (bf16[27,256,128]{2,1,0:T(8,128)(2,1)S(1)}, bf16[27,256,128]{2,1,0:T(8,128)(2,1)}, u32[]{:S(2)}) copy-start(bf16[27,256,128]{2,1,0:T(8,128)(2,1)} %w_any.1) | copy-start | bytes 5308420
  38.4 19.8 %all-to-all-start.1 = ((bf16[8,432,128]{2,1,0:T(8,128)(2,1)}), bf16[8,432,128]{2,1,0:T(8,128)(2,1)S(1)}, u32[]{:S(2)}, u32[]{:S(2)}) async-start(bf16[8,432,128]{2,1,0:T(8,128)(2,1)} %bitcast.8), calls=%async_computation.1 | async-start | bytes 1769472 | tf_op jit(solution)/shard_map/all_to_all | solution.py:339
  45.0 8.3 %collective-permute-start.2 = (bf16[4,128,256]{2,1,0:T(8,128)(2,1)S(1)}, bf16[4,128,256]{2,1,0:T(8,128)(2,1)S(1)}, u32[]{:S(2)}, u32[]{:S(2)}) collective-permute-start(bf16[4,128,256]{2,1,0:T(8,128)(2,1)S(1)} %constant_dynamic-update-slice_fusion.near_ref), channel_id=1, source_target_pairs={{0,4},{4,0},{1,5},{5,1},{2,6},{6,2},{3,7},{7,3},{8,12},{12,8},{9,1... | collective-permute-start | bytes 786440 | tf_op jit(solution)/shard_map/ppermute | solution.py:361
  52.7 0.6 copy-start.1
  58.2 37.4 %copy-start.2 = (f32[128,128]{1,0:T(8,128)S(1)}, f32[128,128]{1,0:T(8,128)}, u32[]{:S(2)}) copy-start(f32[128,128]{1,0:T(8,128)} %copy-done.1) | copy-start | bytes 196612
  58.2 37.4 %copy-start.4 = (s32[1,1,1024]{2,1,0:T(1,128)S(1)}, s32[1,1,1024]{2,1,0:T(1,128)}, u32[]{:S(2)}) copy-start(s32[1,1,1024]{2,1,0:T(1,128)} %param.13) | copy-start | bytes 12292
  92.3 7.5 %all-to-all-start.3 = ((f32[4,16,128]{2,1,0:T(8,128)}), f32[4,16,128]{2,1,0:T(8,128)S(1)}, u32[]{:S(2)}, u32[]{:S(2)}) async-start(f32[4,16,128]{2,1,0:T(8,128)} %shard_map.100), calls=%async_computation.3 | async-start | bytes 65536 | tf_op jit(solution)/shard_map/all_to_all | solution.py:377

commit v8 on v7

--- a/solution.py
+++ b/solution.py
@@ -314,17 +314,16 @@
     returned = lax.all_to_all(outgoing.reshape(peers, slots, out_width), SPACE, 0, 0, tiled=True)
 
     swap = [(0, 1), (1, 0)]
-    one, two = ([(i, i ^ d) for i in range(scenes)] for d in (1, 2))
-    pair = jnp.stack([own_x, lax.ppermute(own_x, "scene", one)])
-    other = lax.ppermute(pair, "scene", two)
+    ring = [
+        lax.ppermute(own_x, "scene", [(i, i ^ d) for i in range(scenes)]) for d in range(1, scenes)
+    ]
 
     table, turned = call(
         functools.partial(table_kernel, targets=targets),
         (shape((offsets, own_rows), I32), shape((out_width, own_rows), BF16)),
     )(pair_in[0, 0], pair_out[0, 0], upstream)
 
-    returned, pair, other = lax.optimization_barrier((returned, pair, other))
-    near = jnp.concatenate([pair, other])
+    returned, *ring = lax.optimization_barrier((returned, *ring))
     gathered = call(
         lookup_kernel,
         shape((offsets * out_width, own_rows), BF16),
@@ -338,6 +337,7 @@
     )(turned, returned.reshape(send_rows, out_width), table)
     group_g = lax.all_to_all(gathered.reshape(group, columns, own_rows), GROUP, 0, 0, tiled=True)
 
+    near = jnp.stack([x] + ring)
     own, words, input_grad = call(
         functools.partial(forward_kernel, free=free),
         (

time: 102 us -> 102 us (level)
  starting transfers between devices: 38 us -> 39.4 us
    ppermute x2 -> x3, starting transfers between devices: 7.77 us -> 9.59 us  [local(): lax.ppermute(own_x, 'scene', [(i, i ^ d) for i in range(scenes)])]
    ppermute x2 -> x3, waiting for transfers between devices: 3.16 us -> 2.52 us  [local(): lax.ppermute(own_x, 'scene', [(i, i ^ d) for i in range(scenes)])]
    unnamed x14 -> x15, local copies, waits for them, and re-layouts: 2.76 us -> 2.75 us
  transfers between devices with their start and end apart: 6 -> 7, of which waited for: 5 -> 3; matrix products, arithmetic and copies ran while one was open for 2% -> 1% of each run, Pallas kernels for 7% -> 7%
where the time goes in v8:
time: 102 us; the launch traced here: 100 us
  starting transfers between devices  39.4 us (39%)
  blocking collectives  32.2 us (32%)
  Pallas kernels  14.2 us (14%)
  waiting for transfers between devices  10.5 us (10%)
  local copies, waits for them, and re-layouts  2.88 us (3%)
    all_to_all x1, blocking collectives, local(): lax.all_to_all(packed.reshape(peers, WORDS, LANES), SPACE, 0, 0, tiled=True)  32.2 us
    all_to_all x1, starting transfers between devices, local(): lax.all_to_all(outgoing.reshape(peers, slots, out_width), SPACE, 0, 0, ti...  18.6 us
    ppermute x3, starting transfers between devices, local(): lax.ppermute(own_x, 'scene', [(i, i ^ d) for i in range(scenes)])  9.59 us
    all_to_all x1, starting transfers between devices, local(): lax.all_to_all(gathered.reshape(group, columns, own_rows), GROUP, 0, 0, t...  6.09 us
    pallas_call x1, Pallas kernels, local(): call(functools.partial(forward_kernel, free=free), (shape((own_rows, out_...  5.78 us
    all_to_all x1, waiting for transfers between devices, local(): lax.all_to_all(gathered.reshape(group, columns, own_rows), GROUP, 0, 0, t...  4.85 us
    all_to_all x1, starting transfers between devices, local(): sums = lax.all_to_all(quarter, 'scene', 0, 0, tiled=True)  3.26 us
    pallas_call x1, Pallas kernels, local(): call(lookup_kernel, shape((offsets * out_width, own_rows), BF16), scratch...  3.2 us
  transfers between devices with their start and end apart: 7, of which 3 were waited for; matrix products, arithmetic and copies ran while one was open for 1% of the time, Pallas kernels for 7%

profile of v8, /device:TPU:1, one launch (start us, length us, event | category | flops | bytes accessed | tf_op | source)
XLA Modules:
  0.0 100.0 jit_solution(7043605766177038853)
XLA Ops:
  0.6 1.8 %shard_map.94 = (bf16[128,128]{1,0:T(8,128)(2,1)}, bf16[1024,128]{1,0:T(8,128)(2,1)}) custom-call(bf16[128,128]{1,0:T(8,128)(2,1)} %bitcast.47, s32[128,128]{1,0:T(8,128)} %bitcast.45, s32[8,128]{1,0:T(8,128)} %bitcast.30), custom_call_target="tpu_custom_call" | custom-call | flops 33554432 | bytes 393216 | tf_op jit(solution)/shard_map/pallas_call | solution.py:299
  2.5 0.0 copy-start.5
  2.5 18.6 %all-to-all-start = ((bf16[128,8,128]{2,1,0:T(8,128)(2,1)}), bf16[128,8,128]{2,1,0:T(8,128)(2,1)S(1)}, u32[]{:S(2)}, u32[]{:S(2)}) async-start(bf16[128,8,128]{2,1,0:T(8,128)(2,1)} %bitcast.32), calls=%async_computation | async-start | bytes 524288 | tf_op jit(solution)/shard_map/all_to_all | solution.py:314
  21.1 3.1 %collective-permute-start = (bf16[128,256]{1,0:T(8,128)(2,1)}, bf16[128,256]{1,0:T(8,128)(2,1)S(1)}, u32[]{:S(2)}, u32[]{:S(2)}) collective-permute-start(bf16[128,256]{1,0:T(8,128)(2,1)} %bitcast.37), channel_id=1, source_target_pairs={{0,1},{1,0},{2,3},{3,2},{4,5},{5,4},{6,7},{7,6},{8,9},{9,8},{10,11... | collective-permute-start | bytes 196616 | tf_op jit(solution)/shard_map/ppermute | solution.py:318
  24.2 4.4 %collective-permute-start.1 = (bf16[128,256]{1,0:T(8,128)(2,1)}, bf16[128,256]{1,0:T(8,128)(2,1)S(1)}, u32[]{:S(2)}, u32[]{:S(2)}) collective-permute-start(bf16[128,256]{1,0:T(8,128)(2,1)} %bitcast.38), channel_id=1, source_target_pairs={{0,2},{1,3},{2,0},{3,1},{4,6},{5,7},{6,4},{7,5},{8,10},{9,11},{10,... | collective-permute-start | bytes 196616 | tf_op jit(solution)/shard_map/ppermute | solution.py:318
  28.6 2.1 %collective-permute-start.2 = (bf16[128,256]{1,0:T(8,128)(2,1)}, bf16[128,256]{1,0:T(8,128)(2,1)S(1)}, u32[]{:S(2)}, u32[]{:S(2)}) collective-permute-start(bf16[128,256]{1,0:T(8,128)(2,1)} %bitcast.39), channel_id=1, source_target_pairs={{0,3},{1,2},{2,1},{3,0},{4,7},{5,6},{6,5},{7,4},{8,11},{9,10},{10,... | collective-permute-start | bytes 196616 | tf_op jit(solution)/shard_map/ppermute | solution.py:318
  30.7 0.7 copy_bitcast_fusion.1
  31.4 0.0 copy-start.3
  31.4 0.8 copy-done.3
  32.2 0.0 copy-start
  32.2 0.6 shard_map.95
  32.8 0.0 collective-permute-done
  32.8 0.0 collective-permute-done.1
  32.8 2.5 %collective-permute-done.2 = bf16[128,256]{1,0:T(8,128)(2,1)S(1)} collective-permute-done((bf16[128,256]{1,0:T(8,128)(2,1)}, bf16[128,256]{1,0:T(8,128)(2,1)S(1)}, u32[]{:S(2)}, u32[]{:S(2)}) %collective-permute-start.2) | collective-permute-done | bytes 65568 | tf_op jit(solution)/shard_map/ppermute | solution.py:318
  35.3 0.0 all-to-all-done
  35.3 3.2 %shard_map.96.gathered_any = bf16[3456,128]{1,0:T(8,128)(2,1)} custom-call(bf16[128,128]{1,0:T(8,128)(2,1)S(1)} %get-tuple-element.24.turned_ref, bf16[1024,128]{1,0:T(8,128)(2,1)S(1)} %bitcast.29, s32[27,128]{1,0:T(8,128)S(1)} %get-tuple-element.23.table_ref), custom_call_target="tpu_custom_call" | custom-call | tf_op jit(solution)/shard_map/pallas_call | solution.py:327
  38.5 6.1 %all-to-all-start.1 = ((bf16[8,432,128]{2,1,0:T(8,128)(2,1)}), bf16[8,432,128]{2,1,0:T(8,128)(2,1)S(1)}, u32[]{:S(2)}, u32[]{:S(2)}) async-start(bf16[8,432,128]{2,1,0:T(8,128)(2,1)} %bitcast.9), calls=%async_computation.1 | async-start | bytes 1769472 | tf_op jit(solution)/shard_map/all_to_all | solution.py:338
  44.6 0.0 copy-done.5
  44.6 1.9 %collective-permute-start.3 = (bf16[4,128,256]{2,1,0:T(8,128)(2,1)S(1)}, bf16[4,128,256]{2,1,0:T(8,128)(2,1)S(1)}, u32[]{:S(2)}, u32[]{:S(2)}) collective-permute-start(bf16[4,128,256]{2,1,0:T(8,128)(2,1)S(1)} %pad_maximum_fusion.near_ref), channel_id=1, source_target_pairs={{0,4},{4,0},{1,5},{5,1},{2,6},{6,2},{3,7},{7,3},{8,12},{12,8},{9,1... | collective-permute-start | bytes 786440 | tf_op jit(solution)/shard_map/ppermute | solution.py:361
  46.6 0.0 copy-done
  46.6 5.8 %shard_map.97 = (f32[128,128]{1,0:T(8,128)S(1)}, s32[5,128,128]{2,1,0:T(8,128)S(1)}, bf16[128,256]{1,0:T(8,128)(2,1)}) custom-call(bf16[4,128,256]{2,1,0:T(8,128)(2,1)S(1)} %pad_maximum_fusion.near_ref, bf16[27,256,128]{2,1,0:T(8,128)(2,1)S(1)} %copy-done, s32[27,128]{1,0:T(8,128)S(1)} %get-tuple-element.23.table_ref, bf16[3456,128]{1,0:T(8,128)(2,1)} %shard_map.96.gathered_any), custom_call_target="tpu_custom_call" | custom-call | tf_op jit(solution)/shard_map/pallas_call | solution.py:341
  52.4 0.0 copy-start.1
  52.4 0.6 copy-done.1
  53.0 0.0 collective-permute-done.3.far_ref
  53.0 4.8 %all-to-all-done.1.g_ref = bf16[8,432,128]{2,1,0:T(8,128)(2,1)S(1)} async-done(((bf16[8,432,128]{2,1,0:T(8,128)(2,1)}), bf16[8,432,128]{2,1,0:T(8,128)(2,1)S(1)}, u32[]{:S(2)}, u32[]{:S(2)}) %all-to-all-start.1) | async-done | bytes 884768 | tf_op jit(solution)/shard_map/all_to_all | solution.py:338
  57.8 0.0 copy-start.2
  57.8 0.0 copy-start.4
  57.8 0.9 shard_map.98
  58.8 32.2 %all_to_all.20 = s32[128,8,128]{2,1,0:T(8,128)S(1)} all-to-all(s32[128,8,128]{2,1,0:T(8,128)S(1)} %bitcast.28), channel_id=1, replica_groups=mesh['y'=8,'z'=8,'core'=2,'scene'=4] {'y','z','core'}, dimensions={0} | all-to-all | bytes 1048576 | tf_op jit(solution)/shard_map/all_to_all | solution.py:369
  91.0 0.7 shard_map.100
  91.7 3.3 %all-to-all-start.3 = ((f32[4,16,128]{2,1,0:T(8,128)}), f32[4,16,128]{2,1,0:T(8,128)S(1)}, u32[]{:S(2)}, u32[]{:S(2)}) async-start(f32[4,16,128]{2,1,0:T(8,128)} %shard_map.100), calls=%async_computation.3 | async-start | bytes 65536 | tf_op jit(solution)/shard_map/all_to_all | solution.py:377
  95.0 0.0 copy-done.2
  95.0 0.0 copy-done.4
  95.0 1.1 %shard_map.99 = bf16[128,128]{1,0:T(8,128)(2,1)} custom-call(f32[128,128]{1,0:T(8,128)S(1)} %copy-done.2, s32[1024,128]{1,0:T(8,128)S(1)} %bitcast.27, s32[8,128]{1,0:T(8,128)S(1)} %bitcast.31), custom_call_target="tpu_custom_call" | custom-call | flops 67108864 | bytes 524288 | tf_op jit(solution)/shard_map/pallas_call | solution.py:378
  96.1 3.1 %all-to-all-done.3 = f32[4,16,128]{2,1,0:T(8,128)S(1)} async-done(((f32[4,16,128]{2,1,0:T(8,128)}), f32[4,16,128]{2,1,0:T(8,128)S(1)}, u32[]{:S(2)}, u32[]{:S(2)}) %all-to-all-start.3) | async-done | bytes 32800 | tf_op jit(solution)/shard_map/all_to_all | solution.py:377
  99.3 0.1 mul.17
  99.4 0.6 copy.15
  (6 shorter events, 0.1 us)
Async XLA Ops:
  2.5 42.1 %copy-start.5 = (bf16[1,128,256]{2,1,0:T(8,128)(2,1)S(1)}, bf16[1,128,256]{2,1,0:T(8,128)(2,1)}, u32[]{:S(2)}) copy-start(bf16[1,128,256]{2,1,0:T(8,128)(2,1)} %param.7) | copy-start | bytes 196612
  2.5 32.8 %all-to-all-start = ((bf16[128,8,128]{2,1,0:T(8,128)(2,1)}), bf16[128,8,128]{2,1,0:T(8,128)(2,1)S(1)}, u32[]{:S(2)}, u32[]{:S(2)}) async-start(bf16[128,8,128]{2,1,0:T(8,128)(2,1)} %bitcast.32), calls=%async_computation | async-start | bytes 524288 | tf_op jit(solution)/shard_map/all_to_all | solution.py:314
  21.1 11.7 %collective-permute-start = (bf16[128,256]{1,0:T(8,128)(2,1)}, bf16[128,256]{1,0:T(8,128)(2,1)S(1)}, u32[]{:S(2)}, u32[]{:S(2)}) collective-permute-start(bf16[128,256]{1,0:T(8,128)(2,1)} %bitcast.37), channel_id=1, source_target_pairs={{0,1},{1,0},{2,3},{3,2},{4,5},{5,4},{6,7},{7,6},{8,9},{9,8},{10,11... | collective-permute-start | bytes 196616 | tf_op jit(solution)/shard_map/ppermute | solution.py:318
  24.2 8.6 %collective-permute-start.1 = (bf16[128,256]{1,0:T(8,128)(2,1)}, bf16[128,256]{1,0:T(8,128)(2,1)S(1)}, u32[]{:S(2)}, u32[]{:S(2)}) collective-permute-start(bf16[128,256]{1,0:T(8,128)(2,1)} %bitcast.38), channel_id=1, source_target_pairs={{0,2},{1,3},{2,0},{3,1},{4,6},{5,7},{6,4},{7,5},{8,10},{9,11},{10,... | collective-permute-start | bytes 196616 | tf_op jit(solution)/shard_map/ppermute | solution.py:318
  28.6 6.7 %collective-permute-start.2 = (bf16[128,256]{1,0:T(8,128)(2,1)}, bf16[128,256]{1,0:T(8,128)(2,1)S(1)}, u32[]{:S(2)}, u32[]{:S(2)}) collective-permute-start(bf16[128,256]{1,0:T(8,128)(2,1)} %bitcast.39), channel_id=1, source_target_pairs={{0,3},{1,2},{2,1},{3,0},{4,7},{5,6},{6,5},{7,4},{8,11},{9,10},{10,... | collective-permute-start | bytes 196616 | tf_op jit(solution)/shard_map/ppermute | solution.py:318
  31.4 0.8 copy-start.3
  32.2 14.4 %copy-start = (bf16[27,256,128]{2,1,0:T(8,128)(2,1)S(1)}, bf16[27,256,128]{2,1,0:T(8,128)(2,1)}, u32[]{:S(2)}) copy-start(bf16[27,256,128]{2,1,0:T(8,128)(2,1)} %w_any.1) | copy-start | bytes 5308420
  38.5 19.3 %all-to-all-start.1 = ((bf16[8,432,128]{2,1,0:T(8,128)(2,1)}), bf16[8,432,128]{2,1,0:T(8,128)(2,1)S(1)}, u32[]{:S(2)}, u32[]{:S(2)}) async-start(bf16[8,432,128]{2,1,0:T(8,128)(2,1)} %bitcast.9), calls=%async_computation.1 | async-start | bytes 1769472 | tf_op jit(solution)/shard_map/all_to_all | solution.py:338
  44.6 8.3 %collective-permute-start.3 = (bf16[4,128,256]{2,1,0:T(8,128)(2,1)S(1)}, bf16[4,128,256]{2,1,0:T(8,128)(2,1)S(1)}, u32[]{:S(2)}, u32[]{:S(2)}) collective-permute-start(bf16[4,128,256]{2,1,0:T(8,128)(2,1)S(1)} %pad_maximum_fusion.near_ref), channel_id=1, source_target_pairs={{0,4},{4,0},{1,5},{5,1},{2,6},{6,2},{3,7},{7,3},{8,12},{12,8},{9,1... | collective-permute-start | bytes 786440 | tf_op jit(solution)/shard_map/ppermute | solution.py:361
  52.4 0.6 copy-start.1
  57.8 37.1 %copy-start.2 = (f32[128,128]{1,0:T(8,128)S(1)}, f32[128,128]{1,0:T(8,128)}, u32[]{:S(2)}) copy-start(f32[128,128]{1,0:T(8,128)} %copy-done.1) | copy-start | bytes 196612
  57.8 37.2 %copy-start.4 = (s32[1,1,1024]{2,1,0:T(1,128)S(1)}, s32[1,1,1024]{2,1,0:T(1,128)}, u32[]{:S(2)}) copy-start(s32[1,1,1024]{2,1,0:T(1,128)} %param.13) | copy-start | bytes 12292
  91.7 7.5 %all-to-all-start.3 = ((f32[4,16,128]{2,1,0:T(8,128)}), f32[4,16,128]{2,1,0:T(8,128)S(1)}, u32[]{:S(2)}, u32[]{:S(2)}) async-start(f32[4,16,128]{2,1,0:T(8,128)} %shard_map.100), calls=%async_computation.3 | async-start | bytes 65536 | tf_op jit(solution)/shard_map/all_to_all | solution.py:377

commit v9 on v8

--- a/solution.py
+++ b/solution.py
@@ -323,7 +323,6 @@
         (shape((offsets, own_rows), I32), shape((out_width, own_rows), BF16)),
     )(pair_in[0, 0], pair_out[0, 0], upstream)
 
-    returned, *ring = lax.optimization_barrier((returned, *ring))
     gathered = call(
         lookup_kernel,
         shape((offsets * out_width, own_rows), BF16),
@@ -335,6 +334,7 @@
         ),
         out_specs=hbm,
     )(turned, returned.reshape(send_rows, out_width), table)
+    gathered, *ring = lax.optimization_barrier((gathered, *ring))
     group_g = lax.all_to_all(gathered.reshape(group, columns, own_rows), GROUP, 0, 0, tiled=True)
 
     near = jnp.stack([x] + ring)

time: 102 us -> 99.1 us (0.972)
  blocking collectives: 32.2 us -> 29.6 us
    all_to_all x1, blocking collectives: 32.2 us -> 29.6 us  [local(): lax.all_to_all(packed.reshape(peers, WORDS, LANES), SPACE, 0, 0, tiled=True)]
    all_to_all x1, waiting for transfers between devices: 0.01 us -> 2.53 us  [local(): lax.all_to_all(outgoing.reshape(peers, slots, out_width), SPACE, 0, 0, ti...]
    ppermute x3, waiting for transfers between devices: 2.52 us -> 0.01 us  [local(): lax.ppermute(own_x, 'scene', [(i, i ^ d) for i in range(scenes)])]
  transfers between devices with their start and end apart: 7 -> 7, of which waited for: 3 -> 3; matrix products, arithmetic and copies ran while one was open for 1% -> 1% of each run, Pallas kernels for 7% -> 11%
where the time goes in v9:
time: 99.1 us; the launch traced here: 97.5 us
  starting transfers between devices  39.4 us (40%)
  blocking collectives  29.6 us (30%)
  Pallas kernels  14.2 us (14%)
  waiting for transfers between devices  10.5 us (11%)
  local copies, waits for them, and re-layouts  2.88 us (3%)
    all_to_all x1, blocking collectives, local(): lax.all_to_all(packed.reshape(peers, WORDS, LANES), SPACE, 0, 0, tiled=True)  29.6 us
    all_to_all x1, starting transfers between devices, local(): lax.all_to_all(outgoing.reshape(peers, slots, out_width), SPACE, 0, 0, ti...  18.6 us
    ppermute x3, starting transfers between devices, local(): lax.ppermute(own_x, 'scene', [(i, i ^ d) for i in range(scenes)])  9.59 us
    all_to_all x1, starting transfers between devices, local(): lax.all_to_all(gathered.reshape(group, columns, own_rows), GROUP, 0, 0, t...  6.09 us
    pallas_call x1, Pallas kernels, local(): call(functools.partial(forward_kernel, free=free), (shape((own_rows, out_...  5.77 us
    all_to_all x1, waiting for transfers between devices, local(): lax.all_to_all(gathered.reshape(group, columns, own_rows), GROUP, 0, 0, t...  4.85 us
    all_to_all x1, starting transfers between devices, local(): sums = lax.all_to_all(quarter, 'scene', 0, 0, tiled=True)  3.26 us
    pallas_call x1, Pallas kernels, local(): call(lookup_kernel, shape((offsets * out_width, own_rows), BF16), scratch...  3.21 us
  transfers between devices with their start and end apart: 7, of which 3 were waited for; matrix products, arithmetic and copies ran while one was open for 1% of the time, Pallas kernels for 11%

profile of v9, /device:TPU:1, one launch (start us, length us, event | category | flops | bytes accessed | tf_op | source)
XLA Modules:
  0.0 97.5 jit_solution(18129224766026025318)
XLA Ops:
  0.6 1.8 %shard_map.94 = (bf16[128,128]{1,0:T(8,128)(2,1)}, bf16[1024,128]{1,0:T(8,128)(2,1)}) custom-call(bf16[128,128]{1,0:T(8,128)(2,1)} %bitcast.47, s32[128,128]{1,0:T(8,128)} %bitcast.45, s32[8,128]{1,0:T(8,128)} %bitcast.30), custom_call_target="tpu_custom_call" | custom-call | flops 33554432 | bytes 393216 | tf_op jit(solution)/shard_map/pallas_call | solution.py:299
  2.5 0.0 copy-start.5
  2.5 18.6 %all-to-all-start = ((bf16[128,8,128]{2,1,0:T(8,128)(2,1)}), bf16[128,8,128]{2,1,0:T(8,128)(2,1)S(1)}, u32[]{:S(2)}, u32[]{:S(2)}) async-start(bf16[128,8,128]{2,1,0:T(8,128)(2,1)} %bitcast.32), calls=%async_computation | async-start | bytes 524288 | tf_op jit(solution)/shard_map/all_to_all | solution.py:314
  21.1 3.1 %collective-permute-start = (bf16[128,256]{1,0:T(8,128)(2,1)}, bf16[128,256]{1,0:T(8,128)(2,1)S(1)}, u32[]{:S(2)}, u32[]{:S(2)}) collective-permute-start(bf16[128,256]{1,0:T(8,128)(2,1)} %bitcast.37), channel_id=1, source_target_pairs={{0,1},{1,0},{2,3},{3,2},{4,5},{5,4},{6,7},{7,6},{8,9},{9,8},{10,11... | collective-permute-start | bytes 196616 | tf_op jit(solution)/shard_map/ppermute | solution.py:318
  24.2 4.4 %collective-permute-start.1 = (bf16[128,256]{1,0:T(8,128)(2,1)}, bf16[128,256]{1,0:T(8,128)(2,1)S(1)}, u32[]{:S(2)}, u32[]{:S(2)}) collective-permute-start(bf16[128,256]{1,0:T(8,128)(2,1)} %bitcast.38), channel_id=1, source_target_pairs={{0,2},{1,3},{2,0},{3,1},{4,6},{5,7},{6,4},{7,5},{8,10},{9,11},{10,... | collective-permute-start | bytes 196616 | tf_op jit(solution)/shard_map/ppermute | solution.py:318
  28.6 2.1 %collective-permute-start.2 = (bf16[128,256]{1,0:T(8,128)(2,1)}, bf16[128,256]{1,0:T(8,128)(2,1)S(1)}, u32[]{:S(2)}, u32[]{:S(2)}) collective-permute-start(bf16[128,256]{1,0:T(8,128)(2,1)} %bitcast.39), channel_id=1, source_target_pairs={{0,3},{1,2},{2,1},{3,0},{4,7},{5,6},{6,5},{7,4},{8,11},{9,10},{10,... | collective-permute-start | bytes 196616 | tf_op jit(solution)/shard_map/ppermute | solution.py:318
  30.7 0.7 copy_bitcast_fusion.1
  31.4 0.0 copy-start.3
  31.4 0.8 copy-done.3
  32.2 0.0 copy-start
  32.2 0.6 shard_map.95
  32.8 2.5 %all-to-all-done = bf16[128,8,128]{2,1,0:T(8,128)(2,1)S(1)} async-done(((bf16[128,8,128]{2,1,0:T(8,128)(2,1)}), bf16[128,8,128]{2,1,0:T(8,128)(2,1)S(1)}, u32[]{:S(2)}, u32[]{:S(2)}) %all-to-all-start) | async-done | bytes 262176 | tf_op jit(solution)/shard_map/all_to_all | solution.py:314
  35.3 3.2 %shard_map.96.gathered_any = bf16[3456,128]{1,0:T(8,128)(2,1)} custom-call(bf16[128,128]{1,0:T(8,128)(2,1)S(1)} %get-tuple-element.17.turned_ref, bf16[1024,128]{1,0:T(8,128)(2,1)S(1)} %bitcast.29, s32[27,128]{1,0:T(8,128)S(1)} %get-tuple-element.20.table_ref), custom_call_target="tpu_custom_call" | custom-call | tf_op jit(solution)/shard_map/pallas_call | solution.py:326
  38.5 0.0 collective-permute-done
  38.5 0.0 collective-permute-done.1
  38.5 0.0 collective-permute-done.2
  38.5 6.1 %all-to-all-start.1 = ((bf16[8,432,128]{2,1,0:T(8,128)(2,1)}), bf16[8,432,128]{2,1,0:T(8,128)(2,1)S(1)}, u32[]{:S(2)}, u32[]{:S(2)}) async-start(bf16[8,432,128]{2,1,0:T(8,128)(2,1)} %bitcast.9), calls=%async_computation.1 | async-start | bytes 1769472 | tf_op jit(solution)/shard_map/all_to_all | solution.py:338
  44.6 0.0 copy-done.5
  44.7 1.9 %collective-permute-start.3 = (bf16[4,128,256]{2,1,0:T(8,128)(2,1)S(1)}, bf16[4,128,256]{2,1,0:T(8,128)(2,1)S(1)}, u32[]{:S(2)}, u32[]{:S(2)}) collective-permute-start(bf16[4,128,256]{2,1,0:T(8,128)(2,1)S(1)} %pad_maximum_fusion.near_ref), channel_id=1, source_target_pairs={{0,4},{4,0},{1,5},{5,1},{2,6},{6,2},{3,7},{7,3},{8,12},{12,8},{9,1... | collective-permute-start | bytes 786440 | tf_op jit(solution)/shard_map/ppermute | solution.py:361
  46.6 0.0 copy-done
  46.6 5.8 %shard_map.97 = (f32[128,128]{1,0:T(8,128)S(1)}, s32[5,128,128]{2,1,0:T(8,128)S(1)}, bf16[128,256]{1,0:T(8,128)(2,1)}) custom-call(bf16[4,128,256]{2,1,0:T(8,128)(2,1)S(1)} %pad_maximum_fusion.near_ref, bf16[27,256,128]{2,1,0:T(8,128)(2,1)S(1)} %copy-done, s32[27,128]{1,0:T(8,128)S(1)} %get-tuple-element.20.table_ref, bf16[3456,128]{1,0:T(8,128)(2,1)} %shard_map.96.gathered_any), custom_call_target="tpu_custom_call" | custom-call | tf_op jit(solution)/shard_map/pallas_call | solution.py:341
  52.4 0.0 copy-start.1
  52.4 0.6 copy-done.1
  53.0 0.0 collective-permute-done.3.far_ref
  53.0 4.8 %all-to-all-done.1.g_ref = bf16[8,432,128]{2,1,0:T(8,128)(2,1)S(1)} async-done(((bf16[8,432,128]{2,1,0:T(8,128)(2,1)}), bf16[8,432,128]{2,1,0:T(8,128)(2,1)S(1)}, u32[]{:S(2)}, u32[]{:S(2)}) %all-to-all-start.1) | async-done | bytes 884768 | tf_op jit(solution)/shard_map/all_to_all | solution.py:338
  57.9 0.0 copy-start.2
  57.9 0.0 copy-start.4
  57.9 0.9 shard_map.98
  58.8 29.6 %all_to_all.20 = s32[128,8,128]{2,1,0:T(8,128)S(1)} all-to-all(s32[128,8,128]{2,1,0:T(8,128)S(1)} %bitcast.28), channel_id=1, replica_groups=mesh['y'=8,'z'=8,'core'=2,'scene'=4] {'y','z','core'}, dimensions={0} | all-to-all | bytes 1048576 | tf_op jit(solution)/shard_map/all_to_all | solution.py:369
  88.4 0.7 shard_map.100
  89.2 3.3 %all-to-all-start.3 = ((f32[4,16,128]{2,1,0:T(8,128)}), f32[4,16,128]{2,1,0:T(8,128)S(1)}, u32[]{:S(2)}, u32[]{:S(2)}) async-start(f32[4,16,128]{2,1,0:T(8,128)} %shard_map.100), calls=%async_computation.3 | async-start | bytes 65536 | tf_op jit(solution)/shard_map/all_to_all | solution.py:377
  92.5 0.0 copy-done.2
  92.5 0.0 copy-done.4
  92.5 1.1 %shard_map.99 = bf16[128,128]{1,0:T(8,128)(2,1)} custom-call(f32[128,128]{1,0:T(8,128)S(1)} %copy-done.2, s32[1024,128]{1,0:T(8,128)S(1)} %bitcast.27, s32[8,128]{1,0:T(8,128)S(1)} %bitcast.31), custom_call_target="tpu_custom_call" | custom-call | flops 67108864 | bytes 524288 | tf_op jit(solution)/shard_map/pallas_call | solution.py:378
  93.6 3.1 %all-to-all-done.3 = f32[4,16,128]{2,1,0:T(8,128)S(1)} async-done(((f32[4,16,128]{2,1,0:T(8,128)}), f32[4,16,128]{2,1,0:T(8,128)S(1)}, u32[]{:S(2)}, u32[]{:S(2)}) %all-to-all-start.3) | async-done | bytes 32800 | tf_op jit(solution)/shard_map/all_to_all | solution.py:377
  96.8 0.1 mul.17
  96.9 0.6 copy.15
  (6 shorter events, 0.1 us)
Async XLA Ops:
  2.5 42.1 %copy-start.5 = (bf16[1,128,256]{2,1,0:T(8,128)(2,1)S(1)}, bf16[1,128,256]{2,1,0:T(8,128)(2,1)}, u32[]{:S(2)}) copy-start(bf16[1,128,256]{2,1,0:T(8,128)(2,1)} %param.7) | copy-start | bytes 196612
  2.5 32.8 %all-to-all-start = ((bf16[128,8,128]{2,1,0:T(8,128)(2,1)}), bf16[128,8,128]{2,1,0:T(8,128)(2,1)S(1)}, u32[]{:S(2)}, u32[]{:S(2)}) async-start(bf16[128,8,128]{2,1,0:T(8,128)(2,1)} %bitcast.32), calls=%async_computation | async-start | bytes 524288 | tf_op jit(solution)/shard_map/all_to_all | solution.py:314
  21.1 17.4 %collective-permute-start = (bf16[128,256]{1,0:T(8,128)(2,1)}, bf16[128,256]{1,0:T(8,128)(2,1)S(1)}, u32[]{:S(2)}, u32[]{:S(2)}) collective-permute-start(bf16[128,256]{1,0:T(8,128)(2,1)} %bitcast.37), channel_id=1, source_target_pairs={{0,1},{1,0},{2,3},{3,2},{4,5},{5,4},{6,7},{7,6},{8,9},{9,8},{10,11... | collective-permute-start | bytes 196616 | tf_op jit(solution)/shard_map/ppermute | solution.py:318
  24.2 14.3 %collective-permute-start.1 = (bf16[128,256]{1,0:T(8,128)(2,1)}, bf16[128,256]{1,0:T(8,128)(2,1)S(1)}, u32[]{:S(2)}, u32[]{:S(2)}) collective-permute-start(bf16[128,256]{1,0:T(8,128)(2,1)} %bitcast.38), channel_id=1, source_target_pairs={{0,2},{1,3},{2,0},{3,1},{4,6},{5,7},{6,4},{7,5},{8,10},{9,11},{10,... | collective-permute-start | bytes 196616 | tf_op jit(solution)/shard_map/ppermute | solution.py:318
  28.6 10.0 %collective-permute-start.2 = (bf16[128,256]{1,0:T(8,128)(2,1)}, bf16[128,256]{1,0:T(8,128)(2,1)S(1)}, u32[]{:S(2)}, u32[]{:S(2)}) collective-permute-start(bf16[128,256]{1,0:T(8,128)(2,1)} %bitcast.39), channel_id=1, source_target_pairs={{0,3},{1,2},{2,1},{3,0},{4,7},{5,6},{6,5},{7,4},{8,11},{9,10},{10,... | collective-permute-start | bytes 196616 | tf_op jit(solution)/shard_map/ppermute | solution.py:318
  31.4 0.8 copy-start.3
  32.2 14.4 %copy-start = (bf16[27,256,128]{2,1,0:T(8,128)(2,1)S(1)}, bf16[27,256,128]{2,1,0:T(8,128)(2,1)}, u32[]{:S(2)}) copy-start(bf16[27,256,128]{2,1,0:T(8,128)(2,1)} %w_any.1) | copy-start | bytes 5308420
  38.5 19.3 %all-to-all-start.1 = ((bf16[8,432,128]{2,1,0:T(8,128)(2,1)}), bf16[8,432,128]{2,1,0:T(8,128)(2,1)S(1)}, u32[]{:S(2)}, u32[]{:S(2)}) async-start(bf16[8,432,128]{2,1,0:T(8,128)(2,1)} %bitcast.9), calls=%async_computation.1 | async-start | bytes 1769472 | tf_op jit(solution)/shard_map/all_to_all | solution.py:338
  44.7 8.3 %collective-permute-start.3 = (bf16[4,128,256]{2,1,0:T(8,128)(2,1)S(1)}, bf16[4,128,256]{2,1,0:T(8,128)(2,1)S(1)}, u32[]{:S(2)}, u32[]{:S(2)}) collective-permute-start(bf16[4,128,256]{2,1,0:T(8,128)(2,1)S(1)} %pad_maximum_fusion.near_ref), channel_id=1, source_target_pairs={{0,4},{4,0},{1,5},{5,1},{2,6},{6,2},{3,7},{7,3},{8,12},{12,8},{9,1... | collective-permute-start | bytes 786440 | tf_op jit(solution)/shard_map/ppermute | solution.py:361
  52.4 0.6 copy-start.1
  57.9 34.6 %copy-start.2 = (f32[128,128]{1,0:T(8,128)S(1)}, f32[128,128]{1,0:T(8,128)}, u32[]{:S(2)}) copy-start(f32[128,128]{1,0:T(8,128)} %copy-done.1) | copy-start | bytes 196612
  57.9 34.6 %copy-start.4 = (s32[1,1,1024]{2,1,0:T(1,128)S(1)}, s32[1,1,1024]{2,1,0:T(1,128)}, u32[]{:S(2)}) copy-start(s32[1,1,1024]{2,1,0:T(1,128)} %param.13) | copy-start | bytes 12292
  89.2 7.5 %all-to-all-start.3 = ((f32[4,16,128]{2,1,0:T(8,128)}), f32[4,16,128]{2,1,0:T(8,128)S(1)}, u32[]{:S(2)}, u32[]{:S(2)}) async-start(f32[4,16,128]{2,1,0:T(8,128)} %shard_map.100), calls=%async_computation.3 | async-start | bytes 65536 | tf_op jit(solution)/shard_map/all_to_all | solution.py:377

commit v10 on v9

--- a/solution.py
+++ b/solution.py
@@ -57,40 +57,53 @@
     return slice(k * LANES, (k + 1) * LANES)
 
 
-def gather_kernel(cot_any, mask_any, recv_any, up_ref, out_ref, cot_ref, mask_ref, recv_ref, sems):
-    pairs = ((cot_any, cot_ref), (mask_any, mask_ref), (recv_any, recv_ref))
+def gather_kernel(
+    cot_any, mask_any, recv_any, in_any, pair_any, shared_ref, out_ref, cot_ref, mask_ref, recv_ref, in_ref, pair_ref, digit_ref, sems, *, targets
+):
+    pairs = (
+        (cot_any, cot_ref),
+        (mask_any, mask_ref),
+        (recv_any, recv_ref),
+        (in_any, in_ref),
+        (pair_any, pair_ref),
+    )
     copies = [pltpu.make_async_copy(a, b, sems.at[i]) for i, (a, b) in enumerate(pairs)]
     for copy in copies:
         copy.start()
+    digit_ref[...] = jnp.zeros_like(digit_ref)
     for copy in copies:
         copy.wait()
     up = (cot_ref[...].astype(F32) * mask_ref[...].astype(F32)).astype(BF16)
-    up_ref[...] = up
+    shared_ref[0:LANES, :] = up.T
     iota = rows_iota(LANES)
     for g in range(recv_ref.shape[0]):
         hot = one_hot(iota, recv_ref[g : g + 1, :])
         rows = lax.dot_general(hot, up, (((0,), (0,)), ((), ())), preferred_element_type=F32)
         out_ref[lane_block(g), :] = rows.astype(BF16)
-
-
-def table_kernel(in_ref, out_ref, up_ref, table_ref, turned_ref, *, targets):
-    turned_ref[...] = up_ref[...].T
-    iota = rows_iota(LANES)
     picks = rows_iota(16)
     for k in range(in_ref.shape[0]):
-        hot = one_hot(iota, in_ref[k : k + 1, :])
-        target = out_ref[k : k + 1, :]
+        hot = one_hot(iota, in_ref[k])
+        target = pair_ref[k]
         code = jnp.where(target < targets, target + 1, 0)
         digits = jnp.where(picks == 0, code >> 7, jnp.where(picks == 1, code & 127, 0))
         found = lax.dot_general(
             digits.astype(F32).astype(BF16), hot, (((1,), (1,)), ((), ())), preferred_element_type=F32
         )
-        table_ref[k : k + 1, :] = (found[0:1] * 128.0 + found[1:2] - 1.0).astype(I32)
+        digit_ref[k : k + 1, :] = found[0:1]
+        digit_ref[32 + k : 33 + k, :] = found[1:2]
+    shared_ref[LANES : LANES + 64, :] = digit_ref[...].astype(BF16)
+
+
+def table_kernel(shared_ref, table_ref, turned_ref):
+    high = shared_ref[LANES : LANES + 32, :].astype(F32)
+    low = shared_ref[LANES + 32 : LANES + 64, :].astype(F32)
+    table_ref[...] = (high * 128.0 + low - 1.0).astype(I32)
+    turned_ref[...] = shared_ref[0:LANES, :]
 
 
 def lookup_kernel(turned_ref, back_ref, table_ref, gathered_any, ext_ref, hot_ref, gathered_ref, sems):
     blocks = back_ref.shape[0] // LANES
-    offsets = table_ref.shape[0]
+    offsets = gathered_ref.shape[0] // LANES
     ext_ref[:, 0:LANES] = turned_ref[...]
     for b in range(blocks):
         ext_ref[:, lane_block(b + 1)] = back_ref[lane_block(b), :].T
@@ -296,20 +309,24 @@
     blocks = -(-columns // LANES)
     free = columns - (blocks - 1) * LANES
 
-    upstream, outgoing = call(
-        gather_kernel,
-        (shape((own_rows, out_width), BF16), shape((send_rows, out_width), BF16)),
+    lists = [pairs.reshape(offsets, 1, own_rows) for pairs in (pair_in, pair_out)]
+    shared, outgoing = call(
+        functools.partial(gather_kernel, targets=targets),
+        (shape((out_width + 64, own_rows), BF16), shape((send_rows, out_width), BF16)),
         scratch=(
             pltpu.VMEM((own_rows, out_width), BF16),
             pltpu.VMEM((own_rows, out_width), I32),
             pltpu.VMEM(recv.shape, I32),
-            pltpu.SemaphoreType.DMA((3,)),
+            pltpu.VMEM(lists[0].shape, I32),
+            pltpu.VMEM(lists[1].shape, I32),
+            pltpu.VMEM((64, own_rows), F32),
+            pltpu.SemaphoreType.DMA((5,)),
         ),
-        in_specs=[hbm] * 3,
+        in_specs=[hbm] * 5,
         vmem=MOST_VMEM,
         flops=2 * send_rows * own_rows * out_width,
         moved=send_rows * out_width * 3,
-    )(cotangent[0], relu_mask[0], recv)
+    )(cotangent[0], relu_mask[0], recv, *lists)
     own_x, outgoing = lax.optimization_barrier((x, outgoing))
     returned = lax.all_to_all(outgoing.reshape(peers, slots, out_width), SPACE, 0, 0, tiled=True)
 
@@ -319,10 +336,8 @@
     ]
 
     table, turned = call(
-        functools.partial(table_kernel, targets=targets),
-        (shape((offsets, own_rows), I32), shape((out_width, own_rows), BF16)),
-    )(pair_in[0, 0], pair_out[0, 0], upstream)
-
+        table_kernel, (shape((32, own_rows), I32), shape((out_width, own_rows), BF16))
+    )(shared)
     gathered = call(
         lookup_kernel,
         shape((offsets * out_width, own_rows), BF16),

time: 99.1 us -> 98.8 us (level)
  waiting for transfers between devices: 10.5 us -> 11.8 us
    all_to_all x1, waiting for transfers between devices: 2.53 us -> 3.8 us  [local(): lax.all_to_all(outgoing.reshape(peers, slots, out_width), SPACE, 0, 0, ti...]
    unnamed x15 -> x14, local copies, waits for them, and re-layouts: 2.75 us -> 2.06 us
  transfers between devices with their start and end apart: 7 -> 7, of which waited for: 3 -> 3; matrix products, arithmetic and copies ran while one was open for 1% -> 0% of each run, Pallas kernels for 11% -> 10%
where the time goes in v10:
time: 98.8 us; the launch traced here: 97.2 us
  starting transfers between devices  39.4 us (40%)
  blocking collectives  28.9 us (29%)
  Pallas kernels  14 us (14%)
  waiting for transfers between devices  11.8 us (12%)
  local copies, waits for them, and re-layouts  2.19 us (2%)
    all_to_all x1, blocking collectives, local(): lax.all_to_all(packed.reshape(peers, WORDS, LANES), SPACE, 0, 0, tiled=True)  28.9 us
    all_to_all x1, starting transfers between devices, local(): lax.all_to_all(outgoing.reshape(peers, slots, out_width), SPACE, 0, 0, ti...  18.6 us
    ppermute x3, starting transfers between devices, local(): lax.ppermute(own_x, 'scene', [(i, i ^ d) for i in range(scenes)])  9.59 us
    all_to_all x1, starting transfers between devices, local(): lax.all_to_all(gathered.reshape(group, columns, own_rows), GROUP, 0, 0, t...  6.11 us
    pallas_call x1, Pallas kernels, local(): call(functools.partial(forward_kernel, free=free), (shape((own_rows, out_...  5.78 us
    all_to_all x1, waiting for transfers between devices, local(): lax.all_to_all(gathered.reshape(group, columns, own_rows), GROUP, 0, 0, t...  4.84 us
    all_to_all x1, waiting for transfers between devices, local(): lax.all_to_all(outgoing.reshape(peers, slots, out_width), SPACE, 0, 0, ti...  3.8 us
    all_to_all x1, starting transfers between devices, local(): sums = lax.all_to_all(quarter, 'scene', 0, 0, tiled=True)  3.26 us
  transfers between devices with their start and end apart: 7, of which 3 were waited for; matrix products, arithmetic and copies ran while one was open for 0% of the time, Pallas kernels for 10%

profile of v10, /device:TPU:1, one launch (start us, length us, event | category | flops | bytes accessed | tf_op | source)
XLA Modules:
  0.0 97.2 jit_solution(10225962945896911185)
XLA Ops:
  0.6 2.2 %shard_map.94 = (bf16[192,128]{1,0:T(8,128)(2,1)}, bf16[1024,128]{1,0:T(8,128)(2,1)}) custom-call(bf16[128,128]{1,0:T(8,128)(2,1)} %bitcast.44, s32[128,128]{1,0:T(8,128)} %bitcast.35, s32[8,128]{1,0:T(8,128)} %bitcast.28, s32[27,1,128]{2,1,0:T(1,128)} %bitcast.45, s32[27,1,128]{2,1,0:T(1,128)} %bitcast.46), custom_call_target="tpu_custom_call" | custom-call | flops 33554432 | bytes 393216 | tf_op jit(solution)/shard_map/pallas_call | solution.py:313
  2.9 0.0 copy-start.5
  2.9 18.6 %all-to-all-start = ((bf16[128,8,128]{2,1,0:T(8,128)(2,1)}), bf16[128,8,128]{2,1,0:T(8,128)(2,1)S(1)}, u32[]{:S(2)}, u32[]{:S(2)}) async-start(bf16[128,8,128]{2,1,0:T(8,128)(2,1)} %bitcast.30), calls=%async_computation | async-start | bytes 524288 | tf_op jit(solution)/shard_map/all_to_all | solution.py:331
  21.5 3.1 %collective-permute-start = (bf16[128,256]{1,0:T(8,128)(2,1)}, bf16[128,256]{1,0:T(8,128)(2,1)S(1)}, u32[]{:S(2)}, u32[]{:S(2)}) collective-permute-start(bf16[128,256]{1,0:T(8,128)(2,1)} %bitcast.36), channel_id=1, source_target_pairs={{0,1},{1,0},{2,3},{3,2},{4,5},{5,4},{6,7},{7,6},{8,9},{9,8},{10,11... | collective-permute-start | bytes 196616 | tf_op jit(solution)/shard_map/ppermute | solution.py:335
  24.6 4.4 %collective-permute-start.1 = (bf16[128,256]{1,0:T(8,128)(2,1)}, bf16[128,256]{1,0:T(8,128)(2,1)S(1)}, u32[]{:S(2)}, u32[]{:S(2)}) collective-permute-start(bf16[128,256]{1,0:T(8,128)(2,1)} %bitcast.37), channel_id=1, source_target_pairs={{0,2},{1,3},{2,0},{3,1},{4,6},{5,7},{6,4},{7,5},{8,10},{9,11},{10,... | collective-permute-start | bytes 196616 | tf_op jit(solution)/shard_map/ppermute | solution.py:335
  29.0 2.1 %collective-permute-start.2 = (bf16[128,256]{1,0:T(8,128)(2,1)}, bf16[128,256]{1,0:T(8,128)(2,1)S(1)}, u32[]{:S(2)}, u32[]{:S(2)}) collective-permute-start(bf16[128,256]{1,0:T(8,128)(2,1)} %bitcast.38), channel_id=1, source_target_pairs={{0,3},{1,2},{2,1},{3,0},{4,7},{5,6},{6,5},{7,4},{8,11},{9,10},{10,... | collective-permute-start | bytes 196616 | tf_op jit(solution)/shard_map/ppermute | solution.py:335
  31.1 0.0 copy-start.3
  31.1 0.8 copy-done.3
  31.9 0.0 copy-start
  31.9 3.8 %all-to-all-done = bf16[128,8,128]{2,1,0:T(8,128)(2,1)S(1)} async-done(((bf16[128,8,128]{2,1,0:T(8,128)(2,1)}), bf16[128,8,128]{2,1,0:T(8,128)(2,1)S(1)}, u32[]{:S(2)}, u32[]{:S(2)}) %all-to-all-start) | async-done | bytes 262176 | tf_op jit(solution)/shard_map/all_to_all | solution.py:331
  35.7 3.2 %shard_map.96.gathered_any = bf16[3456,128]{1,0:T(8,128)(2,1)} custom-call(bf16[128,128]{1,0:T(8,128)(2,1)S(1)} %get-tuple-element.17.turned_ref, bf16[1024,128]{1,0:T(8,128)(2,1)S(1)} %bitcast.27, s32[32,128]{1,0:T(8,128)S(1)} %get-tuple-element.20.table_ref), custom_call_target="tpu_custom_call" | custom-call | tf_op jit(solution)/shard_map/pallas_call | solution.py:341
  38.9 0.0 collective-permute-done
  38.9 0.0 collective-permute-done.1
  38.9 0.0 collective-permute-done.2
  38.9 6.1 %all-to-all-start.1 = ((bf16[8,432,128]{2,1,0:T(8,128)(2,1)}), bf16[8,432,128]{2,1,0:T(8,128)(2,1)S(1)}, u32[]{:S(2)}, u32[]{:S(2)}) async-start(bf16[8,432,128]{2,1,0:T(8,128)(2,1)} %bitcast.11), calls=%async_computation.1 | async-start | bytes 1769472 | tf_op jit(solution)/shard_map/all_to_all | solution.py:353
  45.0 0.0 copy-done.5
  45.1 1.9 %collective-permute-start.3 = (bf16[4,128,256]{2,1,0:T(8,128)(2,1)S(1)}, bf16[4,128,256]{2,1,0:T(8,128)(2,1)S(1)}, u32[]{:S(2)}, u32[]{:S(2)}) collective-permute-start(bf16[4,128,256]{2,1,0:T(8,128)(2,1)S(1)} %pad_maximum_fusion.near_ref), channel_id=1, source_target_pairs={{0,4},{4,0},{1,5},{5,1},{2,6},{6,2},{3,7},{7,3},{8,12},{12,8},{9,1... | collective-permute-start | bytes 786440 | tf_op jit(solution)/shard_map/ppermute | solution.py:376
  47.0 0.0 copy-done
  47.0 5.8 %shard_map.97 = (f32[128,128]{1,0:T(8,128)S(1)}, s32[5,128,128]{2,1,0:T(8,128)S(1)}, bf16[128,256]{1,0:T(8,128)(2,1)}) custom-call(bf16[4,128,256]{2,1,0:T(8,128)(2,1)S(1)} %pad_maximum_fusion.near_ref, bf16[27,256,128]{2,1,0:T(8,128)(2,1)S(1)} %copy-done, s32[32,128]{1,0:T(8,128)S(1)} %get-tuple-element.20.table_ref, bf16[3456,128]{1,0:T(8,128)(2,1)} %shard_map.96.gathered_any), custom_call_target="tpu_custom_call" | custom-call | tf_op jit(solution)/shard_map/pallas_call | solution.py:356
  52.8 0.0 copy-start.1
  52.8 0.6 copy-done.1
  53.4 0.0 collective-permute-done.3.far_ref
  53.4 4.8 %all-to-all-done.1.g_ref = bf16[8,432,128]{2,1,0:T(8,128)(2,1)S(1)} async-done(((bf16[8,432,128]{2,1,0:T(8,128)(2,1)}), bf16[8,432,128]{2,1,0:T(8,128)(2,1)S(1)}, u32[]{:S(2)}, u32[]{:S(2)}) %all-to-all-start.1) | async-done | bytes 884768 | tf_op jit(solution)/shard_map/all_to_all | solution.py:353
  58.3 0.0 copy-start.2
  58.3 0.0 copy-start.4
  58.3 0.9 shard_map.98
  59.2 28.9 %all_to_all.20 = s32[128,8,128]{2,1,0:T(8,128)S(1)} all-to-all(s32[128,8,128]{2,1,0:T(8,128)S(1)} %bitcast.26), channel_id=1, replica_groups=mesh['y'=8,'z'=8,'core'=2,'scene'=4] {'y','z','core'}, dimensions={0} | all-to-all | bytes 1048576 | tf_op jit(solution)/shard_map/all_to_all | solution.py:384
  88.1 0.7 shard_map.100
  88.9 3.3 %all-to-all-start.3 = ((f32[4,16,128]{2,1,0:T(8,128)}), f32[4,16,128]{2,1,0:T(8,128)S(1)}, u32[]{:S(2)}, u32[]{:S(2)}) async-start(f32[4,16,128]{2,1,0:T(8,128)} %shard_map.100), calls=%async_computation.3 | async-start | bytes 65536 | tf_op jit(solution)/shard_map/all_to_all | solution.py:392
  92.1 0.0 copy-done.2
  92.2 0.0 copy-done.4
  92.2 1.1 %shard_map.99 = bf16[128,128]{1,0:T(8,128)(2,1)} custom-call(f32[128,128]{1,0:T(8,128)S(1)} %copy-done.2, s32[1024,128]{1,0:T(8,128)S(1)} %bitcast.25, s32[8,128]{1,0:T(8,128)S(1)} %bitcast.29), custom_call_target="tpu_custom_call" | custom-call | flops 67108864 | bytes 524288 | tf_op jit(solution)/shard_map/pallas_call | solution.py:393
  93.3 3.1 %all-to-all-done.3 = f32[4,16,128]{2,1,0:T(8,128)S(1)} async-done(((f32[4,16,128]{2,1,0:T(8,128)}), f32[4,16,128]{2,1,0:T(8,128)S(1)}, u32[]{:S(2)}, u32[]{:S(2)}) %all-to-all-start.3) | async-done | bytes 32800 | tf_op jit(solution)/shard_map/all_to_all | solution.py:392
  96.5 0.1 mul.17
  96.6 0.6 copy.13
  (7 shorter events, 0.1 us)
Async XLA Ops:
  2.9 42.2 %copy-start.5 = (bf16[1,128,256]{2,1,0:T(8,128)(2,1)S(1)}, bf16[1,128,256]{2,1,0:T(8,128)(2,1)}, u32[]{:S(2)}) copy-start(bf16[1,128,256]{2,1,0:T(8,128)(2,1)} %param.7) | copy-start | bytes 196612
  2.9 32.8 %all-to-all-start = ((bf16[128,8,128]{2,1,0:T(8,128)(2,1)}), bf16[128,8,128]{2,1,0:T(8,128)(2,1)S(1)}, u32[]{:S(2)}, u32[]{:S(2)}) async-start(bf16[128,8,128]{2,1,0:T(8,128)(2,1)} %bitcast.30), calls=%async_computation | async-start | bytes 524288 | tf_op jit(solution)/shard_map/all_to_all | solution.py:331
  21.5 17.4 %collective-permute-start = (bf16[128,256]{1,0:T(8,128)(2,1)}, bf16[128,256]{1,0:T(8,128)(2,1)S(1)}, u32[]{:S(2)}, u32[]{:S(2)}) collective-permute-start(bf16[128,256]{1,0:T(8,128)(2,1)} %bitcast.36), channel_id=1, source_target_pairs={{0,1},{1,0},{2,3},{3,2},{4,5},{5,4},{6,7},{7,6},{8,9},{9,8},{10,11... | collective-permute-start | bytes 196616 | tf_op jit(solution)/shard_map/ppermute | solution.py:335
  24.6 14.3 %collective-permute-start.1 = (bf16[128,256]{1,0:T(8,128)(2,1)}, bf16[128,256]{1,0:T(8,128)(2,1)S(1)}, u32[]{:S(2)}, u32[]{:S(2)}) collective-permute-start(bf16[128,256]{1,0:T(8,128)(2,1)} %bitcast.37), channel_id=1, source_target_pairs={{0,2},{1,3},{2,0},{3,1},{4,6},{5,7},{6,4},{7,5},{8,10},{9,11},{10,... | collective-permute-start | bytes 196616 | tf_op jit(solution)/shard_map/ppermute | solution.py:335
  29.0 10.0 %collective-permute-start.2 = (bf16[128,256]{1,0:T(8,128)(2,1)}, bf16[128,256]{1,0:T(8,128)(2,1)S(1)}, u32[]{:S(2)}, u32[]{:S(2)}) collective-permute-start(bf16[128,256]{1,0:T(8,128)(2,1)} %bitcast.38), channel_id=1, source_target_pairs={{0,3},{1,2},{2,1},{3,0},{4,7},{5,6},{6,5},{7,4},{8,11},{9,10},{10,... | collective-permute-start | bytes 196616 | tf_op jit(solution)/shard_map/ppermute | solution.py:335
  31.1 0.8 copy-start.3
  31.9 15.1 %copy-start = (bf16[27,256,128]{2,1,0:T(8,128)(2,1)S(1)}, bf16[27,256,128]{2,1,0:T(8,128)(2,1)}, u32[]{:S(2)}) copy-start(bf16[27,256,128]{2,1,0:T(8,128)(2,1)} %w_any.1) | copy-start | bytes 5308420
  38.9 19.3 %all-to-all-start.1 = ((bf16[8,432,128]{2,1,0:T(8,128)(2,1)}), bf16[8,432,128]{2,1,0:T(8,128)(2,1)S(1)}, u32[]{:S(2)}, u32[]{:S(2)}) async-start(bf16[8,432,128]{2,1,0:T(8,128)(2,1)} %bitcast.11), calls=%async_computation.1 | async-start | bytes 1769472 | tf_op jit(solution)/shard_map/all_to_all | solution.py:353
  45.1 8.3 %collective-permute-start.3 = (bf16[4,128,256]{2,1,0:T(8,128)(2,1)S(1)}, bf16[4,128,256]{2,1,0:T(8,128)(2,1)S(1)}, u32[]{:S(2)}, u32[]{:S(2)}) collective-permute-start(bf16[4,128,256]{2,1,0:T(8,128)(2,1)S(1)} %pad_maximum_fusion.near_ref), channel_id=1, source_target_pairs={{0,4},{4,0},{1,5},{5,1},{2,6},{6,2},{3,7},{7,3},{8,12},{12,8},{9,1... | collective-permute-start | bytes 786440 | tf_op jit(solution)/shard_map/ppermute | solution.py:376
  52.8 0.6 copy-start.1
  58.3 33.9 %copy-start.2 = (f32[128,128]{1,0:T(8,128)S(1)}, f32[128,128]{1,0:T(8,128)}, u32[]{:S(2)}) copy-start(f32[128,128]{1,0:T(8,128)} %copy-done.1) | copy-start | bytes 196612
  58.3 33.9 %copy-start.4 = (s32[1,1,1024]{2,1,0:T(1,128)S(1)}, s32[1,1,1024]{2,1,0:T(1,128)}, u32[]{:S(2)}) copy-start(s32[1,1,1024]{2,1,0:T(1,128)} %param.13) | copy-start | bytes 12292
  88.9 7.5 %all-to-all-start.3 = ((f32[4,16,128]{2,1,0:T(8,128)}), f32[4,16,128]{2,1,0:T(8,128)S(1)}, u32[]{:S(2)}, u32[]{:S(2)}) async-start(f32[4,16,128]{2,1,0:T(8,128)} %shard_map.100), calls=%async_computation.3 | async-start | bytes 65536 | tf_op jit(solution)/shard_map/all_to_all | solution.py:392

commit v11 on v10

--- a/solution.py
+++ b/solution.py
@@ -135,7 +135,7 @@
 
 
 def unit(level):
-    return jnp.exp2(level.astype(F32) * 0.125) * (1.0 / 32767.0)
+    return jnp.exp2(level.astype(F32) * 0.125)
 
 
 def join(first, second):
@@ -143,7 +143,8 @@
 
 
 def halves(word):
-    return (word >> 16).astype(F32), ((word << 16) >> 16).astype(F32)
+    scale = 1.0 / 32767.0
+    return (word >> 16).astype(F32) * scale, ((word << 16) >> 16).astype(F32) * scale
 
 
 def row_top(value):
@@ -235,10 +236,13 @@
     scenes = near_ref.shape[0]
     core, scene = (lax.axis_index(axis) for axis in GROUP)
     total = jnp.zeros((columns, near_ref.shape[2]), F32)
-    for s in range(g_ref.shape[0]):
+    for s in range(0, g_ref.shape[0], 2):
         x_ref, holder = (near_ref, core) if s < scenes else (far_ref, 1 - core)
-        sender = holder * scenes + (scene ^ (s % scenes))
-        total += jnp.dot(g_ref[sender], x_ref[s % scenes], preferred_element_type=F32)
+        senders = [holder * scenes + (scene ^ ((s + i) % scenes)) for i in range(2)]
+        both = jnp.concatenate([g_ref[sender] for sender in senders], axis=1)
+        first = s % scenes
+        rows = x_ref[first : first + 2].reshape(both.shape[1], total.shape[1])
+        total += jnp.dot(both, rows, preferred_element_type=F32)
     rest = blocks * LANES - columns
     total = jnp.concatenate([total, jnp.zeros((rest, total.shape[1]), F32)], axis=0)
     for h in range(blocks):

time: 98.8 us -> 98.6 us (level)
  no operation moved by 1% of the time
where the time goes in v11:
time: 98.6 us; the launch traced here: 97 us
  starting transfers between devices  39.4 us (40%)
  blocking collectives  28.9 us (29%)
  Pallas kernels  13.8 us (14%)
  waiting for transfers between devices  11.8 us (12%)
  local copies, waits for them, and re-layouts  2.19 us (2%)
    all_to_all x1, blocking collectives, local(): lax.all_to_all(packed.reshape(peers, WORDS, LANES), SPACE, 0, 0, tiled=True)  28.9 us
    all_to_all x1, starting transfers between devices, local(): lax.all_to_all(outgoing.reshape(peers, slots, out_width), SPACE, 0, 0, ti...  18.6 us
    ppermute x3, starting transfers between devices, local(): lax.ppermute(own_x, 'scene', [(i, i ^ d) for i in range(scenes)])  9.59 us
    all_to_all x1, starting transfers between devices, local(): lax.all_to_all(gathered.reshape(group, columns, own_rows), GROUP, 0, 0, t...  6.11 us
    pallas_call x1, Pallas kernels, local(): call(functools.partial(forward_kernel, free=free), (shape((own_rows, out_...  5.78 us
    all_to_all x1, waiting for transfers between devices, local(): lax.all_to_all(gathered.reshape(group, columns, own_rows), GROUP, 0, 0, t...  4.84 us
    all_to_all x1, waiting for transfers between devices, local(): lax.all_to_all(outgoing.reshape(peers, slots, out_width), SPACE, 0, 0, ti...  3.8 us
    all_to_all x1, starting transfers between devices, local(): sums = lax.all_to_all(quarter, 'scene', 0, 0, tiled=True)  3.26 us
  transfers between devices with their start and end apart: 7, of which 3 were waited for; matrix products, arithmetic and copies ran while one was open for 0% of the time, Pallas kernels for 10%

profile of v11, /device:TPU:1, one launch (start us, length us, event | category | flops | bytes accessed | tf_op | source)
XLA Modules:
  0.0 97.0 jit_solution(18316918520909063415)
XLA Ops:
  0.6 2.2 %shard_map.94 = (bf16[192,128]{1,0:T(8,128)(2,1)}, bf16[1024,128]{1,0:T(8,128)(2,1)}) custom-call(bf16[128,128]{1,0:T(8,128)(2,1)} %bitcast.44, s32[128,128]{1,0:T(8,128)} %bitcast.35, s32[8,128]{1,0:T(8,128)} %bitcast.28, s32[27,1,128]{2,1,0:T(1,128)} %bitcast.45, s32[27,1,128]{2,1,0:T(1,128)} %bitcast.46), custom_call_target="tpu_custom_call" | custom-call | flops 33554432 | bytes 393216 | tf_op jit(solution)/shard_map/pallas_call | solution.py:317
  2.9 0.0 copy-start.5
  2.9 18.6 %all-to-all-start = ((bf16[128,8,128]{2,1,0:T(8,128)(2,1)}), bf16[128,8,128]{2,1,0:T(8,128)(2,1)S(1)}, u32[]{:S(2)}, u32[]{:S(2)}) async-start(bf16[128,8,128]{2,1,0:T(8,128)(2,1)} %bitcast.30), calls=%async_computation | async-start | bytes 524288 | tf_op jit(solution)/shard_map/all_to_all | solution.py:335
  21.5 3.1 %collective-permute-start = (bf16[128,256]{1,0:T(8,128)(2,1)}, bf16[128,256]{1,0:T(8,128)(2,1)S(1)}, u32[]{:S(2)}, u32[]{:S(2)}) collective-permute-start(bf16[128,256]{1,0:T(8,128)(2,1)} %bitcast.36), channel_id=1, source_target_pairs={{0,1},{1,0},{2,3},{3,2},{4,5},{5,4},{6,7},{7,6},{8,9},{9,8},{10,11... | collective-permute-start | bytes 196616 | tf_op jit(solution)/shard_map/ppermute | solution.py:339
  24.6 4.4 %collective-permute-start.1 = (bf16[128,256]{1,0:T(8,128)(2,1)}, bf16[128,256]{1,0:T(8,128)(2,1)S(1)}, u32[]{:S(2)}, u32[]{:S(2)}) collective-permute-start(bf16[128,256]{1,0:T(8,128)(2,1)} %bitcast.37), channel_id=1, source_target_pairs={{0,2},{1,3},{2,0},{3,1},{4,6},{5,7},{6,4},{7,5},{8,10},{9,11},{10,... | collective-permute-start | bytes 196616 | tf_op jit(solution)/shard_map/ppermute | solution.py:339
  29.0 2.1 %collective-permute-start.2 = (bf16[128,256]{1,0:T(8,128)(2,1)}, bf16[128,256]{1,0:T(8,128)(2,1)S(1)}, u32[]{:S(2)}, u32[]{:S(2)}) collective-permute-start(bf16[128,256]{1,0:T(8,128)(2,1)} %bitcast.38), channel_id=1, source_target_pairs={{0,3},{1,2},{2,1},{3,0},{4,7},{5,6},{6,5},{7,4},{8,11},{9,10},{10,... | collective-permute-start | bytes 196616 | tf_op jit(solution)/shard_map/ppermute | solution.py:339
  31.1 0.0 copy-start.3
  31.1 0.8 copy-done.3
  31.9 0.0 copy-start
  31.9 3.8 %all-to-all-done = bf16[128,8,128]{2,1,0:T(8,128)(2,1)S(1)} async-done(((bf16[128,8,128]{2,1,0:T(8,128)(2,1)}), bf16[128,8,128]{2,1,0:T(8,128)(2,1)S(1)}, u32[]{:S(2)}, u32[]{:S(2)}) %all-to-all-start) | async-done | bytes 262176 | tf_op jit(solution)/shard_map/all_to_all | solution.py:335
  35.7 3.2 %shard_map.96.gathered_any = bf16[3456,128]{1,0:T(8,128)(2,1)} custom-call(bf16[128,128]{1,0:T(8,128)(2,1)S(1)} %get-tuple-element.17.turned_ref, bf16[1024,128]{1,0:T(8,128)(2,1)S(1)} %bitcast.27, s32[32,128]{1,0:T(8,128)S(1)} %get-tuple-element.20.table_ref), custom_call_target="tpu_custom_call" | custom-call | tf_op jit(solution)/shard_map/pallas_call | solution.py:345
  38.9 0.0 collective-permute-done
  38.9 0.0 collective-permute-done.1
  38.9 0.0 collective-permute-done.2
  38.9 6.1 %all-to-all-start.1 = ((bf16[8,432,128]{2,1,0:T(8,128)(2,1)}), bf16[8,432,128]{2,1,0:T(8,128)(2,1)S(1)}, u32[]{:S(2)}, u32[]{:S(2)}) async-start(bf16[8,432,128]{2,1,0:T(8,128)(2,1)} %bitcast.11), calls=%async_computation.1 | async-start | bytes 1769472 | tf_op jit(solution)/shard_map/all_to_all | solution.py:357
  45.0 0.0 copy-done.5
  45.1 1.9 %collective-permute-start.3 = (bf16[4,128,256]{2,1,0:T(8,128)(2,1)S(1)}, bf16[4,128,256]{2,1,0:T(8,128)(2,1)S(1)}, u32[]{:S(2)}, u32[]{:S(2)}) collective-permute-start(bf16[4,128,256]{2,1,0:T(8,128)(2,1)S(1)} %pad_maximum_fusion.near_ref), channel_id=1, source_target_pairs={{0,4},{4,0},{1,5},{5,1},{2,6},{6,2},{3,7},{7,3},{8,12},{12,8},{9,1... | collective-permute-start | bytes 786440 | tf_op jit(solution)/shard_map/ppermute | solution.py:380
  47.0 0.0 copy-done
  47.0 5.8 %shard_map.97 = (f32[128,128]{1,0:T(8,128)S(1)}, s32[5,128,128]{2,1,0:T(8,128)S(1)}, bf16[128,256]{1,0:T(8,128)(2,1)}) custom-call(bf16[4,128,256]{2,1,0:T(8,128)(2,1)S(1)} %pad_maximum_fusion.near_ref, bf16[27,256,128]{2,1,0:T(8,128)(2,1)S(1)} %copy-done, s32[32,128]{1,0:T(8,128)S(1)} %get-tuple-element.20.table_ref, bf16[3456,128]{1,0:T(8,128)(2,1)} %shard_map.96.gathered_any), custom_call_target="tpu_custom_call" | custom-call | tf_op jit(solution)/shard_map/pallas_call | solution.py:360
  52.8 0.0 copy-start.1
  52.8 0.6 copy-done.1
  53.4 0.0 collective-permute-done.3.far_ref
  53.4 4.8 %all-to-all-done.1.g_ref = bf16[8,432,128]{2,1,0:T(8,128)(2,1)S(1)} async-done(((bf16[8,432,128]{2,1,0:T(8,128)(2,1)}), bf16[8,432,128]{2,1,0:T(8,128)(2,1)S(1)}, u32[]{:S(2)}, u32[]{:S(2)}) %all-to-all-start.1) | async-done | bytes 884768 | tf_op jit(solution)/shard_map/all_to_all | solution.py:357
  58.3 0.0 copy-start.2
  58.3 0.0 copy-start.4
  58.3 0.7 shard_map.98
  59.0 28.9 %all_to_all.20 = s32[128,8,128]{2,1,0:T(8,128)S(1)} all-to-all(s32[128,8,128]{2,1,0:T(8,128)S(1)} %bitcast.26), channel_id=1, replica_groups=mesh['y'=8,'z'=8,'core'=2,'scene'=4] {'y','z','core'}, dimensions={0} | all-to-all | bytes 1048576 | tf_op jit(solution)/shard_map/all_to_all | solution.py:388
  87.9 0.7 shard_map.100
  88.7 3.3 %all-to-all-start.3 = ((f32[4,16,128]{2,1,0:T(8,128)}), f32[4,16,128]{2,1,0:T(8,128)S(1)}, u32[]{:S(2)}, u32[]{:S(2)}) async-start(f32[4,16,128]{2,1,0:T(8,128)} %shard_map.100), calls=%async_computation.3 | async-start | bytes 65536 | tf_op jit(solution)/shard_map/all_to_all | solution.py:396
  91.9 0.0 copy-done.2
  92.0 0.0 copy-done.4
  92.0 1.1 %shard_map.99 = bf16[128,128]{1,0:T(8,128)(2,1)} custom-call(f32[128,128]{1,0:T(8,128)S(1)} %copy-done.2, s32[1024,128]{1,0:T(8,128)S(1)} %bitcast.25, s32[8,128]{1,0:T(8,128)S(1)} %bitcast.29), custom_call_target="tpu_custom_call" | custom-call | flops 67108864 | bytes 524288 | tf_op jit(solution)/shard_map/pallas_call | solution.py:397
  93.1 3.1 %all-to-all-done.3 = f32[4,16,128]{2,1,0:T(8,128)S(1)} async-done(((f32[4,16,128]{2,1,0:T(8,128)}), f32[4,16,128]{2,1,0:T(8,128)S(1)}, u32[]{:S(2)}, u32[]{:S(2)}) %all-to-all-start.3) | async-done | bytes 32800 | tf_op jit(solution)/shard_map/all_to_all | solution.py:396
  96.3 0.1 mul.17
  96.4 0.6 copy.13
  (7 shorter events, 0.1 us)
Async XLA Ops:
  2.9 42.2 %copy-start.5 = (bf16[1,128,256]{2,1,0:T(8,128)(2,1)S(1)}, bf16[1,128,256]{2,1,0:T(8,128)(2,1)}, u32[]{:S(2)}) copy-start(bf16[1,128,256]{2,1,0:T(8,128)(2,1)} %param.7) | copy-start | bytes 196612
  2.9 32.8 %all-to-all-start = ((bf16[128,8,128]{2,1,0:T(8,128)(2,1)}), bf16[128,8,128]{2,1,0:T(8,128)(2,1)S(1)}, u32[]{:S(2)}, u32[]{:S(2)}) async-start(bf16[128,8,128]{2,1,0:T(8,128)(2,1)} %bitcast.30), calls=%async_computation | async-start | bytes 524288 | tf_op jit(solution)/shard_map/all_to_all | solution.py:335
  21.5 17.4 %collective-permute-start = (bf16[128,256]{1,0:T(8,128)(2,1)}, bf16[128,256]{1,0:T(8,128)(2,1)S(1)}, u32[]{:S(2)}, u32[]{:S(2)}) collective-permute-start(bf16[128,256]{1,0:T(8,128)(2,1)} %bitcast.36), channel_id=1, source_target_pairs={{0,1},{1,0},{2,3},{3,2},{4,5},{5,4},{6,7},{7,6},{8,9},{9,8},{10,11... | collective-permute-start | bytes 196616 | tf_op jit(solution)/shard_map/ppermute | solution.py:339
  24.6 14.3 %collective-permute-start.1 = (bf16[128,256]{1,0:T(8,128)(2,1)}, bf16[128,256]{1,0:T(8,128)(2,1)S(1)}, u32[]{:S(2)}, u32[]{:S(2)}) collective-permute-start(bf16[128,256]{1,0:T(8,128)(2,1)} %bitcast.37), channel_id=1, source_target_pairs={{0,2},{1,3},{2,0},{3,1},{4,6},{5,7},{6,4},{7,5},{8,10},{9,11},{10,... | collective-permute-start | bytes 196616 | tf_op jit(solution)/shard_map/ppermute | solution.py:339
  29.0 10.0 %collective-permute-start.2 = (bf16[128,256]{1,0:T(8,128)(2,1)}, bf16[128,256]{1,0:T(8,128)(2,1)S(1)}, u32[]{:S(2)}, u32[]{:S(2)}) collective-permute-start(bf16[128,256]{1,0:T(8,128)(2,1)} %bitcast.38), channel_id=1, source_target_pairs={{0,3},{1,2},{2,1},{3,0},{4,7},{5,6},{6,5},{7,4},{8,11},{9,10},{10,... | collective-permute-start | bytes 196616 | tf_op jit(solution)/shard_map/ppermute | solution.py:339
  31.1 0.8 copy-start.3
  31.9 15.1 %copy-start = (bf16[27,256,128]{2,1,0:T(8,128)(2,1)S(1)}, bf16[27,256,128]{2,1,0:T(8,128)(2,1)}, u32[]{:S(2)}) copy-start(bf16[27,256,128]{2,1,0:T(8,128)(2,1)} %w_any.1) | copy-start | bytes 5308420
  38.9 19.3 %all-to-all-start.1 = ((bf16[8,432,128]{2,1,0:T(8,128)(2,1)}), bf16[8,432,128]{2,1,0:T(8,128)(2,1)S(1)}, u32[]{:S(2)}, u32[]{:S(2)}) async-start(bf16[8,432,128]{2,1,0:T(8,128)(2,1)} %bitcast.11), calls=%async_computation.1 | async-start | bytes 1769472 | tf_op jit(solution)/shard_map/all_to_all | solution.py:357
  45.1 8.3 %collective-permute-start.3 = (bf16[4,128,256]{2,1,0:T(8,128)(2,1)S(1)}, bf16[4,128,256]{2,1,0:T(8,128)(2,1)S(1)}, u32[]{:S(2)}, u32[]{:S(2)}) collective-permute-start(bf16[4,128,256]{2,1,0:T(8,128)(2,1)S(1)} %pad_maximum_fusion.near_ref), channel_id=1, source_target_pairs={{0,4},{4,0},{1,5},{5,1},{2,6},{6,2},{3,7},{7,3},{8,12},{12,8},{9,1... | collective-permute-start | bytes 786440 | tf_op jit(solution)/shard_map/ppermute | solution.py:380
  52.8 0.6 copy-start.1
  58.3 33.7 %copy-start.2 = (f32[128,128]{1,0:T(8,128)S(1)}, f32[128,128]{1,0:T(8,128)}, u32[]{:S(2)}) copy-start(f32[128,128]{1,0:T(8,128)} %copy-done.1) | copy-start | bytes 196612
  58.3 33.7 %copy-start.4 = (s32[1,1,1024]{2,1,0:T(1,128)S(1)}, s32[1,1,1024]{2,1,0:T(1,128)}, u32[]{:S(2)}) copy-start(s32[1,1,1024]{2,1,0:T(1,128)} %param.13) | copy-start | bytes 12292
  88.7 7.5 %all-to-all-start.3 = ((f32[4,16,128]{2,1,0:T(8,128)}), f32[4,16,128]{2,1,0:T(8,128)S(1)}, u32[]{:S(2)}, u32[]{:S(2)}) async-start(f32[4,16,128]{2,1,0:T(8,128)} %shard_map.100), calls=%async_computation.3 | async-start | bytes 65536 | tf_op jit(solution)/shard_map/all_to_all | solution.py:396

commit v12 on v11

--- a/solution.py
+++ b/solution.py
@@ -335,13 +335,14 @@
     returned = lax.all_to_all(outgoing.reshape(peers, slots, out_width), SPACE, 0, 0, tiled=True)
 
     swap = [(0, 1), (1, 0)]
-    ring = [
-        lax.ppermute(own_x, "scene", [(i, i ^ d) for i in range(scenes)]) for d in range(1, scenes)
-    ]
-
+    one, two = ([(i, i ^ d) for i in range(scenes)] for d in (1, 2))
+    beside = lax.ppermute(own_x, "scene", one)
     table, turned = call(
         table_kernel, (shape((32, own_rows), I32), shape((out_width, own_rows), BF16))
     )(shared)
+    beside, table, turned = lax.optimization_barrier((beside, table, turned))
+    pair = jnp.stack([own_x, beside])
+    other = lax.ppermute(pair, "scene", two)
     gathered = call(
         lookup_kernel,
         shape((offsets * out_width, own_rows), BF16),
@@ -353,10 +354,10 @@
         ),
         out_specs=hbm,
     )(turned, returned.reshape(send_rows, out_width), table)
-    gathered, *ring = lax.optimization_barrier((gathered, *ring))
+    gathered, pair, other = lax.optimization_barrier((gathered, pair, other))
     group_g = lax.all_to_all(gathered.reshape(group, columns, own_rows), GROUP, 0, 0, tiled=True)
 
-    near = jnp.stack([x] + ring)
+    near = jnp.concatenate([pair, other])
     own, words, input_grad = call(
         functools.partial(forward_kernel, free=free),
         (

time: 98.6 us -> 99.3 us (level)
  starting transfers between devices: 39.4 us -> 37.6 us
    ppermute x3 -> x2, starting transfers between devices: 9.59 us -> 7.92 us  [the longest x1 4.79 us: local(): other = lax.ppermute(pair, 'scene', two)]
    ppermute x3 -> x2, waiting for transfers between devices: 0.01 us -> 1.57 us  [the longest x1 1.57 us: local(): beside = lax.ppermute(own_x, 'scene', one)]
    unnamed x14 -> x13, local copies, waits for them, and re-layouts: 2.06 us -> 2.06 us
  transfers between devices with their start and end apart: 7 -> 6, of which waited for: 3 -> 4; matrix products, arithmetic and copies ran while one was open for 0% -> 1% of each run, Pallas kernels for 10% -> 10%
where the time goes in v12:
time: 99.3 us; the launch traced here: 97.8 us
  starting transfers between devices  37.6 us (38%)
  blocking collectives  29.8 us (30%)
  Pallas kernels  13.8 us (14%)
  waiting for transfers between devices  12.6 us (13%)
  local copies, waits for them, and re-layouts  2.2 us (2%)
    all_to_all x1, blocking collectives, local(): lax.all_to_all(packed.reshape(peers, WORDS, LANES), SPACE, 0, 0, tiled=True)  29.8 us
    all_to_all x1, starting transfers between devices, local(): lax.all_to_all(outgoing.reshape(peers, slots, out_width), SPACE, 0, 0, ti...  18.4 us
    all_to_all x1, starting transfers between devices, local(): lax.all_to_all(gathered.reshape(group, columns, own_rows), GROUP, 0, 0, t...  6.11 us
    pallas_call x1, Pallas kernels, local(): call(functools.partial(forward_kernel, free=free), (shape((own_rows, out_...  5.77 us
    all_to_all x1, waiting for transfers between devices, local(): lax.all_to_all(gathered.reshape(group, columns, own_rows), GROUP, 0, 0, t...  4.85 us
    ppermute x1, starting transfers between devices, local(): other = lax.ppermute(pair, 'scene', two)  4.79 us
    all_to_all x1, starting transfers between devices, local(): sums = lax.all_to_all(quarter, 'scene', 0, 0, tiled=True)  3.26 us
    pallas_call x1, Pallas kernels, local(): call(lookup_kernel, shape((offsets * out_width, own_rows), BF16), scratch...  3.2 us
  transfers between devices with their start and end apart: 6, of which 4 were waited for; matrix products, arithmetic and copies ran while one was open for 1% of the time, Pallas kernels for 10%

profile of v12, /device:TPU:1, one launch (start us, length us, event | category | flops | bytes accessed | tf_op | source)
XLA Modules:
  0.0 97.8 jit_solution(14779803617867779485)
XLA Ops:
  0.6 2.2 %shard_map.94 = (bf16[192,128]{1,0:T(8,128)(2,1)}, bf16[1024,128]{1,0:T(8,128)(2,1)}) custom-call(bf16[128,128]{1,0:T(8,128)(2,1)} %bitcast.39, s32[128,128]{1,0:T(8,128)} %bitcast.34, s32[8,128]{1,0:T(8,128)} %bitcast.27, s32[27,1,128]{2,1,0:T(1,128)} %bitcast.40, s32[27,1,128]{2,1,0:T(1,128)} %bitcast.41), custom_call_target="tpu_custom_call" | custom-call | flops 33554432 | bytes 393216 | tf_op jit(solution)/shard_map/pallas_call | solution.py:317
  2.9 18.4 %all-to-all-start = ((bf16[128,8,128]{2,1,0:T(8,128)(2,1)}), bf16[128,8,128]{2,1,0:T(8,128)(2,1)S(1)}, u32[]{:S(2)}, u32[]{:S(2)}) async-start(bf16[128,8,128]{2,1,0:T(8,128)(2,1)} %bitcast.29), calls=%async_computation | async-start | bytes 524288 | tf_op jit(solution)/shard_map/all_to_all | solution.py:335
  21.3 3.1 %collective-permute-start = (bf16[128,256]{1,0:T(8,128)(2,1)}, bf16[128,256]{1,0:T(8,128)(2,1)S(1)}, u32[]{:S(2)}, u32[]{:S(2)}) collective-permute-start(bf16[128,256]{1,0:T(8,128)(2,1)} %bitcast.35), channel_id=1, source_target_pairs={{0,1},{1,0},{2,3},{3,2},{4,5},{5,4},{6,7},{7,6},{8,9},{9,8},{10,11... | collective-permute-start | bytes 196616 | tf_op jit(solution)/shard_map/ppermute | solution.py:339
  24.5 0.0 copy-start.3
  24.5 0.8 copy-done.3
  25.3 1.6 %collective-permute-done = bf16[128,256]{1,0:T(8,128)(2,1)S(1)} collective-permute-done((bf16[128,256]{1,0:T(8,128)(2,1)}, bf16[128,256]{1,0:T(8,128)(2,1)S(1)}, u32[]{:S(2)}, u32[]{:S(2)}) %collective-permute-start) | collective-permute-done | bytes 65568 | tf_op jit(solution)/shard_map/ppermute | solution.py:339
  26.8 0.9 pad_maximum_fusion
  27.7 0.0 copy-start
  27.7 4.8 %collective-permute-start.1 = (bf16[2,128,256]{2,1,0:T(8,128)(2,1)S(1)}, bf16[2,128,256]{2,1,0:T(8,128)(2,1)S(1)}, u32[]{:S(2)}, u32[]{:S(2)}) collective-permute-start(bf16[2,128,256]{2,1,0:T(8,128)(2,1)S(1)} %pad_maximum_fusion), channel_id=1, source_target_pairs={{0,2},{1,3},{2,0},{3,1},{4,6},{5,7},{6,4},{7,5},{8,10},{9,11},{10,... | collective-permute-start | bytes 393224 | tf_op jit(solution)/shard_map/ppermute | solution.py:345
  32.5 3.0 %all-to-all-done = bf16[128,8,128]{2,1,0:T(8,128)(2,1)S(1)} async-done(((bf16[128,8,128]{2,1,0:T(8,128)(2,1)}), bf16[128,8,128]{2,1,0:T(8,128)(2,1)S(1)}, u32[]{:S(2)}, u32[]{:S(2)}) %all-to-all-start) | async-done | bytes 262176 | tf_op jit(solution)/shard_map/all_to_all | solution.py:335
  35.6 3.2 %shard_map.96.gathered_any = bf16[3456,128]{1,0:T(8,128)(2,1)} custom-call(bf16[128,128]{1,0:T(8,128)(2,1)S(1)} %get-tuple-element.23.turned_ref, bf16[1024,128]{1,0:T(8,128)(2,1)S(1)} %bitcast.26, s32[32,128]{1,0:T(8,128)S(1)} %get-tuple-element.25.table_ref), custom_call_target="tpu_custom_call" | custom-call | tf_op jit(solution)/shard_map/pallas_call | solution.py:346
  38.8 0.0 collective-permute-done.1
  38.8 6.1 %all-to-all-start.1 = ((bf16[8,432,128]{2,1,0:T(8,128)(2,1)}), bf16[8,432,128]{2,1,0:T(8,128)(2,1)S(1)}, u32[]{:S(2)}, u32[]{:S(2)}) async-start(bf16[8,432,128]{2,1,0:T(8,128)(2,1)} %bitcast.10), calls=%async_computation.1 | async-start | bytes 1769472 | tf_op jit(solution)/shard_map/all_to_all | solution.py:358
  44.9 1.9 %collective-permute-start.2 = (bf16[4,128,256]{2,1,0:T(8,128)(2,1)S(1)}, bf16[4,128,256]{2,1,0:T(8,128)(2,1)S(1)}, u32[]{:S(2)}, u32[]{:S(2)}) collective-permute-start(bf16[4,128,256]{2,1,0:T(8,128)(2,1)S(1)} %constant_dynamic-update-slice_fusion.near_ref), channel_id=1, source_target_pairs={{0,4},{4,0},{1,5},{5,1},{2,6},{6,2},{3,7},{7,3},{8,12},{12,8},{9,1... | collective-permute-start | bytes 786440 | tf_op jit(solution)/shard_map/ppermute | solution.py:381
  46.8 0.0 copy-done
  46.8 5.8 %shard_map.97 = (f32[128,128]{1,0:T(8,128)S(1)}, s32[5,128,128]{2,1,0:T(8,128)S(1)}, bf16[128,256]{1,0:T(8,128)(2,1)}) custom-call(bf16[4,128,256]{2,1,0:T(8,128)(2,1)S(1)} %constant_dynamic-update-slice_fusion.near_ref, bf16[27,256,128]{2,1,0:T(8,128)(2,1)S(1)} %copy-done, s32[32,128]{1,0:T(8,128)S(1)} %get-tuple-element.25.table_ref, ...), custom_call_target="tpu_custom_call" | custom-call | tf_op jit(solution)/shard_map/pallas_call | solution.py:361
  52.6 0.0 copy-start.1
  52.6 0.6 copy-done.1
  53.3 0.0 collective-permute-done.2.far_ref
  53.3 4.9 %all-to-all-done.1.g_ref = bf16[8,432,128]{2,1,0:T(8,128)(2,1)S(1)} async-done(((bf16[8,432,128]{2,1,0:T(8,128)(2,1)}), bf16[8,432,128]{2,1,0:T(8,128)(2,1)S(1)}, u32[]{:S(2)}, u32[]{:S(2)}) %all-to-all-start.1) | async-done | bytes 884768 | tf_op jit(solution)/shard_map/all_to_all | solution.py:358
  58.1 0.0 copy-start.2
  58.1 0.0 copy-start.4
  58.1 0.7 shard_map.98
  58.9 29.8 %all_to_all.20 = s32[128,8,128]{2,1,0:T(8,128)S(1)} all-to-all(s32[128,8,128]{2,1,0:T(8,128)S(1)} %bitcast.25), channel_id=1, replica_groups=mesh['y'=8,'z'=8,'core'=2,'scene'=4] {'y','z','core'}, dimensions={0} | all-to-all | bytes 1048576 | tf_op jit(solution)/shard_map/all_to_all | solution.py:389
  88.7 0.7 shard_map.100
  89.4 3.3 %all-to-all-start.3 = ((f32[4,16,128]{2,1,0:T(8,128)}), f32[4,16,128]{2,1,0:T(8,128)S(1)}, u32[]{:S(2)}, u32[]{:S(2)}) async-start(f32[4,16,128]{2,1,0:T(8,128)} %shard_map.100), calls=%async_computation.3 | async-start | bytes 65536 | tf_op jit(solution)/shard_map/all_to_all | solution.py:397
  92.7 0.0 copy-done.2
  92.7 0.0 copy-done.4
  92.7 1.1 %shard_map.99 = bf16[128,128]{1,0:T(8,128)(2,1)} custom-call(f32[128,128]{1,0:T(8,128)S(1)} %copy-done.2, s32[1024,128]{1,0:T(8,128)S(1)} %bitcast.24, s32[8,128]{1,0:T(8,128)S(1)} %bitcast.28), custom_call_target="tpu_custom_call" | custom-call | flops 67108864 | bytes 524288 | tf_op jit(solution)/shard_map/pallas_call | solution.py:398
  93.9 3.1 %all-to-all-done.3 = f32[4,16,128]{2,1,0:T(8,128)S(1)} async-done(((f32[4,16,128]{2,1,0:T(8,128)}), f32[4,16,128]{2,1,0:T(8,128)S(1)}, u32[]{:S(2)}, u32[]{:S(2)}) %all-to-all-start.3) | async-done | bytes 32800 | tf_op jit(solution)/shard_map/all_to_all | solution.py:397
  97.0 0.1 mul.17
  97.2 0.6 copy.13
  (8 shorter events, 0.1 us)
Async XLA Ops:
  2.9 32.7 %all-to-all-start = ((bf16[128,8,128]{2,1,0:T(8,128)(2,1)}), bf16[128,8,128]{2,1,0:T(8,128)(2,1)S(1)}, u32[]{:S(2)}, u32[]{:S(2)}) async-start(bf16[128,8,128]{2,1,0:T(8,128)(2,1)} %bitcast.29), calls=%async_computation | async-start | bytes 524288 | tf_op jit(solution)/shard_map/all_to_all | solution.py:335
  21.3 5.5 %collective-permute-start = (bf16[128,256]{1,0:T(8,128)(2,1)}, bf16[128,256]{1,0:T(8,128)(2,1)S(1)}, u32[]{:S(2)}, u32[]{:S(2)}) collective-permute-start(bf16[128,256]{1,0:T(8,128)(2,1)} %bitcast.35), channel_id=1, source_target_pairs={{0,1},{1,0},{2,3},{3,2},{4,5},{5,4},{6,7},{7,6},{8,9},{9,8},{10,11... | collective-permute-start | bytes 196616 | tf_op jit(solution)/shard_map/ppermute | solution.py:339
  24.5 0.8 copy-start.3
  27.7 19.1 %copy-start = (bf16[27,256,128]{2,1,0:T(8,128)(2,1)S(1)}, bf16[27,256,128]{2,1,0:T(8,128)(2,1)}, u32[]{:S(2)}) copy-start(bf16[27,256,128]{2,1,0:T(8,128)(2,1)} %w_any.1) | copy-start | bytes 5308420
  27.7 11.1 %collective-permute-start.1 = (bf16[2,128,256]{2,1,0:T(8,128)(2,1)S(1)}, bf16[2,128,256]{2,1,0:T(8,128)(2,1)S(1)}, u32[]{:S(2)}, u32[]{:S(2)}) collective-permute-start(bf16[2,128,256]{2,1,0:T(8,128)(2,1)S(1)} %pad_maximum_fusion), channel_id=1, source_target_pairs={{0,2},{1,3},{2,0},{3,1},{4,6},{5,7},{6,4},{7,5},{8,10},{9,11},{10,... | collective-permute-start | bytes 393224 | tf_op jit(solution)/shard_map/ppermute | solution.py:345
  38.8 19.3 %all-to-all-start.1 = ((bf16[8,432,128]{2,1,0:T(8,128)(2,1)}), bf16[8,432,128]{2,1,0:T(8,128)(2,1)S(1)}, u32[]{:S(2)}, u32[]{:S(2)}) async-start(bf16[8,432,128]{2,1,0:T(8,128)(2,1)} %bitcast.10), calls=%async_computation.1 | async-start | bytes 1769472 | tf_op jit(solution)/shard_map/all_to_all | solution.py:358
  44.9 8.3 %collective-permute-start.2 = (bf16[4,128,256]{2,1,0:T(8,128)(2,1)S(1)}, bf16[4,128,256]{2,1,0:T(8,128)(2,1)S(1)}, u32[]{:S(2)}, u32[]{:S(2)}) collective-permute-start(bf16[4,128,256]{2,1,0:T(8,128)(2,1)S(1)} %constant_dynamic-update-slice_fusion.near_ref), channel_id=1, source_target_pairs={{0,4},{4,0},{1,5},{5,1},{2,6},{6,2},{3,7},{7,3},{8,12},{12,8},{9,1... | collective-permute-start | bytes 786440 | tf_op jit(solution)/shard_map/ppermute | solution.py:381
  52.6 0.6 copy-start.1
  58.1 34.6 %copy-start.2 = (f32[128,128]{1,0:T(8,128)S(1)}, f32[128,128]{1,0:T(8,128)}, u32[]{:S(2)}) copy-start(f32[128,128]{1,0:T(8,128)} %copy-done.1) | copy-start | bytes 196612
  58.1 34.6 %copy-start.4 = (s32[1,1,1024]{2,1,0:T(1,128)S(1)}, s32[1,1,1024]{2,1,0:T(1,128)}, u32[]{:S(2)}) copy-start(s32[1,1,1024]{2,1,0:T(1,128)} %param.13) | copy-start | bytes 12292
  89.4 7.5 %all-to-all-start.3 = ((f32[4,16,128]{2,1,0:T(8,128)}), f32[4,16,128]{2,1,0:T(8,128)S(1)}, u32[]{:S(2)}, u32[]{:S(2)}) async-start(f32[4,16,128]{2,1,0:T(8,128)} %shard_map.100), calls=%async_computation.3 | async-start | bytes 65536 | tf_op jit(solution)/shard_map/all_to_all | solution.py:397

commit v13 on v11

--- a/solution.py
+++ b/solution.py
@@ -271,9 +271,10 @@
         for c, value in enumerate(halves(words[h])):
             total = (value * scale).reshape(peers // 8, 8, LANES).sum(axis=0)
             total = (total[0:2] + total[2:4]) + (total[4:6] + total[6:8])
-            row = 2 * (4 * c + h)
-            for s in range(out_ref.shape[0]):
-                out_ref[s, row : row + 2, :] = total
+            for core in range(2):
+                row = 4 * (2 * c + core) + h
+                for s in range(out_ref.shape[0]):
+                    out_ref[s, row : row + 1, :] = total[core : core + 1]
 
 
 def receive_kernel(own_ref, arrived_ref, recv_ref, out_ref, rows_ref, *, free):
@@ -403,10 +404,10 @@
     )(own, arrived, recv)
 
     own_in = in_width // peers
-    sums = sums.reshape(scenes, own_in, blocks, 2, LANES).transpose(1, 3, 0, 2, 4)
+    sums = sums.reshape(scenes, own_in, 2, blocks, LANES).transpose(1, 2, 0, 3, 4)
     sums = sums.reshape(own_in, group, blocks * LANES)[:, :, :columns]
     kernel_grad = sums.reshape(own_in, offsets, out_width)
-    kernel_grad = kernel_grad.transpose(1, 0, 2).reshape(offsets, own_in * out_width)
+    kernel_grad = jnp.concatenate([kernel_grad[c] for c in range(own_in)], axis=1)
     normalizer = 1.0 / math.sqrt(scenes * peers * own_rows)
     return (conv_out[None], input_grad[None], kernel_grad * normalizer)
 

time: 98.6 us -> 98.6 us (level)
    unnamed x14 -> x12, local copies, waits for them, and re-layouts: 2.06 us -> 1.42 us
where the time goes in v13:
time: 98.6 us; the launch traced here: 97.1 us
  starting transfers between devices  39.4 us (40%)
  blocking collectives  28.9 us (29%)
  Pallas kernels  13.8 us (14%)
  waiting for transfers between devices  11.8 us (12%)
  local copies, waits for them, and re-layouts  1.61 us (2%)
    all_to_all x1, blocking collectives, local(): lax.all_to_all(packed.reshape(peers, WORDS, LANES), SPACE, 0, 0, tiled=True)  28.9 us
    all_to_all x1, starting transfers between devices, local(): lax.all_to_all(outgoing.reshape(peers, slots, out_width), SPACE, 0, 0, ti...  18.6 us
    ppermute x3, starting transfers between devices, local(): lax.ppermute(own_x, 'scene', [(i, i ^ d) for i in range(scenes)])  9.59 us
    all_to_all x1, starting transfers between devices, local(): lax.all_to_all(gathered.reshape(group, columns, own_rows), GROUP, 0, 0, t...  6.11 us
    pallas_call x1, Pallas kernels, local(): call(functools.partial(forward_kernel, free=free), (shape((own_rows, out_...  5.77 us
    all_to_all x1, waiting for transfers between devices, local(): lax.all_to_all(gathered.reshape(group, columns, own_rows), GROUP, 0, 0, t...  4.85 us
    all_to_all x1, waiting for transfers between devices, local(): lax.all_to_all(outgoing.reshape(peers, slots, out_width), SPACE, 0, 0, ti...  3.8 us
    all_to_all x1, starting transfers between devices, local(): sums = lax.all_to_all(quarter, 'scene', 0, 0, tiled=True)  3.26 us
  transfers between devices with their start and end apart: 7, of which 3 were waited for; matrix products, arithmetic and copies ran while one was open for 0% of the time, Pallas kernels for 10%

profile of v13, /device:TPU:1, one launch (start us, length us, event | category | flops | bytes accessed | tf_op | source)
XLA Modules:
  0.0 97.1 jit_solution(6141338672183448499)
XLA Ops:
  0.6 2.2 %shard_map.94 = (bf16[192,128]{1,0:T(8,128)(2,1)}, bf16[1024,128]{1,0:T(8,128)(2,1)}) custom-call(bf16[128,128]{1,0:T(8,128)(2,1)} %bitcast.37, s32[128,128]{1,0:T(8,128)} %bitcast.29, s32[8,128]{1,0:T(8,128)} %bitcast.24, s32[27,1,128]{2,1,0:T(1,128)} %bitcast.38, s32[27,1,128]{2,1,0:T(1,128)} %bitcast.39), custom_call_target="tpu_custom_call" | custom-call | flops 33554432 | bytes 393216 | tf_op jit(solution)/shard_map/pallas_call | solution.py:318
  2.9 0.0 copy-start.5
  2.9 18.6 %all-to-all-start = ((bf16[128,8,128]{2,1,0:T(8,128)(2,1)}), bf16[128,8,128]{2,1,0:T(8,128)(2,1)S(1)}, u32[]{:S(2)}, u32[]{:S(2)}) async-start(bf16[128,8,128]{2,1,0:T(8,128)(2,1)} %bitcast.26), calls=%async_computation | async-start | bytes 524288 | tf_op jit(solution)/shard_map/all_to_all | solution.py:336
  21.5 3.1 %collective-permute-start = (bf16[128,256]{1,0:T(8,128)(2,1)}, bf16[128,256]{1,0:T(8,128)(2,1)S(1)}, u32[]{:S(2)}, u32[]{:S(2)}) collective-permute-start(bf16[128,256]{1,0:T(8,128)(2,1)} %bitcast.30), channel_id=1, source_target_pairs={{0,1},{1,0},{2,3},{3,2},{4,5},{5,4},{6,7},{7,6},{8,9},{9,8},{10,11... | collective-permute-start | bytes 196616 | tf_op jit(solution)/shard_map/ppermute | solution.py:340
  24.6 4.4 %collective-permute-start.1 = (bf16[128,256]{1,0:T(8,128)(2,1)}, bf16[128,256]{1,0:T(8,128)(2,1)S(1)}, u32[]{:S(2)}, u32[]{:S(2)}) collective-permute-start(bf16[128,256]{1,0:T(8,128)(2,1)} %bitcast.31), channel_id=1, source_target_pairs={{0,2},{1,3},{2,0},{3,1},{4,6},{5,7},{6,4},{7,5},{8,10},{9,11},{10,... | collective-permute-start | bytes 196616 | tf_op jit(solution)/shard_map/ppermute | solution.py:340
  29.0 2.1 %collective-permute-start.2 = (bf16[128,256]{1,0:T(8,128)(2,1)}, bf16[128,256]{1,0:T(8,128)(2,1)S(1)}, u32[]{:S(2)}, u32[]{:S(2)}) collective-permute-start(bf16[128,256]{1,0:T(8,128)(2,1)} %bitcast.32), channel_id=1, source_target_pairs={{0,3},{1,2},{2,1},{3,0},{4,7},{5,6},{6,5},{7,4},{8,11},{9,10},{10,... | collective-permute-start | bytes 196616 | tf_op jit(solution)/shard_map/ppermute | solution.py:340
  31.1 0.0 copy-start.3
  31.1 0.8 copy-done.3
  31.9 0.0 copy-start
  31.9 3.8 %all-to-all-done = bf16[128,8,128]{2,1,0:T(8,128)(2,1)S(1)} async-done(((bf16[128,8,128]{2,1,0:T(8,128)(2,1)}), bf16[128,8,128]{2,1,0:T(8,128)(2,1)S(1)}, u32[]{:S(2)}, u32[]{:S(2)}) %all-to-all-start) | async-done | bytes 262176 | tf_op jit(solution)/shard_map/all_to_all | solution.py:336
  35.7 3.2 %shard_map.96.gathered_any = bf16[3456,128]{1,0:T(8,128)(2,1)} custom-call(bf16[128,128]{1,0:T(8,128)(2,1)S(1)} %get-tuple-element.17.turned_ref, bf16[1024,128]{1,0:T(8,128)(2,1)S(1)} %bitcast.23, s32[32,128]{1,0:T(8,128)S(1)} %get-tuple-element.20.table_ref), custom_call_target="tpu_custom_call" | custom-call | tf_op jit(solution)/shard_map/pallas_call | solution.py:346
  38.9 0.0 collective-permute-done
  38.9 0.0 collective-permute-done.1
  38.9 0.0 collective-permute-done.2
  38.9 6.1 %all-to-all-start.1 = ((bf16[8,432,128]{2,1,0:T(8,128)(2,1)}), bf16[8,432,128]{2,1,0:T(8,128)(2,1)S(1)}, u32[]{:S(2)}, u32[]{:S(2)}) async-start(bf16[8,432,128]{2,1,0:T(8,128)(2,1)} %bitcast.11), calls=%async_computation.1 | async-start | bytes 1769472 | tf_op jit(solution)/shard_map/all_to_all | solution.py:358
  45.0 0.0 copy-done.5
  45.1 1.9 %collective-permute-start.3 = (bf16[4,128,256]{2,1,0:T(8,128)(2,1)S(1)}, bf16[4,128,256]{2,1,0:T(8,128)(2,1)S(1)}, u32[]{:S(2)}, u32[]{:S(2)}) collective-permute-start(bf16[4,128,256]{2,1,0:T(8,128)(2,1)S(1)} %pad_maximum_fusion.near_ref), channel_id=1, source_target_pairs={{0,4},{4,0},{1,5},{5,1},{2,6},{6,2},{3,7},{7,3},{8,12},{12,8},{9,1... | collective-permute-start | bytes 786440 | tf_op jit(solution)/shard_map/ppermute | solution.py:381
  47.0 0.0 copy-done
  47.0 5.8 %shard_map.97 = (f32[128,128]{1,0:T(8,128)S(1)}, s32[5,128,128]{2,1,0:T(8,128)S(1)}, bf16[128,256]{1,0:T(8,128)(2,1)}) custom-call(bf16[4,128,256]{2,1,0:T(8,128)(2,1)S(1)} %pad_maximum_fusion.near_ref, bf16[27,256,128]{2,1,0:T(8,128)(2,1)S(1)} %copy-done, s32[32,128]{1,0:T(8,128)S(1)} %get-tuple-element.20.table_ref, bf16[3456,128]{1,0:T(8,128)(2,1)} %shard_map.96.gathered_any), custom_call_target="tpu_custom_call" | custom-call | tf_op jit(solution)/shard_map/pallas_call | solution.py:361
  52.8 0.0 copy-start.1
  52.8 0.6 copy-done.1
  53.4 0.0 collective-permute-done.3.far_ref
  53.4 4.8 %all-to-all-done.1.g_ref = bf16[8,432,128]{2,1,0:T(8,128)(2,1)S(1)} async-done(((bf16[8,432,128]{2,1,0:T(8,128)(2,1)}), bf16[8,432,128]{2,1,0:T(8,128)(2,1)S(1)}, u32[]{:S(2)}, u32[]{:S(2)}) %all-to-all-start.1) | async-done | bytes 884768 | tf_op jit(solution)/shard_map/all_to_all | solution.py:358
  58.3 0.0 copy-start.2
  58.3 0.0 copy-start.4
  58.3 0.7 shard_map.98
  59.0 28.9 %all_to_all.20 = s32[128,8,128]{2,1,0:T(8,128)S(1)} all-to-all(s32[128,8,128]{2,1,0:T(8,128)S(1)} %bitcast.22), channel_id=1, replica_groups=mesh['y'=8,'z'=8,'core'=2,'scene'=4] {'y','z','core'}, dimensions={0} | all-to-all | bytes 1048576 | tf_op jit(solution)/shard_map/all_to_all | solution.py:389
  87.9 0.8 shard_map.100
  88.7 3.3 %all-to-all-start.3 = ((f32[4,16,128]{2,1,0:T(8,128)}), f32[4,16,128]{2,1,0:T(8,128)S(1)}, u32[]{:S(2)}, u32[]{:S(2)}) async-start(f32[4,16,128]{2,1,0:T(8,128)} %shard_map.100), calls=%async_computation.3 | async-start | bytes 65536 | tf_op jit(solution)/shard_map/all_to_all | solution.py:397
  92.0 0.0 copy-done.2
  92.0 0.0 copy-done.4
  92.0 1.1 %shard_map.99 = bf16[128,128]{1,0:T(8,128)(2,1)} custom-call(f32[128,128]{1,0:T(8,128)S(1)} %copy-done.2, s32[1024,128]{1,0:T(8,128)S(1)} %bitcast.21, s32[8,128]{1,0:T(8,128)S(1)} %bitcast.25), custom_call_target="tpu_custom_call" | custom-call | flops 67108864 | bytes 524288 | tf_op jit(solution)/shard_map/pallas_call | solution.py:398
  93.1 3.1 %all-to-all-done.3 = f32[4,16,128]{2,1,0:T(8,128)S(1)} async-done(((f32[4,16,128]{2,1,0:T(8,128)}), f32[4,16,128]{2,1,0:T(8,128)S(1)}, u32[]{:S(2)}, u32[]{:S(2)}) %all-to-all-start.3) | async-done | bytes 32800 | tf_op jit(solution)/shard_map/all_to_all | solution.py:397
  96.3 0.1 squeeze.19
  96.3 0.1 squeeze.18
  96.4 0.6 maximum_multiply_fusion
  (5 shorter events, 0.1 us)
Async XLA Ops:
  2.9 42.2 %copy-start.5 = (bf16[1,128,256]{2,1,0:T(8,128)(2,1)S(1)}, bf16[1,128,256]{2,1,0:T(8,128)(2,1)}, u32[]{:S(2)}) copy-start(bf16[1,128,256]{2,1,0:T(8,128)(2,1)} %param.7) | copy-start | bytes 196612
  2.9 32.8 %all-to-all-start = ((bf16[128,8,128]{2,1,0:T(8,128)(2,1)}), bf16[128,8,128]{2,1,0:T(8,128)(2,1)S(1)}, u32[]{:S(2)}, u32[]{:S(2)}) async-start(bf16[128,8,128]{2,1,0:T(8,128)(2,1)} %bitcast.26), calls=%async_computation | async-start | bytes 524288 | tf_op jit(solution)/shard_map/all_to_all | solution.py:336
  21.5 17.4 %collective-permute-start = (bf16[128,256]{1,0:T(8,128)(2,1)}, bf16[128,256]{1,0:T(8,128)(2,1)S(1)}, u32[]{:S(2)}, u32[]{:S(2)}) collective-permute-start(bf16[128,256]{1,0:T(8,128)(2,1)} %bitcast.30), channel_id=1, source_target_pairs={{0,1},{1,0},{2,3},{3,2},{4,5},{5,4},{6,7},{7,6},{8,9},{9,8},{10,11... | collective-permute-start | bytes 196616 | tf_op jit(solution)/shard_map/ppermute | solution.py:340
  24.6 14.3 %collective-permute-start.1 = (bf16[128,256]{1,0:T(8,128)(2,1)}, bf16[128,256]{1,0:T(8,128)(2,1)S(1)}, u32[]{:S(2)}, u32[]{:S(2)}) collective-permute-start(bf16[128,256]{1,0:T(8,128)(2,1)} %bitcast.31), channel_id=1, source_target_pairs={{0,2},{1,3},{2,0},{3,1},{4,6},{5,7},{6,4},{7,5},{8,10},{9,11},{10,... | collective-permute-start | bytes 196616 | tf_op jit(solution)/shard_map/ppermute | solution.py:340
  29.0 10.0 %collective-permute-start.2 = (bf16[128,256]{1,0:T(8,128)(2,1)}, bf16[128,256]{1,0:T(8,128)(2,1)S(1)}, u32[]{:S(2)}, u32[]{:S(2)}) collective-permute-start(bf16[128,256]{1,0:T(8,128)(2,1)} %bitcast.32), channel_id=1, source_target_pairs={{0,3},{1,2},{2,1},{3,0},{4,7},{5,6},{6,5},{7,4},{8,11},{9,10},{10,... | collective-permute-start | bytes 196616 | tf_op jit(solution)/shard_map/ppermute | solution.py:340
  31.1 0.8 copy-start.3
  31.9 15.1 %copy-start = (bf16[27,256,128]{2,1,0:T(8,128)(2,1)S(1)}, bf16[27,256,128]{2,1,0:T(8,128)(2,1)}, u32[]{:S(2)}) copy-start(bf16[27,256,128]{2,1,0:T(8,128)(2,1)} %w_any.1) | copy-start | bytes 5308420
  38.9 19.3 %all-to-all-start.1 = ((bf16[8,432,128]{2,1,0:T(8,128)(2,1)}), bf16[8,432,128]{2,1,0:T(8,128)(2,1)S(1)}, u32[]{:S(2)}, u32[]{:S(2)}) async-start(bf16[8,432,128]{2,1,0:T(8,128)(2,1)} %bitcast.11), calls=%async_computation.1 | async-start | bytes 1769472 | tf_op jit(solution)/shard_map/all_to_all | solution.py:358
  45.1 8.3 %collective-permute-start.3 = (bf16[4,128,256]{2,1,0:T(8,128)(2,1)S(1)}, bf16[4,128,256]{2,1,0:T(8,128)(2,1)S(1)}, u32[]{:S(2)}, u32[]{:S(2)}) collective-permute-start(bf16[4,128,256]{2,1,0:T(8,128)(2,1)S(1)} %pad_maximum_fusion.near_ref), channel_id=1, source_target_pairs={{0,4},{4,0},{1,5},{5,1},{2,6},{6,2},{3,7},{7,3},{8,12},{12,8},{9,1... | collective-permute-start | bytes 786440 | tf_op jit(solution)/shard_map/ppermute | solution.py:381
  52.8 0.6 copy-start.1
  58.3 33.7 %copy-start.2 = (f32[128,128]{1,0:T(8,128)S(1)}, f32[128,128]{1,0:T(8,128)}, u32[]{:S(2)}) copy-start(f32[128,128]{1,0:T(8,128)} %copy-done.1) | copy-start | bytes 196612
  58.3 33.7 %copy-start.4 = (s32[1,1,1024]{2,1,0:T(1,128)S(1)}, s32[1,1,1024]{2,1,0:T(1,128)}, u32[]{:S(2)}) copy-start(s32[1,1,1024]{2,1,0:T(1,128)} %param.13) | copy-start | bytes 12292
  88.7 7.5 %all-to-all-start.3 = ((f32[4,16,128]{2,1,0:T(8,128)}), f32[4,16,128]{2,1,0:T(8,128)S(1)}, u32[]{:S(2)}, u32[]{:S(2)}) async-start(f32[4,16,128]{2,1,0:T(8,128)} %shard_map.100), calls=%async_computation.3 | async-start | bytes 65536 | tf_op jit(solution)/shard_map/all_to_all | solution.py:397

commit v14 on v11

--- a/solution.py
+++ b/solution.py
@@ -13,7 +13,7 @@
 BF16 = jnp.bfloat16
 I32 = jnp.int32
 LANES = 128
-STEP = 4
+STEP = 2
 WORDS = 8
 VMEM_BYTES = 24 * 1024 * 1024
 MOST_VMEM = 64 * 1024 * 1024 - 128 * 1024

time: 98.6 us -> 98.6 us (level)
  no operation moved by 1% of the time
where the time goes in v14:
time: 98.6 us; the launch traced here: 97 us
  starting transfers between devices  39.4 us (40%)
  blocking collectives  29.2 us (30%)
  Pallas kernels  13.6 us (14%)
  waiting for transfers between devices  11.8 us (12%)
  local copies, waits for them, and re-layouts  2.19 us (2%)
    all_to_all x1, blocking collectives, local(): lax.all_to_all(packed.reshape(peers, WORDS, LANES), SPACE, 0, 0, tiled=True)  29.2 us
    all_to_all x1, starting transfers between devices, local(): lax.all_to_all(outgoing.reshape(peers, slots, out_width), SPACE, 0, 0, ti...  18.6 us
    ppermute x3, starting transfers between devices, local(): lax.ppermute(own_x, 'scene', [(i, i ^ d) for i in range(scenes)])  9.59 us
    all_to_all x1, starting transfers between devices, local(): lax.all_to_all(gathered.reshape(group, columns, own_rows), GROUP, 0, 0, t...  6.1 us
    pallas_call x1, Pallas kernels, local(): call(functools.partial(forward_kernel, free=free), (shape((own_rows, out_...  5.77 us
    all_to_all x1, waiting for transfers between devices, local(): lax.all_to_all(gathered.reshape(group, columns, own_rows), GROUP, 0, 0, t...  4.84 us
    all_to_all x1, waiting for transfers between devices, local(): lax.all_to_all(outgoing.reshape(peers, slots, out_width), SPACE, 0, 0, ti...  3.8 us
    all_to_all x1, starting transfers between devices, local(): sums = lax.all_to_all(quarter, 'scene', 0, 0, tiled=True)  3.26 us
  transfers between devices with their start and end apart: 7, of which 3 were waited for; matrix products, arithmetic and copies ran while one was open for 0% of the time, Pallas kernels for 10%

profile of v14, /device:TPU:1, one launch (start us, length us, event | category | flops | bytes accessed | tf_op | source)
XLA Modules:
  0.0 97.0 jit_solution(11590837543488887090)
XLA Ops:
  0.6 2.2 %shard_map.94 = (bf16[192,128]{1,0:T(8,128)(2,1)}, bf16[1024,128]{1,0:T(8,128)(2,1)}) custom-call(bf16[128,128]{1,0:T(8,128)(2,1)} %bitcast.44, s32[128,128]{1,0:T(8,128)} %bitcast.35, s32[8,128]{1,0:T(8,128)} %bitcast.28, s32[27,1,128]{2,1,0:T(1,128)} %bitcast.45, s32[27,1,128]{2,1,0:T(1,128)} %bitcast.46), custom_call_target="tpu_custom_call" | custom-call | flops 33554432 | bytes 393216 | tf_op jit(solution)/shard_map/pallas_call | solution.py:317
  2.9 0.0 copy-start.5
  2.9 18.6 %all-to-all-start = ((bf16[128,8,128]{2,1,0:T(8,128)(2,1)}), bf16[128,8,128]{2,1,0:T(8,128)(2,1)S(1)}, u32[]{:S(2)}, u32[]{:S(2)}) async-start(bf16[128,8,128]{2,1,0:T(8,128)(2,1)} %bitcast.30), calls=%async_computation | async-start | bytes 524288 | tf_op jit(solution)/shard_map/all_to_all | solution.py:335
  21.5 3.1 %collective-permute-start = (bf16[128,256]{1,0:T(8,128)(2,1)}, bf16[128,256]{1,0:T(8,128)(2,1)S(1)}, u32[]{:S(2)}, u32[]{:S(2)}) collective-permute-start(bf16[128,256]{1,0:T(8,128)(2,1)} %bitcast.36), channel_id=1, source_target_pairs={{0,1},{1,0},{2,3},{3,2},{4,5},{5,4},{6,7},{7,6},{8,9},{9,8},{10,11... | collective-permute-start | bytes 196616 | tf_op jit(solution)/shard_map/ppermute | solution.py:339
  24.6 4.4 %collective-permute-start.1 = (bf16[128,256]{1,0:T(8,128)(2,1)}, bf16[128,256]{1,0:T(8,128)(2,1)S(1)}, u32[]{:S(2)}, u32[]{:S(2)}) collective-permute-start(bf16[128,256]{1,0:T(8,128)(2,1)} %bitcast.37), channel_id=1, source_target_pairs={{0,2},{1,3},{2,0},{3,1},{4,6},{5,7},{6,4},{7,5},{8,10},{9,11},{10,... | collective-permute-start | bytes 196616 | tf_op jit(solution)/shard_map/ppermute | solution.py:339
  29.0 2.1 %collective-permute-start.2 = (bf16[128,256]{1,0:T(8,128)(2,1)}, bf16[128,256]{1,0:T(8,128)(2,1)S(1)}, u32[]{:S(2)}, u32[]{:S(2)}) collective-permute-start(bf16[128,256]{1,0:T(8,128)(2,1)} %bitcast.38), channel_id=1, source_target_pairs={{0,3},{1,2},{2,1},{3,0},{4,7},{5,6},{6,5},{7,4},{8,11},{9,10},{10,... | collective-permute-start | bytes 196616 | tf_op jit(solution)/shard_map/ppermute | solution.py:339
  31.1 0.0 copy-start.3
  31.1 0.8 copy-done.3
  31.9 0.0 copy-start
  31.9 3.8 %all-to-all-done = bf16[128,8,128]{2,1,0:T(8,128)(2,1)S(1)} async-done(((bf16[128,8,128]{2,1,0:T(8,128)(2,1)}), bf16[128,8,128]{2,1,0:T(8,128)(2,1)S(1)}, u32[]{:S(2)}, u32[]{:S(2)}) %all-to-all-start) | async-done | bytes 262176 | tf_op jit(solution)/shard_map/all_to_all | solution.py:335
  35.7 3.0 %shard_map.96.gathered_any = bf16[3456,128]{1,0:T(8,128)(2,1)} custom-call(bf16[128,128]{1,0:T(8,128)(2,1)S(1)} %get-tuple-element.17.turned_ref, bf16[1024,128]{1,0:T(8,128)(2,1)S(1)} %bitcast.27, s32[32,128]{1,0:T(8,128)S(1)} %get-tuple-element.20.table_ref), custom_call_target="tpu_custom_call" | custom-call | tf_op jit(solution)/shard_map/pallas_call | solution.py:345
  38.7 0.0 collective-permute-done
  38.7 0.0 collective-permute-done.1
  38.7 0.0 collective-permute-done.2
  38.7 6.1 %all-to-all-start.1 = ((bf16[8,432,128]{2,1,0:T(8,128)(2,1)}), bf16[8,432,128]{2,1,0:T(8,128)(2,1)S(1)}, u32[]{:S(2)}, u32[]{:S(2)}) async-start(bf16[8,432,128]{2,1,0:T(8,128)(2,1)} %bitcast.11), calls=%async_computation.1 | async-start | bytes 1769472 | tf_op jit(solution)/shard_map/all_to_all | solution.py:357
  44.8 0.0 copy-done.5
  44.8 1.9 %collective-permute-start.3 = (bf16[4,128,256]{2,1,0:T(8,128)(2,1)S(1)}, bf16[4,128,256]{2,1,0:T(8,128)(2,1)S(1)}, u32[]{:S(2)}, u32[]{:S(2)}) collective-permute-start(bf16[4,128,256]{2,1,0:T(8,128)(2,1)S(1)} %pad_maximum_fusion.near_ref), channel_id=1, source_target_pairs={{0,4},{4,0},{1,5},{5,1},{2,6},{6,2},{3,7},{7,3},{8,12},{12,8},{9,1... | collective-permute-start | bytes 786440 | tf_op jit(solution)/shard_map/ppermute | solution.py:380
  46.8 0.0 copy-done
  46.8 5.8 %shard_map.97 = (f32[128,128]{1,0:T(8,128)S(1)}, s32[5,128,128]{2,1,0:T(8,128)S(1)}, bf16[128,256]{1,0:T(8,128)(2,1)}) custom-call(bf16[4,128,256]{2,1,0:T(8,128)(2,1)S(1)} %pad_maximum_fusion.near_ref, bf16[27,256,128]{2,1,0:T(8,128)(2,1)S(1)} %copy-done, s32[32,128]{1,0:T(8,128)S(1)} %get-tuple-element.20.table_ref, bf16[3456,128]{1,0:T(8,128)(2,1)} %shard_map.96.gathered_any), custom_call_target="tpu_custom_call" | custom-call | tf_op jit(solution)/shard_map/pallas_call | solution.py:360
  52.5 0.0 copy-start.1
  52.6 0.6 copy-done.1
  53.2 0.0 collective-permute-done.3.far_ref
  53.2 4.8 %all-to-all-done.1.g_ref = bf16[8,432,128]{2,1,0:T(8,128)(2,1)S(1)} async-done(((bf16[8,432,128]{2,1,0:T(8,128)(2,1)}), bf16[8,432,128]{2,1,0:T(8,128)(2,1)S(1)}, u32[]{:S(2)}, u32[]{:S(2)}) %all-to-all-start.1) | async-done | bytes 884768 | tf_op jit(solution)/shard_map/all_to_all | solution.py:357
  58.0 0.0 copy-start.2
  58.0 0.0 copy-start.4
  58.0 0.7 shard_map.98
  58.8 29.2 %all_to_all.20 = s32[128,8,128]{2,1,0:T(8,128)S(1)} all-to-all(s32[128,8,128]{2,1,0:T(8,128)S(1)} %bitcast.26), channel_id=1, replica_groups=mesh['y'=8,'z'=8,'core'=2,'scene'=4] {'y','z','core'}, dimensions={0} | all-to-all | bytes 1048576 | tf_op jit(solution)/shard_map/all_to_all | solution.py:388
  87.9 0.7 shard_map.100
  88.7 3.3 %all-to-all-start.3 = ((f32[4,16,128]{2,1,0:T(8,128)}), f32[4,16,128]{2,1,0:T(8,128)S(1)}, u32[]{:S(2)}, u32[]{:S(2)}) async-start(f32[4,16,128]{2,1,0:T(8,128)} %shard_map.100), calls=%async_computation.3 | async-start | bytes 65536 | tf_op jit(solution)/shard_map/all_to_all | solution.py:396
  91.9 0.0 copy-done.2
  92.0 0.0 copy-done.4
  92.0 1.1 %shard_map.99 = bf16[128,128]{1,0:T(8,128)(2,1)} custom-call(f32[128,128]{1,0:T(8,128)S(1)} %copy-done.2, s32[1024,128]{1,0:T(8,128)S(1)} %bitcast.25, s32[8,128]{1,0:T(8,128)S(1)} %bitcast.29), custom_call_target="tpu_custom_call" | custom-call | flops 67108864 | bytes 524288 | tf_op jit(solution)/shard_map/pallas_call | solution.py:397
  93.1 3.1 %all-to-all-done.3 = f32[4,16,128]{2,1,0:T(8,128)S(1)} async-done(((f32[4,16,128]{2,1,0:T(8,128)}), f32[4,16,128]{2,1,0:T(8,128)S(1)}, u32[]{:S(2)}, u32[]{:S(2)}) %all-to-all-start.3) | async-done | bytes 32800 | tf_op jit(solution)/shard_map/all_to_all | solution.py:396
  96.3 0.1 mul.17
  96.4 0.6 copy.13
  (7 shorter events, 0.1 us)
Async XLA Ops:
  2.9 41.9 %copy-start.5 = (bf16[1,128,256]{2,1,0:T(8,128)(2,1)S(1)}, bf16[1,128,256]{2,1,0:T(8,128)(2,1)}, u32[]{:S(2)}) copy-start(bf16[1,128,256]{2,1,0:T(8,128)(2,1)} %param.7) | copy-start | bytes 196612
  2.9 32.8 %all-to-all-start = ((bf16[128,8,128]{2,1,0:T(8,128)(2,1)}), bf16[128,8,128]{2,1,0:T(8,128)(2,1)S(1)}, u32[]{:S(2)}, u32[]{:S(2)}) async-start(bf16[128,8,128]{2,1,0:T(8,128)(2,1)} %bitcast.30), calls=%async_computation | async-start | bytes 524288 | tf_op jit(solution)/shard_map/all_to_all | solution.py:335
  21.5 17.2 %collective-permute-start = (bf16[128,256]{1,0:T(8,128)(2,1)}, bf16[128,256]{1,0:T(8,128)(2,1)S(1)}, u32[]{:S(2)}, u32[]{:S(2)}) collective-permute-start(bf16[128,256]{1,0:T(8,128)(2,1)} %bitcast.36), channel_id=1, source_target_pairs={{0,1},{1,0},{2,3},{3,2},{4,5},{5,4},{6,7},{7,6},{8,9},{9,8},{10,11... | collective-permute-start | bytes 196616 | tf_op jit(solution)/shard_map/ppermute | solution.py:339
  24.6 14.1 %collective-permute-start.1 = (bf16[128,256]{1,0:T(8,128)(2,1)}, bf16[128,256]{1,0:T(8,128)(2,1)S(1)}, u32[]{:S(2)}, u32[]{:S(2)}) collective-permute-start(bf16[128,256]{1,0:T(8,128)(2,1)} %bitcast.37), channel_id=1, source_target_pairs={{0,2},{1,3},{2,0},{3,1},{4,6},{5,7},{6,4},{7,5},{8,10},{9,11},{10,... | collective-permute-start | bytes 196616 | tf_op jit(solution)/shard_map/ppermute | solution.py:339
  29.0 9.7 %collective-permute-start.2 = (bf16[128,256]{1,0:T(8,128)(2,1)}, bf16[128,256]{1,0:T(8,128)(2,1)S(1)}, u32[]{:S(2)}, u32[]{:S(2)}) collective-permute-start(bf16[128,256]{1,0:T(8,128)(2,1)} %bitcast.38), channel_id=1, source_target_pairs={{0,3},{1,2},{2,1},{3,0},{4,7},{5,6},{6,5},{7,4},{8,11},{9,10},{10,... | collective-permute-start | bytes 196616 | tf_op jit(solution)/shard_map/ppermute | solution.py:339
  31.1 0.8 copy-start.3
  31.9 14.9 %copy-start = (bf16[27,256,128]{2,1,0:T(8,128)(2,1)S(1)}, bf16[27,256,128]{2,1,0:T(8,128)(2,1)}, u32[]{:S(2)}) copy-start(bf16[27,256,128]{2,1,0:T(8,128)(2,1)} %w_any.1) | copy-start | bytes 5308420
  38.7 19.3 %all-to-all-start.1 = ((bf16[8,432,128]{2,1,0:T(8,128)(2,1)}), bf16[8,432,128]{2,1,0:T(8,128)(2,1)S(1)}, u32[]{:S(2)}, u32[]{:S(2)}) async-start(bf16[8,432,128]{2,1,0:T(8,128)(2,1)} %bitcast.11), calls=%async_computation.1 | async-start | bytes 1769472 | tf_op jit(solution)/shard_map/all_to_all | solution.py:357
  44.8 8.3 %collective-permute-start.3 = (bf16[4,128,256]{2,1,0:T(8,128)(2,1)S(1)}, bf16[4,128,256]{2,1,0:T(8,128)(2,1)S(1)}, u32[]{:S(2)}, u32[]{:S(2)}) collective-permute-start(bf16[4,128,256]{2,1,0:T(8,128)(2,1)S(1)} %pad_maximum_fusion.near_ref), channel_id=1, source_target_pairs={{0,4},{4,0},{1,5},{5,1},{2,6},{6,2},{3,7},{7,3},{8,12},{12,8},{9,1... | collective-permute-start | bytes 786440 | tf_op jit(solution)/shard_map/ppermute | solution.py:380
  52.5 0.6 copy-start.1
  58.0 33.9 %copy-start.2 = (f32[128,128]{1,0:T(8,128)S(1)}, f32[128,128]{1,0:T(8,128)}, u32[]{:S(2)}) copy-start(f32[128,128]{1,0:T(8,128)} %copy-done.1) | copy-start | bytes 196612
  58.0 33.9 %copy-start.4 = (s32[1,1,1024]{2,1,0:T(1,128)S(1)}, s32[1,1,1024]{2,1,0:T(1,128)}, u32[]{:S(2)}) copy-start(s32[1,1,1024]{2,1,0:T(1,128)} %param.13) | copy-start | bytes 12292
  88.7 7.5 %all-to-all-start.3 = ((f32[4,16,128]{2,1,0:T(8,128)}), f32[4,16,128]{2,1,0:T(8,128)S(1)}, u32[]{:S(2)}, u32[]{:S(2)}) async-start(f32[4,16,128]{2,1,0:T(8,128)} %shard_map.100), calls=%async_computation.3 | async-start | bytes 65536 | tf_op jit(solution)/shard_map/all_to_all | solution.py:396

commit v15 on v13

--- a/solution.py
+++ b/solution.py
@@ -13,7 +13,7 @@
 BF16 = jnp.bfloat16
 I32 = jnp.int32
 LANES = 128
-STEP = 4
+STEP = 2
 WORDS = 8
 VMEM_BYTES = 24 * 1024 * 1024
 MOST_VMEM = 64 * 1024 * 1024 - 128 * 1024

time: 98.6 us -> 98.6 us (level)
  no operation moved by 1% of the time
where the time goes in v15:
time: 98.6 us; the launch traced here: 97.1 us
  starting transfers between devices  39.4 us (40%)
  blocking collectives  29.2 us (30%)
  Pallas kernels  13.6 us (14%)
  waiting for transfers between devices  11.8 us (12%)
  local copies, waits for them, and re-layouts  1.61 us (2%)
    all_to_all x1, blocking collectives, local(): lax.all_to_all(packed.reshape(peers, WORDS, LANES), SPACE, 0, 0, tiled=True)  29.2 us
    all_to_all x1, starting transfers between devices, local(): lax.all_to_all(outgoing.reshape(peers, slots, out_width), SPACE, 0, 0, ti...  18.6 us
    ppermute x3, starting transfers between devices, local(): lax.ppermute(own_x, 'scene', [(i, i ^ d) for i in range(scenes)])  9.59 us
    all_to_all x1, starting transfers between devices, local(): lax.all_to_all(gathered.reshape(group, columns, own_rows), GROUP, 0, 0, t...  6.1 us
    pallas_call x1, Pallas kernels, local(): call(functools.partial(forward_kernel, free=free), (shape((own_rows, out_...  5.77 us
    all_to_all x1, waiting for transfers between devices, local(): lax.all_to_all(gathered.reshape(group, columns, own_rows), GROUP, 0, 0, t...  4.85 us
    all_to_all x1, waiting for transfers between devices, local(): lax.all_to_all(outgoing.reshape(peers, slots, out_width), SPACE, 0, 0, ti...  3.8 us
    all_to_all x1, starting transfers between devices, local(): sums = lax.all_to_all(quarter, 'scene', 0, 0, tiled=True)  3.26 us
  transfers between devices with their start and end apart: 7, of which 3 were waited for; matrix products, arithmetic and copies ran while one was open for 0% of the time, Pallas kernels for 10%

profile of v15, /device:TPU:1, one launch (start us, length us, event | category | flops | bytes accessed | tf_op | source)
XLA Modules:
  0.0 97.1 jit_solution(2755063026044366462)
XLA Ops:
  0.6 2.2 %shard_map.94 = (bf16[192,128]{1,0:T(8,128)(2,1)}, bf16[1024,128]{1,0:T(8,128)(2,1)}) custom-call(bf16[128,128]{1,0:T(8,128)(2,1)} %bitcast.37, s32[128,128]{1,0:T(8,128)} %bitcast.29, s32[8,128]{1,0:T(8,128)} %bitcast.24, s32[27,1,128]{2,1,0:T(1,128)} %bitcast.38, s32[27,1,128]{2,1,0:T(1,128)} %bitcast.39), custom_call_target="tpu_custom_call" | custom-call | flops 33554432 | bytes 393216 | tf_op jit(solution)/shard_map/pallas_call | solution.py:318
  2.9 0.0 copy-start.5
  2.9 18.6 %all-to-all-start = ((bf16[128,8,128]{2,1,0:T(8,128)(2,1)}), bf16[128,8,128]{2,1,0:T(8,128)(2,1)S(1)}, u32[]{:S(2)}, u32[]{:S(2)}) async-start(bf16[128,8,128]{2,1,0:T(8,128)(2,1)} %bitcast.26), calls=%async_computation | async-start | bytes 524288 | tf_op jit(solution)/shard_map/all_to_all | solution.py:336
  21.5 3.1 %collective-permute-start = (bf16[128,256]{1,0:T(8,128)(2,1)}, bf16[128,256]{1,0:T(8,128)(2,1)S(1)}, u32[]{:S(2)}, u32[]{:S(2)}) collective-permute-start(bf16[128,256]{1,0:T(8,128)(2,1)} %bitcast.30), channel_id=1, source_target_pairs={{0,1},{1,0},{2,3},{3,2},{4,5},{5,4},{6,7},{7,6},{8,9},{9,8},{10,11... | collective-permute-start | bytes 196616 | tf_op jit(solution)/shard_map/ppermute | solution.py:340
  24.6 4.4 %collective-permute-start.1 = (bf16[128,256]{1,0:T(8,128)(2,1)}, bf16[128,256]{1,0:T(8,128)(2,1)S(1)}, u32[]{:S(2)}, u32[]{:S(2)}) collective-permute-start(bf16[128,256]{1,0:T(8,128)(2,1)} %bitcast.31), channel_id=1, source_target_pairs={{0,2},{1,3},{2,0},{3,1},{4,6},{5,7},{6,4},{7,5},{8,10},{9,11},{10,... | collective-permute-start | bytes 196616 | tf_op jit(solution)/shard_map/ppermute | solution.py:340
  29.0 2.1 %collective-permute-start.2 = (bf16[128,256]{1,0:T(8,128)(2,1)}, bf16[128,256]{1,0:T(8,128)(2,1)S(1)}, u32[]{:S(2)}, u32[]{:S(2)}) collective-permute-start(bf16[128,256]{1,0:T(8,128)(2,1)} %bitcast.32), channel_id=1, source_target_pairs={{0,3},{1,2},{2,1},{3,0},{4,7},{5,6},{6,5},{7,4},{8,11},{9,10},{10,... | collective-permute-start | bytes 196616 | tf_op jit(solution)/shard_map/ppermute | solution.py:340
  31.1 0.0 copy-start.3
  31.1 0.8 copy-done.3
  31.9 0.0 copy-start
  31.9 3.8 %all-to-all-done = bf16[128,8,128]{2,1,0:T(8,128)(2,1)S(1)} async-done(((bf16[128,8,128]{2,1,0:T(8,128)(2,1)}), bf16[128,8,128]{2,1,0:T(8,128)(2,1)S(1)}, u32[]{:S(2)}, u32[]{:S(2)}) %all-to-all-start) | async-done | bytes 262176 | tf_op jit(solution)/shard_map/all_to_all | solution.py:336
  35.7 3.0 %shard_map.96.gathered_any = bf16[3456,128]{1,0:T(8,128)(2,1)} custom-call(bf16[128,128]{1,0:T(8,128)(2,1)S(1)} %get-tuple-element.17.turned_ref, bf16[1024,128]{1,0:T(8,128)(2,1)S(1)} %bitcast.23, s32[32,128]{1,0:T(8,128)S(1)} %get-tuple-element.20.table_ref), custom_call_target="tpu_custom_call" | custom-call | tf_op jit(solution)/shard_map/pallas_call | solution.py:346
  38.7 0.0 collective-permute-done
  38.7 0.0 collective-permute-done.1
  38.7 0.0 collective-permute-done.2
  38.7 6.1 %all-to-all-start.1 = ((bf16[8,432,128]{2,1,0:T(8,128)(2,1)}), bf16[8,432,128]{2,1,0:T(8,128)(2,1)S(1)}, u32[]{:S(2)}, u32[]{:S(2)}) async-start(bf16[8,432,128]{2,1,0:T(8,128)(2,1)} %bitcast.11), calls=%async_computation.1 | async-start | bytes 1769472 | tf_op jit(solution)/shard_map/all_to_all | solution.py:358
  44.8 0.0 copy-done.5
  44.8 1.9 %collective-permute-start.3 = (bf16[4,128,256]{2,1,0:T(8,128)(2,1)S(1)}, bf16[4,128,256]{2,1,0:T(8,128)(2,1)S(1)}, u32[]{:S(2)}, u32[]{:S(2)}) collective-permute-start(bf16[4,128,256]{2,1,0:T(8,128)(2,1)S(1)} %pad_maximum_fusion.near_ref), channel_id=1, source_target_pairs={{0,4},{4,0},{1,5},{5,1},{2,6},{6,2},{3,7},{7,3},{8,12},{12,8},{9,1... | collective-permute-start | bytes 786440 | tf_op jit(solution)/shard_map/ppermute | solution.py:381
  46.8 0.0 copy-done
  46.8 5.8 %shard_map.97 = (f32[128,128]{1,0:T(8,128)S(1)}, s32[5,128,128]{2,1,0:T(8,128)S(1)}, bf16[128,256]{1,0:T(8,128)(2,1)}) custom-call(bf16[4,128,256]{2,1,0:T(8,128)(2,1)S(1)} %pad_maximum_fusion.near_ref, bf16[27,256,128]{2,1,0:T(8,128)(2,1)S(1)} %copy-done, s32[32,128]{1,0:T(8,128)S(1)} %get-tuple-element.20.table_ref, bf16[3456,128]{1,0:T(8,128)(2,1)} %shard_map.96.gathered_any), custom_call_target="tpu_custom_call" | custom-call | tf_op jit(solution)/shard_map/pallas_call | solution.py:361
  52.5 0.0 copy-start.1
  52.6 0.6 copy-done.1
  53.2 0.0 collective-permute-done.3.far_ref
  53.2 4.8 %all-to-all-done.1.g_ref = bf16[8,432,128]{2,1,0:T(8,128)(2,1)S(1)} async-done(((bf16[8,432,128]{2,1,0:T(8,128)(2,1)}), bf16[8,432,128]{2,1,0:T(8,128)(2,1)S(1)}, u32[]{:S(2)}, u32[]{:S(2)}) %all-to-all-start.1) | async-done | bytes 884768 | tf_op jit(solution)/shard_map/all_to_all | solution.py:358
  58.0 0.0 copy-start.2
  58.0 0.0 copy-start.4
  58.0 0.7 shard_map.98
  58.8 29.2 %all_to_all.20 = s32[128,8,128]{2,1,0:T(8,128)S(1)} all-to-all(s32[128,8,128]{2,1,0:T(8,128)S(1)} %bitcast.22), channel_id=1, replica_groups=mesh['y'=8,'z'=8,'core'=2,'scene'=4] {'y','z','core'}, dimensions={0} | all-to-all | bytes 1048576 | tf_op jit(solution)/shard_map/all_to_all | solution.py:389
  87.9 0.8 shard_map.100
  88.7 3.3 %all-to-all-start.3 = ((f32[4,16,128]{2,1,0:T(8,128)}), f32[4,16,128]{2,1,0:T(8,128)S(1)}, u32[]{:S(2)}, u32[]{:S(2)}) async-start(f32[4,16,128]{2,1,0:T(8,128)} %shard_map.100), calls=%async_computation.3 | async-start | bytes 65536 | tf_op jit(solution)/shard_map/all_to_all | solution.py:397
  92.0 0.0 copy-done.2
  92.0 0.0 copy-done.4
  92.0 1.1 %shard_map.99 = bf16[128,128]{1,0:T(8,128)(2,1)} custom-call(f32[128,128]{1,0:T(8,128)S(1)} %copy-done.2, s32[1024,128]{1,0:T(8,128)S(1)} %bitcast.21, s32[8,128]{1,0:T(8,128)S(1)} %bitcast.25), custom_call_target="tpu_custom_call" | custom-call | flops 67108864 | bytes 524288 | tf_op jit(solution)/shard_map/pallas_call | solution.py:398
  93.1 3.1 %all-to-all-done.3 = f32[4,16,128]{2,1,0:T(8,128)S(1)} async-done(((f32[4,16,128]{2,1,0:T(8,128)}), f32[4,16,128]{2,1,0:T(8,128)S(1)}, u32[]{:S(2)}, u32[]{:S(2)}) %all-to-all-start.3) | async-done | bytes 32800 | tf_op jit(solution)/shard_map/all_to_all | solution.py:397
  96.3 0.1 squeeze.19
  96.3 0.1 squeeze.18
  96.4 0.6 maximum_multiply_fusion
  (5 shorter events, 0.1 us)
Async XLA Ops:
  2.9 41.9 %copy-start.5 = (bf16[1,128,256]{2,1,0:T(8,128)(2,1)S(1)}, bf16[1,128,256]{2,1,0:T(8,128)(2,1)}, u32[]{:S(2)}) copy-start(bf16[1,128,256]{2,1,0:T(8,128)(2,1)} %param.7) | copy-start | bytes 196612
  2.9 32.8 %all-to-all-start = ((bf16[128,8,128]{2,1,0:T(8,128)(2,1)}), bf16[128,8,128]{2,1,0:T(8,128)(2,1)S(1)}, u32[]{:S(2)}, u32[]{:S(2)}) async-start(bf16[128,8,128]{2,1,0:T(8,128)(2,1)} %bitcast.26), calls=%async_computation | async-start | bytes 524288 | tf_op jit(solution)/shard_map/all_to_all | solution.py:336
  21.5 17.2 %collective-permute-start = (bf16[128,256]{1,0:T(8,128)(2,1)}, bf16[128,256]{1,0:T(8,128)(2,1)S(1)}, u32[]{:S(2)}, u32[]{:S(2)}) collective-permute-start(bf16[128,256]{1,0:T(8,128)(2,1)} %bitcast.30), channel_id=1, source_target_pairs={{0,1},{1,0},{2,3},{3,2},{4,5},{5,4},{6,7},{7,6},{8,9},{9,8},{10,11... | collective-permute-start | bytes 196616 | tf_op jit(solution)/shard_map/ppermute | solution.py:340
  24.6 14.1 %collective-permute-start.1 = (bf16[128,256]{1,0:T(8,128)(2,1)}, bf16[128,256]{1,0:T(8,128)(2,1)S(1)}, u32[]{:S(2)}, u32[]{:S(2)}) collective-permute-start(bf16[128,256]{1,0:T(8,128)(2,1)} %bitcast.31), channel_id=1, source_target_pairs={{0,2},{1,3},{2,0},{3,1},{4,6},{5,7},{6,4},{7,5},{8,10},{9,11},{10,... | collective-permute-start | bytes 196616 | tf_op jit(solution)/shard_map/ppermute | solution.py:340
  29.0 9.7 %collective-permute-start.2 = (bf16[128,256]{1,0:T(8,128)(2,1)}, bf16[128,256]{1,0:T(8,128)(2,1)S(1)}, u32[]{:S(2)}, u32[]{:S(2)}) collective-permute-start(bf16[128,256]{1,0:T(8,128)(2,1)} %bitcast.32), channel_id=1, source_target_pairs={{0,3},{1,2},{2,1},{3,0},{4,7},{5,6},{6,5},{7,4},{8,11},{9,10},{10,... | collective-permute-start | bytes 196616 | tf_op jit(solution)/shard_map/ppermute | solution.py:340
  31.1 0.8 copy-start.3
  31.9 14.9 %copy-start = (bf16[27,256,128]{2,1,0:T(8,128)(2,1)S(1)}, bf16[27,256,128]{2,1,0:T(8,128)(2,1)}, u32[]{:S(2)}) copy-start(bf16[27,256,128]{2,1,0:T(8,128)(2,1)} %w_any.1) | copy-start | bytes 5308420
  38.7 19.3 %all-to-all-start.1 = ((bf16[8,432,128]{2,1,0:T(8,128)(2,1)}), bf16[8,432,128]{2,1,0:T(8,128)(2,1)S(1)}, u32[]{:S(2)}, u32[]{:S(2)}) async-start(bf16[8,432,128]{2,1,0:T(8,128)(2,1)} %bitcast.11), calls=%async_computation.1 | async-start | bytes 1769472 | tf_op jit(solution)/shard_map/all_to_all | solution.py:358
  44.8 8.3 %collective-permute-start.3 = (bf16[4,128,256]{2,1,0:T(8,128)(2,1)S(1)}, bf16[4,128,256]{2,1,0:T(8,128)(2,1)S(1)}, u32[]{:S(2)}, u32[]{:S(2)}) collective-permute-start(bf16[4,128,256]{2,1,0:T(8,128)(2,1)S(1)} %pad_maximum_fusion.near_ref), channel_id=1, source_target_pairs={{0,4},{4,0},{1,5},{5,1},{2,6},{6,2},{3,7},{7,3},{8,12},{12,8},{9,1... | collective-permute-start | bytes 786440 | tf_op jit(solution)/shard_map/ppermute | solution.py:381
  52.5 0.6 copy-start.1
  58.0 33.9 %copy-start.2 = (f32[128,128]{1,0:T(8,128)S(1)}, f32[128,128]{1,0:T(8,128)}, u32[]{:S(2)}) copy-start(f32[128,128]{1,0:T(8,128)} %copy-done.1) | copy-start | bytes 196612
  58.0 33.9 %copy-start.4 = (s32[1,1,1024]{2,1,0:T(1,128)S(1)}, s32[1,1,1024]{2,1,0:T(1,128)}, u32[]{:S(2)}) copy-start(s32[1,1,1024]{2,1,0:T(1,128)} %param.13) | copy-start | bytes 12292
  88.7 7.5 %all-to-all-start.3 = ((f32[4,16,128]{2,1,0:T(8,128)}), f32[4,16,128]{2,1,0:T(8,128)S(1)}, u32[]{:S(2)}, u32[]{:S(2)}) async-start(f32[4,16,128]{2,1,0:T(8,128)} %shard_map.100), calls=%async_computation.3 | async-start | bytes 65536 | tf_op jit(solution)/shard_map/all_to_all | solution.py:397
